TPU v7x, 32 devices: a whole 2x2x4 slice. The times are simulated.
32 devices in a mesh: lat: 4 (over y, x), lon: 2 (over core), blk: 4 (over z).
Axes of the slice: x: 2, y: 2, z: 4, core: 2. Of those that a mesh axis runs over, the one named last changes fastest.
Arguments:
- field: bfloat16 [2, 4, 6220800], P('lon', 'blk', 'lat'), may hold values from -25 to 25
- gain_one: float32 [768], P('blk'), may hold values from 0.5 to 1.5
- shift_one: float32 [768], P('blk'), may hold values from -1 to 1
- spec_w1: bfloat16 [2, 8, 96, 96], P(None, 'blk'), may hold values from -0.4375 to 0.4375
- spec_b1: float32 [2, 8, 96], P(None, 'blk'), may hold values from -1.5 to 1.5
- spec_w2: bfloat16 [2, 8, 96, 96], P(None, 'blk'), may hold values from -0.4375 to 0.4375
- spec_b2: float32 [2, 8, 96], P(None, 'blk'), may hold values from -1.5 to 1.5
- gain_two: float32 [768], P('blk'), may hold values from 0.5 to 1.5
- shift_two: float32 [768], P('blk'), may hold values from -1 to 1
- up_weight: bfloat16 [768, 3072], P(None, 'blk'), may hold values from -0.3125 to 0.3125
- up_bias: bfloat16 [3072], P('blk'), may hold values from -1.5 to 1.5
- down_weight: bfloat16 [3072, 768], P('blk'), may hold values from -0.21875 to 0.21875
- down_bias: float32 [768], P('blk'), may hold values from -1.5 to 1.5
- presence: int32 [360, 180], P('lat', 'lon'), may hold values from 0 to 20
- cotangent: bfloat16 [2, 4, 6220800], P('lon', 'blk', 'lat'), may hold values from -9 to 9
Outputs:
- mixed: bfloat16 [2, 4, 6220800], P('lon', 'blk', 'lat')
- input_grad: float32 [2, 4, 6220800], P('lon', 'blk', 'lat')
- gain_one_grad: float32 [768], P('blk')
- shift_one_grad: float32 [768], P('blk')
- spec_w1_grad: float32 [2, 8, 96, 96], P(None, 'blk')
- spec_b1_grad: float32 [2, 8, 96], P(None, 'blk')
- spec_w2_grad: float32 [2, 8, 96, 96], P(None, 'blk')
- spec_b2_grad: float32 [2, 8, 96], P(None, 'blk')
- gain_two_grad: float32 [768], P('blk')
- shift_two_grad: float32 [768], P('blk')
- up_weight_grad: float32 [768, 3072], P(None, 'blk')
- up_bias_grad: float32 [3072], P('blk')
- down_weight_grad: float32 [3072, 768], P('blk')
- down_bias_grad: float32 [768], P('blk')
All inputs are finite; a program needn't handle non-finite values.
Results may differ from a plain program's by a relative error of at most 0.014.
The roundings to bfloat16 on the way count: a program that leaves them out, or rounds other values in their place, can miss the bound.
Values may be sent and summed in bfloat16 or wider, within the bound.
No kernel may reach another device: no remote copies, remote signals or barrier semaphores. Data moves between devices by JAX's collectives and lax.ppermute only.
A program may use at most 320 MiB of HBM per device.

v0:
```python
import math

import jax
import jax.numpy as jnp
from jax import lax
from jax.sharding import PartitionSpec as P

C = 768
BS = 96
H = 90
W = 180


EPS = 1e-05
SHRINK = 0.01
HIGH = lax.Precision.HIGHEST


def gelu_value(values):
    return jax.nn.gelu(values, approximate=False)


def gelu_slope(values):
    cumulative = 0.5 * (1.0 + lax.erf(values * (1.0 / math.sqrt(2.0))))
    density = jnp.exp(-0.5 * values * values) * (1.0 / math.sqrt(2.0 * math.pi))
    return cumulative + values * density


def shrink_value(values):
    return values - SHRINK * jnp.tanh(values / SHRINK)


def shrink_slope(values):
    bent = jnp.tanh(values / SHRINK)
    return bent * bent


def phase_table(count_left, count_right, period):
    left_index = lax.broadcasted_iota(jnp.int32, (count_left, count_right), 0)
    right_index = lax.broadcasted_iota(jnp.int32, (count_left, count_right), 1)
    return (left_index * right_index % period).astype(jnp.float32) * (2.0 * math.pi / period)


def row_totals(first_sum, second_sum):
    return lax.psum((first_sum, second_sum), "blk")


def norm_forward(values, gain, shift):
    totals = row_totals(jnp.sum(values, axis=-1), jnp.sum(values * values, axis=-1))
    center = totals[0] / C
    spread_sq = totals[1] / C - center * center
    scale_inv = lax.rsqrt(spread_sq + EPS)
    normed = (values - center[..., None]) * scale_inv[..., None]
    return (normed * gain + shift, normed, scale_inv)


def norm_backward(grad_out, normed, scale_inv, gain):
    grad_normed = grad_out * gain
    totals = row_totals(jnp.sum(grad_normed, axis=-1), jnp.sum(grad_normed * normed, axis=-1))
    grad_in = scale_inv[..., None] * (
        grad_normed - totals[0][..., None] / C - normed * (totals[1][..., None] / C)
    )
    return (grad_in, jnp.sum(grad_out * normed, axis=(0, 1)), jnp.sum(grad_out, axis=(0, 1)))


def along_rows(table, values):
    return jnp.einsum("kh,hslc->kslc", table, values, precision=HIGH)


def turn_rows(real_part, imag_part, row_cos, row_sin):
    real_out = along_rows(row_cos, real_part) + along_rows(row_sin, imag_part)
    imag_out = along_rows(row_cos, imag_part) - along_rows(row_sin, real_part)
    return (real_out, imag_out)


def return_rows(real_part, imag_part, row_cos, row_sin):
    real_out = along_rows(row_cos, real_part) - along_rows(row_sin, imag_part)
    imag_out = along_rows(row_cos, imag_part) + along_rows(row_sin, real_part)
    return (real_out, imag_out)


def spread(values, table_real, table_imag, row_cos, row_sin):
    columns = lax.all_to_all(values, "lon", split_axis=0, concat_axis=1, tiled=True)
    real_part = jnp.einsum("rwc,wl->rlc", columns, table_real, precision=HIGH)
    imag_part = jnp.einsum("rwc,wl->rlc", columns, table_imag, precision=HIGH)
    real_part, imag_part = (
        lax.all_to_all(real_part, ("lat", "lon"), split_axis=1, concat_axis=0, tiled=True),
        lax.all_to_all(imag_part, ("lat", "lon"), split_axis=1, concat_axis=0, tiled=True),
    )
    grid_shape = (H, -1) + real_part.shape[1:]
    return turn_rows(real_part.reshape(grid_shape), imag_part.reshape(grid_shape), row_cos, row_sin)


def collect(real_part, imag_part, table_real, table_imag, row_cos, row_sin):
    real_part, imag_part = return_rows(real_part, imag_part, row_cos, row_sin)
    flat_shape = (-1,) + real_part.shape[2:]
    real_part, imag_part = (
        lax.all_to_all(
            real_part.reshape(flat_shape), ("lat", "lon"), split_axis=0, concat_axis=1, tiled=True
        ),
        lax.all_to_all(
            imag_part.reshape(flat_shape), ("lat", "lon"), split_axis=0, concat_axis=1, tiled=True
        ),
    )
    spatial = jnp.einsum("rlc,lw->rwc", real_part, table_real, precision=HIGH) + jnp.einsum(
        "rlc,lw->rwc", imag_part, table_imag, precision=HIGH
    )
    return lax.all_to_all(spatial, "lon", split_axis=1, concat_axis=0, tiled=True)


def complex_layer(real_in, imag_in, weight, bias):

    def product(values, matrix):
        return jnp.einsum("mbi,bio->mbo", values, matrix, preferred_element_type=jnp.float32)

    real_out = product(real_in, weight[0]) - product(imag_in, weight[1]) + bias[0]
    imag_out = product(imag_in, weight[0]) + product(real_in, weight[1]) + bias[1]
    return (real_out, imag_out)


def complex_back(real_in, imag_in, weight, grad_real, grad_imag):

    def outer(left, right):
        return jnp.einsum("mbi,mbo->bio", left, right, preferred_element_type=jnp.float32)

    def inward(grad, matrix):
        return jnp.einsum("mbo,bio->mbi", grad, matrix, preferred_element_type=jnp.float32)

    weight_grad = jnp.stack(
        [
            outer(real_in, grad_real) + outer(imag_in, grad_imag),
            outer(real_in, grad_imag) - outer(imag_in, grad_real),
        ]
    )
    bias_grad = jnp.stack(
        [
            jnp.sum(grad_real.astype(jnp.float32), axis=0),
            jnp.sum(grad_imag.astype(jnp.float32), axis=0),
        ]
    )
    into_real = inward(grad_real, weight[0]) + inward(grad_imag, weight[1])
    into_imag = inward(grad_imag, weight[0]) - inward(grad_real, weight[1])
    return (weight_grad, bias_grad, into_real, into_imag)


def to_tokens(values):
    return lax.all_to_all(values, "blk", split_axis=0, concat_axis=2, tiled=True)


def to_channels(values):
    return lax.all_to_all(values, "blk", split_axis=2, concat_axis=0, tiled=True)


def per_device(
    field,
    gain_one,
    shift_one,
    spec_w1,
    spec_b1,
    spec_w2,
    spec_b2,
    gain_two,
    shift_two,
    up_weight,
    up_bias,
    down_weight,
    down_bias,
    presence,
    cotangent,
):
    rows_here, cols_here = presence.shape
    chans = gain_one.shape[0]
    out_shape = field.shape
    group = lax.axis_size("lat") * lax.axis_size("lon")
    blk_count = lax.axis_size("blk")
    mode_total = (W // 2 + group) // group * group
    blocks_here = spec_w1.shape[1]
    wide = jnp.float32
    narrow = jnp.bfloat16
    width_angle = phase_table(W, mode_total, W)
    mode_index = lax.broadcasted_iota(jnp.int32, (W, mode_total), 1)
    kept = (mode_index <= W // 2).astype(wide)
    doubled = jnp.where((mode_index == 0) | (mode_index == W // 2), 1.0, 2.0) * kept
    width_scale = 1.0 / math.sqrt(W)
    ahead_cos = jnp.cos(width_angle) * kept * width_scale
    ahead_sin = jnp.sin(width_angle) * kept * width_scale
    return_cos = (jnp.cos(width_angle) * doubled * width_scale).T
    return_sin = (jnp.sin(width_angle) * doubled * width_scale).T
    row_angle = phase_table(H, H, H)
    row_cos = jnp.cos(row_angle) * (1.0 / math.sqrt(H))
    row_sin = jnp.sin(row_angle) * (1.0 / math.sqrt(H))
    field_wide = field.reshape(rows_here, cols_here, chans).astype(wide)
    normed_one, unit_one, inverse_one = norm_forward(field_wide, gain_one, shift_one)
    mode_real, mode_imag = spread(normed_one, ahead_cos, -ahead_sin, row_cos, row_sin)
    grid_shape = mode_real.shape
    block_shape = (-1, blocks_here, BS)
    low_real = mode_real.reshape(block_shape).astype(narrow)
    low_imag = mode_imag.reshape(block_shape).astype(narrow)
    first_real, first_imag = complex_layer(low_real, low_imag, spec_w1, spec_b1)
    act_real = gelu_value(first_real).astype(narrow)
    act_imag = gelu_value(first_imag).astype(narrow)
    second_real, second_imag = complex_layer(act_real, act_imag, spec_w2, spec_b2)
    shrunk_real = shrink_value(second_real)
    shrunk_imag = shrink_value(second_imag)
    filtered = collect(
        shrunk_real.reshape(grid_shape),
        shrunk_imag.reshape(grid_shape),
        return_cos,
        -return_sin,
        row_cos,
        row_sin,
    )
    middle = filtered + normed_one + field_wide
    normed_two, unit_two, inverse_two = norm_forward(middle, gain_two, shift_two)
    low_two = normed_two.astype(narrow)
    cot_grid = cotangent.reshape(rows_here, cols_here, chans).astype(wide)
    grad_out = cot_grid * ((1.0 + presence.astype(wide)) * 0.25)[..., None]
    grad_low = grad_out.astype(narrow)
    down_bias_grad = jnp.sum(grad_low.astype(wide), axis=(0, 1))
    pad_rows = -rows_here % blk_count
    edges = ((0, pad_rows), (0, 0), (0, 0))
    up_full, down_full, bias_full = (
        lax.all_gather(up_weight, "blk", axis=1, tiled=True),
        lax.all_gather(down_weight, "blk", axis=0, tiled=True),
        lax.all_gather(up_bias, "blk", axis=0, tiled=True),
    )
    token_rows = to_tokens(jnp.pad(low_two, edges))
    token_shape = token_rows.shape
    token_flat = token_rows.reshape(-1, C)
    before = jnp.dot(token_flat, up_full, preferred_element_type=wide) + bias_full.astype(wide)
    hidden = gelu_value(before).astype(narrow)
    result = jnp.dot(hidden, down_full, preferred_element_type=wide).reshape(token_shape)
    branch = to_channels(result)[:rows_here]
    grad_rows = to_tokens(jnp.pad(grad_low, edges)).reshape(-1, C)
    down_full_grad = jnp.einsum("tf,tc->fc", hidden, grad_rows, preferred_element_type=wide)
    before_grad = (
        jnp.einsum("tc,fc->tf", grad_rows, down_full, preferred_element_type=wide)
        * gelu_slope(before)
    ).astype(narrow)
    up_full_grad = jnp.einsum("tc,tf->cf", token_flat, before_grad, preferred_element_type=wide)
    bias_full_grad = jnp.sum(before_grad.astype(wide), axis=0)
    normed_grad = jnp.einsum(
        "tf,cf->tc", before_grad, up_full, preferred_element_type=wide
    ).reshape(token_shape)
    two_grad = to_channels(normed_grad)[:rows_here]
    up_grad, down_grad, up_bias_grad = (
        lax.psum_scatter(up_full_grad, "blk", scatter_dimension=1, tiled=True),
        lax.psum_scatter(down_full_grad, "blk", scatter_dimension=0, tiled=True),
        lax.psum_scatter(bias_full_grad, "blk", scatter_dimension=0, tiled=True),
    )
    mixed = (middle + (branch + down_bias)).astype(narrow)
    two_back, gain_two_grad, shift_two_grad = norm_backward(
        two_grad, unit_two, inverse_two, gain_two
    )
    middle_grad = grad_out + two_back
    back_real, back_imag = spread(middle_grad, return_cos.T, -return_sin.T, row_cos, row_sin)
    second_grad_real = (back_real.reshape(block_shape) * shrink_slope(second_real)).astype(narrow)
    second_grad_imag = (back_imag.reshape(block_shape) * shrink_slope(second_imag)).astype(narrow)
    w2_grad, b2_grad, into_real, into_imag = complex_back(
        act_real, act_imag, spec_w2, second_grad_real, second_grad_imag
    )
    first_grad_real = (into_real * gelu_slope(first_real)).astype(narrow)
    first_grad_imag = (into_imag * gelu_slope(first_imag)).astype(narrow)
    w1_grad, b1_grad, mode_grad_real, mode_grad_imag = complex_back(
        low_real, low_imag, spec_w1, first_grad_real, first_grad_imag
    )
    spectral_back = collect(
        mode_grad_real.reshape(grid_shape),
        mode_grad_imag.reshape(grid_shape),
        ahead_cos.T,
        -ahead_sin.T,
        row_cos,
        row_sin,
    )
    one_grad = middle_grad + spectral_back
    one_back, gain_one_grad, shift_one_grad = norm_backward(
        one_grad, unit_one, inverse_one, gain_one
    )
    input_grad = middle_grad + one_back
    totals = lax.psum(
        (
            gain_one_grad,
            shift_one_grad,
            w1_grad,
            b1_grad,
            w2_grad,
            b2_grad,
            gain_two_grad,
            shift_two_grad,
            up_grad,
            up_bias_grad,
            down_grad,
            down_bias_grad,
        ),
        ("lat", "lon"),
    )
    return (mixed.reshape(out_shape), input_grad.reshape(out_shape)) + tuple(totals)


def solution(mesh):
    placed = (
        P("lon", "blk", "lat"),
        P("blk"),
        P("blk"),
        P(None, "blk", None, None),
        P(None, "blk", None),
        P(None, "blk", None, None),
        P(None, "blk", None),
        P("blk"),
        P("blk"),
        P(None, "blk"),
        P("blk"),
        P("blk", None),
        P("blk"),
        P("lat", "lon"),
        P("lon", "blk", "lat"),
    )
    return jax.shard_map(
        per_device,
        mesh=mesh,
        in_specs=placed,
        out_specs=(
            P("lon", "blk", "lat"),
            P("lon", "blk", "lat"),
            P("blk"),
            P("blk"),
            P(None, "blk", None, None),
            P(None, "blk", None),
            P(None, "blk", None, None),
            P(None, "blk", None),
            P("blk"),
            P("blk"),
            P(None, "blk"),
            P("blk"),
            P("blk", None),
            P("blk"),
        ),
        check_vma=False,
    )
```

profile of v0, /device:TPU:1, one launch (start us, length us, event | category | flops | bytes accessed | tf_op | source)
XLA Modules:
  0.0 2462.9 jit_solution(13943627352487000894)
XLA Ops:
  7.2 63.8 %convert_reduce_fusion.3 = f32[1555200]{0:T(1024)} fusion(bf16[1,1,1555200]{2,1,0:T(2,128)(2,1)} %param.15), kind=kLoop, calls=%fused_computation.87 | loop fusion | flops 1555200 | bytes 9331200 | tf_op jit(solution)/shard_map/convert_element_type | solution.py:192
  86.1 17.6 all-reduce.8
  104.4 9.9 multiply_add_fusion.2
  114.3 12.2 all-to-all-start
  142.3 20.1 fusion.137
  172.0 11.5 fusion.134
  188.3 34.9 %all-to-all-done.2 = f32[45,96,192]{2,0,1:T(8,128)} async-done(((f32[45,96,192]{2,0,1:T(8,128)}), f32[45,96,192]{2,0,1:T(8,128)}, u32[]{:S(2)}, u32[]{:S(2)}) %all-to-all-start.2) | async-done | bytes 3317792 | tf_op jit(solution)/shard_map/all_to_all | solution.py:88
  242.2 9.2 fusion.54
  258.0 24.8 %all-to-all-done.1 = f32[45,96,192]{2,0,1:T(8,128)} async-done(((f32[45,96,192]{2,0,1:T(8,128)}), f32[45,96,192]{2,0,1:T(8,128)}, u32[]{:S(2)}, u32[]{:S(2)}) %all-to-all-start.1) | async-done | bytes 3317792 | tf_op jit(solution)/shard_map/all_to_all | solution.py:87
  293.7 8.8 add_convert_fusion.1
  311.8 9.4 subtract_convert_fusion
  336.9 10.4 fusion.86
  347.9 9.1 fusion.89
  397.3 9.8 fusion.78
  407.1 9.4 fusion.116
  430.1 9.4 fusion.76
  439.5 9.4 fusion.119
  454.1 39.8 %all-to-all-done.3 = f32[360,12,192]{2,1,0:T(8,128)} async-done(((f32[360,12,192]{2,1,0:T(8,128)}), f32[360,12,192]{2,1,0:T(8,128)}, u32[]{:S(2)}, u32[]{:S(2)}) %all-to-all-start.3) | async-done | bytes 3317792 | tf_op jit(solution)/shard_map/all_to_all | solution.py:98
  502.4 63.8 %convert_reduce_fusion.2 = f32[1555200]{0:T(1024)} fusion(bf16[1,1,1555200]{2,1,0:T(2,128)(2,1)} %param.29), kind=kLoop, calls=%fused_computation.86 | loop fusion | flops 1555200 | bytes 9331200 | tf_op jit(solution)/shard_map/convert_element_type | solution.py:216
  596.5 9.8 fusion.64
  606.4 10.5 add_bitcast_fusion.1
  619.7 12.0 all_to_all.270
  646.4 12.8 copy.179
  659.2 11.5 fusion.154
  671.0 149.0 %all-reduce.7 = (f32[90,90]{1,0:T(8,128)S(1)}, f32[90,90]{1,0:T(8,128)S(1)}) all-reduce(f32[90,90]{1,0:T(8,128)S(1)} %reduce_sum.171, f32[90,90]{1,0:T(8,128)S(1)} %reduce_sum.169), channel_id=1, replica_groups=mesh['lat'=4,'lon'=2,'blk'=4] {'blk'}, use_global_device_ids=true, to_apply=%region_7.8 | all-reduce | flops 16200 | bytes 129600 | tf_op jit(solution)/shard_map/psum | solution.py:45
  820.1 10.3 add_convert_fusion
  839.3 176.8 %all-gather = bf16[4,1,768]{2,1,0:T(2,128)(2,1)S(1)} all-gather(bf16[1,1,768]{2,1,0:T(2,128)(2,1)S(1)} %reshape.160), channel_id=1, replica_groups=mesh['lat'=4,'lon'=2,'blk'=4] {'blk'}, dimensions={0}, use_global_device_ids=true | all-gather | bytes 7680 | tf_op jit(solution)/shard_map/all_gather | solution.py:225
  1049.1 65.5 %fusion.2 = (bf16[2070,3072]{1,0:T(8,128)(2,1)}, f32[2070,3072]{1,0:T(8,128)}) fusion(f32[3072]{0:T(1024)S(1)} %bitcast.338, bf16[2070,768]{1,0:T(8,128)(2,1)} %reshape.143, bf16[768,3072]{1,0:T(8,128)(2,1)} %all-gather.4.cloned.1.call-done), kind=kOutput, calls=%fused_computation.4 | convolution fusion | flops 10187182080 | bytes 46064640 | tf_op jit(solution)/shard_map/dot_general | solution.py:230
  1114.6 23.7 convert_reduce_fusion
  1142.9 12.4 fusion.456
  1162.6 8.9 copy.191
  1177.2 16.2 fusion.455
  1200.7 8.8 copy.187
  1209.5 172.4 %all-to-all-done.9 = f32[23,90,768]{1,0,2:T(8,128)} async-done(((f32[23,90,768]{1,0,2:T(8,128)}), f32[23,90,768]{1,0,2:T(8,128)}, u32[]{:S(2)}, u32[]{:S(2)}) %all-to-all-start.9) | async-done | bytes 6359072 | tf_op jit(solution)/shard_map/all_to_all | solution.py:151
  1387.9 15.7 fusion.461
  1403.6 11.8 copy.256
  1424.0 319.4 %all-to-all-done.7 = f32[23,90,768]{1,0,2:T(8,128)} async-done(((f32[23,90,768]{1,0,2:T(8,128)}), f32[23,90,768]{1,0,2:T(8,128)}, u32[]{:S(2)}, u32[]{:S(2)}) %all-to-all-start.7) | async-done | bytes 6359072 | tf_op jit(solution)/shard_map/all_to_all | solution.py:151
  1743.5 11.8 copy.255
  1755.3 8.8 copy.189
  1764.2 9.6 multiply_reduce_fusion
  1773.8 13.6 all-reduce.6
  1787.4 13.7 multiply_add_fusion.1
  1801.1 16.6 all_to_all.271
  1822.5 10.6 fusion.143
  1842.8 11.5 fusion.140
  1859.1 34.9 %all-to-all-done.12 = f32[45,96,192]{2,0,1:T(8,128)} async-done(((f32[45,96,192]{2,0,1:T(8,128)}), f32[45,96,192]{2,0,1:T(8,128)}, u32[]{:S(2)}, u32[]{:S(2)}) %all-to-all-start.12) | async-done | bytes 3317792 | tf_op jit(solution)/shard_map/all_to_all | solution.py:88
  1902.1 16.1 fusion.462
  1929.2 24.2 all-to-all-done.11
  2076.4 9.4 fusion.70
  2085.8 9.8 fusion.122
  2108.8 9.4 fusion.68
  2118.2 9.4 fusion.125
  2132.8 39.8 %all-to-all-done.13 = f32[360,12,192]{2,1,0:T(8,128)} async-done(((f32[360,12,192]{2,1,0:T(8,128)}), f32[360,12,192]{2,1,0:T(8,128)}, u32[]{:S(2)}, u32[]{:S(2)}) %all-to-all-start.13) | async-done | bytes 3317792 | tf_op jit(solution)/shard_map/all_to_all | solution.py:98
  2198.0 47.0 %all-to-all-done.14 = f32[360,12,192]{2,1,0:T(8,128)} async-done(((f32[360,12,192]{2,1,0:T(8,128)}), f32[360,12,192]{2,1,0:T(8,128)}, u32[]{:S(2)}, u32[]{:S(2)}) %all-to-all-start.14) | async-done | bytes 3317792 | tf_op jit(solution)/shard_map/all_to_all | solution.py:101
  2250.4 10.0 fusion.60
  2260.5 10.3 add_bitcast_fusion
  2273.5 14.3 all_to_all.272
  2296.0 12.1 bitcast_add_fusion
  2308.2 10.8 multiply_reduce_fusion.1
  2328.1 36.3 %reshape.145 = bf16[1,1,1555200]{2,1,0:T(2,128)(2,1)} reshape(bf16[1555200]{0:T(1024)(128)(2,1)S(1)} %reshape.175) | data formatting | bytes 6220800 | tf_op jit(solution)/shard_map/reshape | solution.py:297
  2366.0 13.7 multiply_add_fusion
  2379.7 16.0 reshape.156
  2396.5 19.8 all-reduce.3
  2416.4 31.2 %all-reduce.12.cloned.1.call-done = (f32[2,2,96,96]{3,2,1,0:T(8,128)}, f32[2,2,96,96]{3,2,1,0:T(8,128)}, f32[768,768]{1,0:T(8,128)}, f32[768,768]{1,0:T(8,128)}) async-done(((f32[2,2,96,96]{3,2,1,0:T(8,128)}, f32[2,2,96,96]{3,2,1,0:T(8,128)}, f32[768,768]{1,0:T(8,128)}, f32[768,768]{1,0:T(8,128)}), (f32[2,2,96,96]{3,2,1,0:T(8,128)}, f32[2,2,96,96]{3,2,1,0:T(8,128)}, f32[768,768]{1,0:T(8,128)}, ...) | async-done | bytes 5013520 | tf_op jit(solution)/shard_map/psum | solution.py:280
  (321 shorter events, 544.8 us)
Async XLA Ops:
  79.5 24.9 %copy-start.46 = (f32[192]{0:T(256)S(1)}, f32[192]{0:T(256)}, u32[]{:S(2)}) copy-start(f32[192]{0:T(256)} %param.16) | copy-start | bytes 2308
  79.5 24.9 %copy-start.49 = (f32[192]{0:T(256)S(1)}, f32[192]{0:T(256)}, u32[]{:S(2)}) copy-start(f32[192]{0:T(256)} %param.17) | copy-start | bytes 2308
  114.3 19.6 all-to-all-start
  126.5 45.5 %copy-start.53 = (f32[96]{0:T(128)}, f32[96]{0:T(128)S(1)}, u32[]{:S(2)}) copy-start(f32[96]{0:T(128)S(1)} %compare_convert_fusion) | copy-start | bytes 1156
  142.3 20.1 copy-start.2
  167.1 56.1 %all-to-all-start.2 = ((f32[45,96,192]{2,0,1:T(8,128)}), f32[45,96,192]{2,0,1:T(8,128)}, u32[]{:S(2)}, u32[]{:S(2)}) async-start(f32[45,96,192]{2,0,1:T(8,128)} %copy.147), calls=%async_computation.2 | async-start | bytes 9437184 | tf_op jit(solution)/shard_map/all_to_all | solution.py:88
  188.3 43.3 %copy-start.60 = (f32[2,2,96]{2,1,0:T(2,128)S(1)}, f32[2,2,96]{2,1,0:T(2,128)}, u32[]{:S(2)}) copy-start(f32[2,2,96]{2,1,0:T(2,128)} %param.19) | copy-start | bytes 4612
  188.3 43.3 %copy-start.61 = (f32[2,2,96]{2,1,0:T(2,128)S(1)}, f32[2,2,96]{2,1,0:T(2,128)}, u32[]{:S(2)}) copy-start(f32[2,2,96]{2,1,0:T(2,128)} %param.21) | copy-start | bytes 4612
  223.2 59.6 %all-to-all-start.1 = ((f32[45,96,192]{2,0,1:T(8,128)}), f32[45,96,192]{2,0,1:T(8,128)}, u32[]{:S(2)}, u32[]{:S(2)}) async-start(f32[45,96,192]{2,0,1:T(8,128)} %copy.143), calls=%async_computation.1 | async-start | bytes 9437184 | tf_op jit(solution)/shard_map/all_to_all | solution.py:87
  242.2 9.2 copy-start.4
  311.7 36.2 %copy-start.10 = (bf16[4320,2,96]{0,2,1:T(8,128)(2,1)}, bf16[4320,2,96]{0,2,1:T(8,128)(2,1)S(1)}, u32[]{:S(2)}) copy-start(bf16[4320,2,96]{0,2,1:T(8,128)(2,1)S(1)} %copy.152) | copy-start | bytes 4976644
  324.1 11.5 copy-start.37
  336.9 10.4 copy-start.35
  347.3 30.1 %copy-start.8 = (bf16[4320,2,96]{0,2,1:T(8,128)(2,1)}, bf16[4320,2,96]{0,2,1:T(8,128)(2,1)S(1)}, u32[]{:S(2)}) copy-start(bf16[4320,2,96]{0,2,1:T(8,128)(2,1)S(1)} %get-tuple-element.67) | copy-start | bytes 4976644
  421.6 72.3 %all-to-all-start.3 = ((f32[360,12,192]{2,1,0:T(8,128)}), f32[360,12,192]{2,1,0:T(8,128)}, u32[]{:S(2)}, u32[]{:S(2)}) async-start(f32[360,12,192]{2,1,0:T(8,128)} %bitcast.326), calls=%async_computation.3 | async-start | bytes 11796480 | tf_op jit(solution)/shard_map/all_to_all | solution.py:98
  493.9 97.3 %all-to-all-start.4 = ((f32[360,12,192]{2,1,0:T(8,128)}), f32[360,12,192]{2,1,0:T(8,128)}, u32[]{:S(2)}, u32[]{:S(2)}) async-start(f32[360,12,192]{2,1,0:T(8,128)} %bitcast.325), calls=%async_computation.4 | async-start | bytes 11796480 | tf_op jit(solution)/shard_map/all_to_all | solution.py:101
  583.8 22.6 copy-start.55
  591.2 15.2 slice-start.10
  596.5 9.9 slice-start.11
  631.7 201.9 %all-to-all-start.8 = ((bf16[92,90,192]{2,1,0:T(8,128)(2,1)}), bf16[92,90,192]{2,1,0:T(8,128)(2,1)}, u32[]{:S(2)}, u32[]{:S(2)}) async-start(bf16[92,90,192]{2,1,0:T(8,128)(2,1)} %pad.8), calls=%async_computation.8 | async-start | bytes 9043968 | tf_op jit(solution)/shard_map/all_to_all | solution.py:147
  636.7 412.3 %all-gather.4.cloned.1.call-start = ((), (), s32[]{:S(2)}) async-start(), calls=%async_computation.18 | async-start | bytes 5898240 | tf_op jit(solution)/shard_map/all_gather | solution.py:223
  637.5 21.6 copy-start.50
  646.3 12.8 slice-start.3
  646.3 12.8 slice-start.4
  646.3 12.8 slice-start.5
  646.4 12.8 copy-start.5
  646.4 12.8 copy-start.47
  659.2 160.8 %copy-start.51 = (f32[192]{0:T(256)S(1)}, f32[192]{0:T(256)}, u32[]{:S(2)}) copy-start(f32[192]{0:T(256)} %param.22) | copy-start | bytes 2308
  659.2 160.8 %copy-start.63 = (f32[192]{0:T(256)S(1)}, f32[192]{0:T(256)}, u32[]{:S(2)}) copy-start(f32[192]{0:T(256)} %param.23) | copy-start | bytes 2308
  820.0 10.3 copy-start.39
  820.0 10.3 copy-start.41
  833.5 199.1 %all-to-all-start.6 = ((bf16[92,90,192]{2,1,0:T(8,128)(2,1)}), bf16[92,90,192]{2,1,0:T(8,128)(2,1)}, u32[]{:S(2)}, u32[]{:S(2)}) async-start(bf16[92,90,192]{2,1,0:T(8,128)(2,1)} %pad.7), calls=%async_computation.6 | async-start | bytes 9043968 | tf_op jit(solution)/shard_map/all_to_all | solution.py:147
  838.5 276.0 %all-gather.6.cloned.1.call-start = ((), (), s32[]{:S(2)}) async-start(), calls=%async_computation.19 | async-start | bytes 5898240 | tf_op jit(solution)/shard_map/all_gather | solution.py:224
  1049.1 65.5 %copy-start.25 = (bf16[2070,768]{1,0:T(8,128)(2,1)S(1)}, bf16[2070,768]{1,0:T(8,128)(2,1)}, u32[]{:S(2)}) copy-start(bf16[2070,768]{1,0:T(8,128)(2,1)} %reshape.146) | copy-start | bytes 9538564
  1114.6 28.3 %copy-start.65 = (bf16[768,3072]{1,0:T(8,128)(2,1)S(1)}, bf16[768,3072]{1,0:T(8,128)(2,1)}, u32[]{:S(2)}) copy-start(bf16[768,3072]{1,0:T(8,128)(2,1)} %all-gather.4.cloned.1.call-done) | copy-start | bytes 14155780
  1171.5 210.5 %all-to-all-start.9 = ((f32[23,90,768]{1,0,2:T(8,128)}), f32[23,90,768]{1,0,2:T(8,128)}, u32[]{:S(2)}, u32[]{:S(2)}) async-start(f32[23,90,768]{1,0,2:T(8,128)} %copy.191), calls=%async_computation.9 | async-start | bytes 18874368 | tf_op jit(solution)/shard_map/all_to_all | solution.py:151
  1209.5 178.3 %copy-start.27 = (bf16[2070,768]{1,0:T(8,128)(2,1)S(1)}, bf16[2070,768]{1,0:T(8,128)(2,1)}, u32[]{:S(2)}) copy-start(bf16[2070,768]{1,0:T(8,128)(2,1)} %reshape.143) | copy-start | bytes 9538564
  1382.0 361.5 %all-to-all-start.7 = ((f32[23,90,768]{1,0,2:T(8,128)}), f32[23,90,768]{1,0,2:T(8,128)}, u32[]{:S(2)}, u32[]{:S(2)}) async-start(f32[23,90,768]{1,0,2:T(8,128)} %copy.187), calls=%async_computation.7 | async-start | bytes 18874368 | tf_op jit(solution)/shard_map/all_to_all | solution.py:151
  1387.8 932.1 %reduce-scatter.3.cloned.1.call-start = ((), (), s32[]{:S(2)}) async-start(), calls=%async_computation.20 | async-start | bytes 11796480 | tf_op jit(solution)/shard_map/reduce_scatter | solution.py:247
  1755.3 8.9 copy-start.42
  1764.2 23.2 copy-start.44
  1764.2 23.2 copy-start.64
  1801.1 16.6 copy-start
  1822.5 10.6 copy-start.1
  1837.9 56.1 %all-to-all-start.12 = ((f32[45,96,192]{2,0,1:T(8,128)}), f32[45,96,192]{2,0,1:T(8,128)}, u32[]{:S(2)}, u32[]{:S(2)}) async-start(f32[45,96,192]{2,0,1:T(8,128)} %copy.200), calls=%async_computation.12 | async-start | bytes 9437184 | tf_op jit(solution)/shard_map/all_to_all | solution.py:88
  1859.1 43.0 %copy-start.26 = (bf16[2070,768]{1,0:T(8,128)(2,1)S(1)}, bf16[2070,768]{1,0:T(8,128)(2,1)}, u32[]{:S(2)}) copy-start(bf16[2070,768]{1,0:T(8,128)(2,1)} %reshape.146) | copy-start | bytes 9538564
  1894.0 59.4 %all-to-all-start.11 = ((f32[45,96,192]{2,0,1:T(8,128)}), f32[45,96,192]{2,0,1:T(8,128)}, u32[]{:S(2)}, u32[]{:S(2)}) async-start(f32[45,96,192]{2,0,1:T(8,128)} %copy.196), calls=%async_computation.11 | async-start | bytes 9437184 | tf_op jit(solution)/shard_map/all_to_all | solution.py:87
  1902.1 417.8 %reduce-scatter.5.cloned.1.call-start = ((), (), s32[]{:S(2)}) async-start(), calls=%async_computation.21 | async-start | bytes 11796480 | tf_op jit(solution)/shard_map/reduce_scatter | solution.py:248
  1988.8 14.2 slice-start.6
  2038.2 21.7 copy-start.16
  2042.9 16.5 copy-start.20
  2100.7 71.9 %all-to-all-start.13 = ((f32[360,12,192]{2,1,0:T(8,128)}), f32[360,12,192]{2,1,0:T(8,128)}, u32[]{:S(2)}, u32[]{:S(2)}) async-start(f32[360,12,192]{2,1,0:T(8,128)} %bitcast.327), calls=%async_computation.13 | async-start | bytes 11796480 | tf_op jit(solution)/shard_map/all_to_all | solution.py:98
  2172.6 11.0 copy-start.7
  2172.6 72.4 %all-to-all-start.14 = ((f32[360,12,192]{2,1,0:T(8,128)}), f32[360,12,192]{2,1,0:T(8,128)}, u32[]{:S(2)}, u32[]{:S(2)}) async-start(f32[360,12,192]{2,1,0:T(8,128)} %bitcast.324), calls=%async_computation.14 | async-start | bytes 11796480 | tf_op jit(solution)/shard_map/all_to_all | solution.py:101
  2181.2 183.2 %all-reduce.14.cloned.1.call-start = ((), (), s32[]{:S(2)}) async-start(), calls=%async_computation.23 | async-start | bytes 221184 | tf_op jit(solution)/shard_map/psum | solution.py:45
  2245.0 15.4 slice-start.8
  2250.4 10.1 slice-start.9
  2296.0 12.1 copy-start.31
  2296.0 12.1 copy-start.34
  2296.0 12.1 copy-start.48
  2319.0 128.6 %all-reduce.12.cloned.1.call-start = ((), (), s32[]{:S(2)}) async-start(), calls=%async_computation.22 | async-start | bytes 10223616 | tf_op jit(solution)/shard_map/psum | solution.py:280
  2379.7 16.8 copy-start.57
  2379.7 16.8 copy-start.58
  2379.7 16.8 copy-start.59
  (37 other events, 185.2 us)
Sparse Core Ops, SparseCore 0:
  639.1 165.8 all-gather.3
  841.0 164.9 all-gather.5
  1403.8 335.7 reduce-scatter.2
  1918.4 160.0 reduce-scatter.4
  2319.1 29.9 all-reduce.13
  2353.7 93.8 all-reduce.11
where the time goes:
time: 2480 us; the launch traced here: 2460 us
  waiting for transfers between devices  777 us (31%)
  local copies, waits for them, and re-layouts  486 us (20%)
  matrix products  431 us (17%)
  blocking collectives  420 us (17%)
  other arithmetic  238 us (10%)
  starting transfers between devices  94.2 us (4%)
    all_to_all x2, waiting for transfers between devices, to_channels(): lax.all_to_all(values, 'blk', split_axis=2, concat_axis=0, tiled=True)  492 us
    psum x3, blocking collectives, row_totals(): return lax.psum((first_sum, second_sum), 'blk')  180 us
    all_gather x1, blocking collectives, per_device(): lax.all_gather(up_bias, 'blk', axis=0, tiled=True)  177 us
    dot_general x16, matrix products, along_rows(): return jnp.einsum('kh,hslc->kslc', table, values, precision=HIGH)  134 us
    all_to_all x2, waiting for transfers between devices, collect(): lax.all_to_all(real_part.reshape(flat_shape), ('lat', 'lon'), split_axis=...  79.7 us
    all_to_all x2, waiting for transfers between devices, spread(): lax.all_to_all(imag_part, ('lat', 'lon'), split_axis=1, concat_axis=0, ti...  69.8 us
    dot_general x1, matrix products, per_device(): jnp.dot(token_flat, up_full, preferred_element_type=wide)  65.5 us
    convert_element_type x1, other arithmetic, per_device(): cot_grid = cotangent.reshape(rows_here, cols_here, chans).astype(wide)  63.8 us
  transfers between devices with their start and end apart: 19, of which 11 were waited for; matrix products, arithmetic and copies ran while one was open for 32% of the time, Pallas kernels for 0%

commit v1 on v0

v1 whole, which is shorter than its diff:
```python
import functools
import math

import jax
import jax.numpy as jnp
import ml_dtypes
import numpy as np
from jax import lax
from jax.experimental import pallas as pl
from jax.experimental.pallas import tpu as pltpu
from jax.sharding import PartitionSpec as P

C = 768
BS = 96
H = 90
W = 180
EPS = 1e-05
SHRINK = 0.01
SLOTS = 96
ROW_PAD = 48
VMEM = 60 << 20
wide = jnp.float32
narrow = jnp.bfloat16


def slot_columns():
    cols = np.full((2, SLOTS // 2), -1)
    cols[0, :45] = np.arange(0, 90, 2)
    cols[1, :45] = np.arange(1, 90, 2)
    return cols.reshape(-1)


def column_table(mode_total, doubled):
    cols = slot_columns()
    place = np.concatenate([cols, cols + W // 2])
    valid = np.concatenate([cols >= 0, cols >= 0])
    freq = np.arange(mode_total)
    angle = 2.0 * np.pi * (freq[:, None] * place[None, :] % W) / W
    keep = (freq <= W // 2).astype(np.float64)
    if doubled:
        keep = keep * np.where((freq == 0) | (freq == W // 2), 1.0, 2.0)
    keep = keep[:, None] * valid[None, :] / math.sqrt(W)
    return np.concatenate([np.cos(angle) * keep, -np.sin(angle) * keep], axis=0)


def row_table(rows_total, group):
    snaps = rows_total // H
    half = rows_total // group
    slot = np.arange(group * ROW_PAD)
    row = slot // ROW_PAD * half + slot % ROW_PAD
    valid = slot % ROW_PAD < half
    step, snap = row // snaps, row % snaps
    match = (snap[:, None] == snap[None, :]) & valid[:, None] & valid[None, :]
    angle = 2.0 * np.pi * (step[:, None] * step[None, :] % H) / H
    scale = match / math.sqrt(H)
    return np.concatenate([np.cos(angle) * scale, np.sin(angle) * scale], axis=0)


def split_table(table):
    high = table.astype(ml_dtypes.bfloat16)
    rest = (table - high.astype(np.float64)).astype(ml_dtypes.bfloat16)
    return jnp.asarray(high), jnp.asarray(rest)


def dot(left, right):
    return lax.dot_general(left, right, (((1,), (0,)), ((), ())), preferred_element_type=wide)


def dot_nt(left, right):
    return lax.dot_general(left, right, (((1,), (1,)), ((), ())), preferred_element_type=wide)


def dot_tn(left, right):
    return lax.dot_general(left, right, (((0,), (0,)), ((), ())), preferred_element_type=wide)


def token_sums(values):
    ones = jnp.ones((8, values.shape[1]), narrow)
    high, rest = split(values)
    return dot_nt(ones, high) + dot_nt(ones, rest)


def split(values):
    high = values.astype(narrow)
    return high, (values - high.astype(wide)).astype(narrow)


def fine_dot(table, table_rest, values):
    high, rest = split(values)
    return dot(table, high) + (dot(table, rest) + dot(table_rest, high))


def normal_parts(values):
    cumulative = 0.5 * (1.0 + lax.erf(values * (1.0 / math.sqrt(2.0))))
    density = jnp.exp(-0.5 * values * values) * (1.0 / math.sqrt(2.0 * math.pi))
    return cumulative, density


def gelu_value(values):
    return values * (0.5 * (1.0 + lax.erf(values * (1.0 / math.sqrt(2.0)))))


def gelu_slope(values):
    cumulative, density = normal_parts(values)
    return cumulative + values * density


def norm_columns(sums):
    rows = []
    for side in range(2):
        mean = sums[side, 0:1] * (1.0 / C)
        spread = sums[side, 1:2] * (1.0 / C) - mean * mean
        rows += [mean, lax.rsqrt(spread + EPS)]
    rows.append(jnp.zeros((4, SLOTS), wide))
    return jnp.transpose(jnp.concatenate(rows, axis=0))


def swap_parts(values):
    half = values.shape[1] // 2
    return jnp.concatenate([values[:, half:], values[:, :half]], axis=1)


def part_sign(shape):
    lane = lax.broadcasted_iota(jnp.int32, shape, 1)
    return jnp.where(lane < shape[1] // 2, 1.0, -1.0).astype(wide)


def lane_tiles(lanes):
    return -(-lanes // 128)


def store_modes(scratch, row, values):
    count, lanes = values.shape
    room = lane_tiles(lanes) * 128
    if room != lanes:
        values = jnp.concatenate([values, jnp.zeros((count, room - lanes), wide)], axis=1)
    for tile, ref in enumerate(scratch):
        ref[pl.ds(row, count, stride=ROW_PAD), :] = values[:, 128 * tile : 128 * (tile + 1)]


def load_modes(scratch, row, count, lanes):
    pieces = [ref[pl.ds(row, count, stride=ROW_PAD), :] for ref in scratch]
    return jnp.concatenate(pieces, axis=1)[:, :lanes]


def flush_modes(scratch, parts):
    group, _, _, lanes = parts[0].shape
    share = sum(part.shape[1] for part in parts)
    for tile, ref in enumerate(scratch):
        width = min(128, lanes - 128 * tile)
        block = ref[...].reshape(group, share, ROW_PAD, 128)
        first = 0
        for part in parts:
            last = first + part.shape[1]
            part[:, :, :, 128 * tile : 128 * tile + width] = block[
                :, first:last, :, :width
            ].astype(part.dtype)
            first = last


def fill_modes(scratch, parts):
    group, _, _, lanes = parts[0].shape
    share = sum(part.shape[1] for part in parts)
    for tile, ref in enumerate(scratch):
        width = min(128, lanes - 128 * tile)
        first = 0
        for part in parts:
            count = part.shape[1]
            block = part[:, :, :, 128 * tile : 128 * tile + width].astype(wide)
            for g in range(group):
                start = (g * share + first) * ROW_PAD
                ref[start : start + count * ROW_PAD, :width] = block[g].reshape(
                    count * ROW_PAD, width
                )
            first += count


def mode_parts(share):
    return (share - share // 2, share // 2)


def mode_scratch(mode_total, lanes):
    return [pltpu.VMEM((mode_total * ROW_PAD, 128), wide)] * lane_tiles(lanes)


def params():
    return pltpu.CompilerParams(vmem_limit_bytes=VMEM)


def cost(flops, moved):
    return pl.CostEstimate(flops=int(flops), bytes_accessed=int(moved), transcendentals=0)


def full(shape):
    return pl.BlockSpec(shape, lambda *_: (0,) * len(shape))


def shape_of(shape, kind):
    return jax.ShapeDtypeStruct(shape, kind)


FLAT_ROWS = 18


def from_flat_kernel(with_sums, flat, out, *rest):
    scratch = rest[-1]
    scratch[...] = flat[0].astype(wide).reshape(scratch.shape)
    empty = jnp.zeros((3, 192), wide)
    for q in range(FLAT_ROWS):
        first = scratch[pl.ds(135 * q, 45, stride=3), :]
        second = scratch[pl.ds(135 * q + 1, 45, stride=3), :]
        third = scratch[pl.ds(135 * q + 2, 45, stride=3), :]
        even = jnp.concatenate([first, second[:, :64]], axis=1)
        odd = jnp.concatenate([second[:, 64:], third], axis=1)
        tile = jnp.concatenate([even, empty, odd, empty], axis=0)
        out[q] = tile.astype(narrow)
        if with_sums:
            total, total_sq = token_sums(tile), token_sums(tile * tile)
            rest[0][q] = jnp.concatenate([total[:1], total_sq[:1]], axis=0)


def from_flat(flat, rows, chans, with_sums):
    if chans != 192:
        grid = flat.reshape(rows, 45, 2, chans).transpose(0, 2, 1, 3)
        grid = jnp.pad(grid, ((0, 0), (0, 0), (0, 3), (0, 0))).reshape(rows, SLOTS, chans)
        if not with_sums:
            return grid
        wider = grid.astype(wide)
        return grid, jnp.stack([jnp.sum(wider, axis=2), jnp.sum(wider * wider, axis=2)], axis=1)
    block = FLAT_ROWS * 90 * chans
    out_specs = [pl.BlockSpec((FLAT_ROWS, SLOTS, chans), lambda i: (i, 0, 0))]
    out_shape = [shape_of((rows, SLOTS, chans), narrow)]
    if with_sums:
        out_specs.append(pl.BlockSpec((FLAT_ROWS, 2, SLOTS), lambda i: (i, 0, 0)))
        out_shape.append(shape_of((rows, 2, SLOTS), wide))
    outs = pl.pallas_call(
        functools.partial(from_flat_kernel, with_sums),
        grid=(rows // FLAT_ROWS,),
        in_specs=[pl.BlockSpec((1, 1, block), lambda i: (0, 0, i))],
        out_specs=out_specs,
        out_shape=out_shape,
        scratch_shapes=[pltpu.VMEM((block // 128, 128), wide)],
        compiler_params=params(),
        cost_estimate=cost(1e6, 1e5),
        name="from_flat",
    )(flat)
    return outs if with_sums else outs[0]


def write_flat(scratch, row, tile):
    even, odd = tile[0:45], tile[48:93]
    scratch[pl.ds(135 * row, 45, stride=3), :] = even[:, :128]
    scratch[pl.ds(135 * row + 1, 45, stride=3), :] = jnp.concatenate(
        [even[:, 128:], odd[:, :64]], axis=1
    )
    scratch[pl.ds(135 * row + 2, 45, stride=3), :] = odd[:, 64:]


PAIR_ROWS = 9


def to_flat_kernel(pairs, flat, scratch):
    chans = pairs.shape[1] // 2
    second = pl.program_id(0) == 1
    for q in range(PAIR_ROWS):
        pair = pairs[q * SLOTS : (q + 1) * SLOTS, :].astype(wide)
        write_flat(scratch, q, jnp.where(second, pair[:, chans:], pair[:, :chans]))
    flat[0] = scratch[...].reshape(1, scratch.shape[0] * 128).astype(flat.dtype)


def plain_flat(grid):
    rows, _, chans = grid.shape
    kept = grid.reshape(rows, 2, SLOTS // 2, chans)[:, :, :45].transpose(0, 2, 1, 3)
    return kept.reshape(1, 1, rows * 90 * chans)


def to_flat(pairs):
    chans = pairs.shape[1] // 2
    if chans != 192:
        grid = pairs[: 45 * SLOTS].reshape(45, SLOTS, 2, chans).transpose(2, 0, 1, 3)
        return plain_flat(grid.reshape(90, SLOTS, chans))
    block = PAIR_ROWS * 90 * chans
    steps = 45 // PAIR_ROWS
    return pl.pallas_call(
        to_flat_kernel,
        grid=(2, steps),
        in_specs=[pl.BlockSpec((PAIR_ROWS * SLOTS, 2 * chans), lambda h, i: (i, 0))],
        out_specs=pl.BlockSpec((1, 1, block), lambda h, i: (0, 0, h * steps + i)),
        out_shape=shape_of((1, 1, 90 * 90 * chans), pairs.dtype),
        scratch_shapes=[pltpu.VMEM((block // 128, 128), wide)],
        compiler_params=params(),
        cost_estimate=cost(1e6, 1e5),
        name="to_flat",
    )(pairs)


def final_tile(base, field, sums, grad_sums):
    mean = sums[0:1] * (1.0 / C)
    spread = sums[1:2] * (1.0 / C) - mean * mean
    inverse = lax.rsqrt(spread + EPS)
    shift = inverse * grad_sums[0:1] * (1.0 / C)
    slope = inverse * inverse * grad_sums[1:2] * (1.0 / C)
    cols = jnp.transpose(
        jnp.concatenate([mean, shift, slope, jnp.zeros((5, SLOTS), wide)], axis=0)
    )
    return base - cols[:, 1:2] - (field.astype(wide) - cols[:, 0:1]) * cols[:, 2:3]


def final_kernel(base, field, sums, grad_sums, flat, scratch):
    for q in range(FLAT_ROWS):
        write_flat(scratch, q, final_tile(base[q], field[q], sums[q], grad_sums[q]))
    flat[0] = scratch[...].reshape(1, scratch.shape[0] * 128)


def final_grid_kernel(base, field, sums, grad_sums, out):
    for q in range(FLAT_ROWS):
        out[q] = final_tile(base[q], field[q], sums[q], grad_sums[q])


def final_flat(base, field, sums, grad_sums):
    rows, _, chans = base.shape
    block = FLAT_ROWS * 90 * chans
    tiles = pl.BlockSpec((FLAT_ROWS, SLOTS, chans), lambda i: (i, 0, 0))
    pairs = pl.BlockSpec((FLAT_ROWS, 2, SLOTS), lambda i: (i, 0, 0))
    common = dict(
        grid=(rows // FLAT_ROWS,),
        in_specs=[tiles, tiles, pairs, pairs],
        compiler_params=params(),
        cost_estimate=cost(1e6, 1e5),
        name="final_flat",
    )
    if chans != 192:
        return plain_flat(
            pl.pallas_call(
                final_grid_kernel,
                out_specs=tiles,
                out_shape=shape_of(base.shape, wide),
                **common,
            )(base, field, sums, grad_sums)
        )
    return pl.pallas_call(
        final_kernel,
        out_specs=pl.BlockSpec((1, 1, block), lambda i: (0, 0, i)),
        out_shape=shape_of((1, 1, rows * 90 * chans), wide),
        scratch_shapes=[pltpu.VMEM((block // 128, 128), wide)],
        **common,
    )(base, field, sums, grad_sums)


STEP = 9


def spread_norm_kernel(field, sums, gain, shift, table, table_rest, out_a, out_b, *scratch):
    step = pl.program_id(0)
    for q in range(STEP):
        cols = norm_columns(sums[:, q])
        sides = []
        for side in range(2):
            centered = field[side, q].astype(wide) - cols[:, 2 * side : 2 * side + 1]
            normed = centered * cols[:, 2 * side + 1 : 2 * side + 2] * gain[...] + shift[...]
            sides.append(normed)
        modes = fine_dot(table[...], table_rest[...], jnp.concatenate(sides, axis=0))
        count = modes.shape[0] // 2
        store_modes(
            scratch, step * STEP + q, jnp.concatenate([modes[:count], modes[count:]], axis=1)
        )
    finish_spread(step, scratch, (out_a, out_b))


def spread_kernel(grad, table, out_a, out_b, *scratch):
    step = pl.program_id(0)
    for q in range(STEP):
        pair = grad[q * SLOTS : (q + 1) * SLOTS, :]
        chans = pair.shape[1] // 2
        modes = dot(table[...], jnp.concatenate([pair[:, :chans], pair[:, chans:]], axis=0))
        count = modes.shape[0] // 2
        store_modes(
            scratch, step * STEP + q, jnp.concatenate([modes[:count], modes[count:]], axis=1)
        )
    finish_spread(step, scratch, (out_a, out_b))


def finish_spread(step, scratch, out):
    @pl.when(step == 0)
    def _():
        count = scratch[0].shape[0] // ROW_PAD
        for row in range(45, ROW_PAD):
            for ref in scratch:
                ref[pl.ds(row, count, stride=ROW_PAD), :] = jnp.zeros((count, 128), wide)

    @pl.when(step == pl.num_programs(0) - 1)
    def _():
        flush_modes(scratch, out)


def spread(inputs, in_specs, kernel, tables, group, lanes, kind, name):
    mode_total = tables[0].shape[0] // 2
    outs = [(group, count, ROW_PAD, lanes) for count in mode_parts(mode_total // group)]
    return pl.pallas_call(
        kernel,
        grid=(45 // STEP,),
        in_specs=in_specs + [full(table.shape) for table in tables],
        out_specs=[full(out) for out in outs],
        out_shape=[shape_of(out, kind) for out in outs],
        scratch_shapes=mode_scratch(mode_total, lanes),
        compiler_params=params(),
        cost_estimate=cost(1e6, 1e5),
        name=name,
    )(*inputs, *tables)


TOKEN_STEP = 8
TOKEN_HALVES = ((0, 24), (24, 21))


def collect_kernel(first, modes_a, modes_b, field, sums, gain, shift, table, out, *scratch):
    step = pl.program_id(0)

    @pl.when(step == 0)
    def _():
        fill_modes(scratch, (modes_a, modes_b))

    for q in range(TOKEN_STEP):
        row = first + step * TOKEN_STEP + q
        spatial = spatial_rows(scratch, row, table, modes_a.shape[3])
        cols = norm_columns(sums[:, q])
        sides = []
        for side in range(2):
            centered = field[side, q].astype(wide) - cols[:, 2 * side : 2 * side + 1]
            normed = centered * cols[:, 2 * side + 1 : 2 * side + 2] * gain[...] + shift[...]
            sides.append(spatial[side] + normed + centered)
        pair = jnp.where(row < 45, jnp.concatenate(sides, axis=1), 0.0)
        out[q * SLOTS : (q + 1) * SLOTS, :] = pair.astype(narrow)


def spatial_rows(scratch, row, table, lanes):
    count = table.shape[0] // 2
    pair = load_modes(scratch, row, count, lanes).astype(narrow)
    stacked = jnp.concatenate([pair[:, : lanes // 2], pair[:, lanes // 2 :]], axis=0)
    spatial = dot_tn(table[...], stacked)
    return spatial[:SLOTS], spatial[SLOTS:]


def collect(modes, field, sums, gain, shift, table, rows, tokens):
    chans = field.shape[3]
    first, count = rows
    skip = first // TOKEN_STEP
    mode_total = table.shape[0] // 2
    return pl.pallas_call(
        functools.partial(collect_kernel, first),
        grid=(-(-count // TOKEN_STEP),),
        in_specs=[full(part.shape) for part in modes]
        + [
            pl.BlockSpec((2, TOKEN_STEP, SLOTS, chans), lambda i: (0, i + skip, 0, 0)),
            pl.BlockSpec((2, TOKEN_STEP, 2, SLOTS), lambda i: (0, i + skip, 0, 0)),
            full(gain.shape),
            full(shift.shape),
            full(table.shape),
        ],
        out_specs=pl.BlockSpec((TOKEN_STEP * SLOTS, 2 * chans), lambda i: (i, 0)),
        out_shape=shape_of((tokens, 2 * chans), narrow),
        scratch_shapes=mode_scratch(mode_total, 2 * chans),
        compiler_params=params(),
        cost_estimate=cost(1e6, 1e5),
        name="collect_norm",
    )(*modes, field, sums, gain, shift, table)


def collect_back_kernel(modes_a, modes_b, grad, field, sums, gain, table, base, parts, small, *scratch):
    step = pl.program_id(0)

    @pl.when(step == 0)
    def _():
        fill_modes(scratch, (modes_a, modes_b))
        small[...] = jnp.zeros(small.shape, wide)

    gain_sum = jnp.zeros((1, gain.shape[1]), wide)
    shift_sum = jnp.zeros((1, gain.shape[1]), wide)
    for q in range(STEP):
        spatial = spatial_rows(scratch, step * STEP + q, table, modes_a.shape[3])
        cols = norm_columns(sums[:, q])
        pair = grad[q * SLOTS : (q + 1) * SLOTS, :].astype(wide)
        chans = pair.shape[1] // 2
        for side in range(2):
            inverse = cols[:, 2 * side + 1 : 2 * side + 2]
            normed = (field[side, q].astype(wide) - cols[:, 2 * side : 2 * side + 1]) * inverse
            middle = pair[:, side * chans : (side + 1) * chans]
            total = middle + spatial[side]
            scaled = total * gain[...]
            base[side, q] = middle + inverse * scaled
            turned = scaled * normed
            parts[side, q] = jnp.concatenate(
                [token_sums(scaled)[:1], token_sums(turned)[:1]], axis=0
            )
            gain_sum = gain_sum + jnp.sum(total * normed, axis=0, keepdims=True)
            shift_sum = shift_sum + jnp.sum(total, axis=0, keepdims=True)
    small[0:1] += gain_sum
    small[1:2] += shift_sum


def collect_back(modes, grad, field, sums, gain, table):
    chans = field.shape[3]
    mode_total = table.shape[0] // 2
    return pl.pallas_call(
        collect_back_kernel,
        grid=(45 // STEP,),
        in_specs=[
            *[full(part.shape) for part in modes],
            pl.BlockSpec((STEP * SLOTS, 2 * chans), lambda i: (i, 0)),
            pl.BlockSpec((2, STEP, SLOTS, chans), lambda i: (0, i, 0, 0)),
            pl.BlockSpec((2, STEP, 2, SLOTS), lambda i: (0, i, 0, 0)),
            full(gain.shape),
            full(table.shape),
        ],
        out_specs=[
            pl.BlockSpec((2, STEP, SLOTS, chans), lambda i: (0, i, 0, 0)),
            pl.BlockSpec((2, STEP, 2, SLOTS), lambda i: (0, i, 0, 0)),
            full((8, chans)),
        ],
        out_shape=[
            shape_of(field.shape, wide),
            shape_of(sums.shape, wide),
            shape_of((8, chans), wide),
        ],
        scratch_shapes=mode_scratch(mode_total, 2 * chans),
        compiler_params=params(),
        cost_estimate=cost(1e6, 1e5),
        name="collect_back",
    )(*modes, grad, field, sums, gain, table)


def turn_rows(both):
    count = both.shape[0] // 2
    turned = swap_parts(both[count:])
    return both[:count] + turned * part_sign(turned.shape)


def return_rows(table, values):
    both = dot(table[...], values.astype(narrow))
    count = both.shape[0] // 2
    turned = swap_parts(both[count:])
    return both[:count] - turned * part_sign(turned.shape)


def shrink_bend(values):
    return jnp.tanh(values * (1.0 / SHRINK))


def spectral_kernel(modes, table, table_rest, w1, b1, w2, b2, out, low, act):
    rows = modes.shape[0] * ROW_PAD
    lanes = modes.shape[3]
    exact = fine_dot(table[...], table_rest[...], modes[...].reshape(rows, lanes))
    coarse = turn_rows(exact).astype(narrow)
    low[0] = coarse
    bent = gelu_value(dot(coarse, w1[...]) + b1[...]).astype(narrow)
    act[0] = bent
    second = dot(bent, w2[...]) + b2[...]
    shrunk = second - SHRINK * shrink_bend(second)
    out[...] = return_rows(table, shrunk).astype(narrow).reshape(out.shape)


def spectral(modes, table, table_rest, w1, b1, w2, b2):
    group, share, _, lanes = modes.shape
    rows = group * ROW_PAD
    mode_block = pl.BlockSpec((group, 1, ROW_PAD, lanes), lambda i: (0, i, 0, 0))
    kept_block = pl.BlockSpec((1, rows, lanes), lambda i: (i, 0, 0))
    return pl.pallas_call(
        spectral_kernel,
        grid=(share,),
        in_specs=[mode_block] + [full(x.shape) for x in (table, table_rest, w1, b1, w2, b2)],
        out_specs=[mode_block, kept_block, kept_block],
        out_shape=[
            shape_of(modes.shape, narrow),
            shape_of((share, rows, lanes), narrow),
            shape_of((share, rows, lanes), narrow),
        ],
        compiler_params=params(),
        cost_estimate=cost(1e6, 1e5),
        name="spectral",
    )(modes, table, table_rest, w1, b1, w2, b2)


def spectral_back_kernel(modes, low, act, table, w1, b1, w2, b2, *rest):
    before, (out, *outs) = rest[: -4 - bool(len(rest) > 4)], rest[-4 - bool(len(rest) > 4) :]
    second_part = bool(before)
    grads, (small, g1, g2) = (outs[0] if second_part else None), outs[-3:]
    rows = modes.shape[0] * ROW_PAD
    lanes = modes.shape[3]

    @pl.when(pl.program_id(0) == 0)
    def _():
        for k, ref in enumerate((small, g1, g2)):
            ref[...] = before[k][...] if second_part else jnp.zeros(ref.shape, wide)

    back = turn_rows(dot(table[...], modes[...].reshape(rows, lanes)))
    bent = act[0]
    bend = shrink_bend(dot(bent, w2[...]) + b2[...])
    second = (back * (bend * bend)).astype(narrow)
    g2[...] += dot_tn(bent, second)
    small[1:2] += jnp.sum(second.astype(wide), axis=0, keepdims=True)
    coarse = low[0]
    slope = gelu_slope(dot(coarse, w1[...]) + b1[...])
    first = (dot_nt(second, w2[...]) * slope).astype(narrow)
    g1[...] += dot_tn(coarse, first)
    small[0:1] += jnp.sum(first.astype(wide), axis=0, keepdims=True)
    out[...] = return_rows(table, dot_nt(first, w1[...])).astype(narrow).reshape(out.shape)
    if not second_part:
        return

    @pl.when(pl.program_id(0) == pl.num_programs(0) - 1)
    def _():
        half = lanes // 2
        at = 0
        for outer in (g1[...], g2[...]):
            for part in (
                outer[:half, :half] + outer[half:, half:],
                outer[:half, half:] - outer[half:, :half],
            ):
                for j in range(half // BS):
                    block = slice(j * BS, (j + 1) * BS)
                    grads[at : at + BS, :] = part[block, block]
                    at += BS


def spectral_back(modes, low, act, table, w1, b1, w2, b2, before=()):
    group, share, _, lanes = modes.shape
    rows = group * ROW_PAD
    mode_block = pl.BlockSpec((group, 1, ROW_PAD, lanes), lambda i: (0, i, 0, 0))
    kept_block = pl.BlockSpec((1, rows, lanes), lambda i: (i, 0, 0))
    sums = [shape_of((8, lanes), wide)] + [shape_of((lanes, lanes), wide)] * 2
    outs = [shape_of(modes.shape, narrow)]
    scratch = []
    if before:
        outs += [shape_of((2 * lanes, BS), wide), sums[0]]
        scratch = [pltpu.VMEM(sums[1].shape, wide)] * 2
    else:
        outs += sums
    return pl.pallas_call(
        spectral_back_kernel,
        grid=(share,),
        in_specs=[mode_block, kept_block, kept_block]
        + [full(x.shape) for x in (table, w1, b1, w2, b2, *before)],
        out_specs=[mode_block] + [full(out.shape) for out in outs[1:]],
        out_shape=outs,
        scratch_shapes=scratch,
        compiler_params=params(),
        cost_estimate=cost(1e6, 1e5),
        name="spectral_back",
    )(modes, low, act, table, w1, b1, w2, b2, *before)


def block_matrix_kernel(w1, w2, out1, out2):
    for weight, out in ((w1, out1), (w2, out2)):
        blocks = weight.shape[1]
        empty = jnp.zeros((BS, BS), wide)
        rows = []
        for part in range(2):
            for block in range(blocks):
                real, imag = weight[0, block].astype(wide), weight[1, block].astype(wide)
                pair = (real, imag) if part == 0 else (-imag, real)
                rows.append(
                    jnp.concatenate(
                        [piece if k == block else empty for piece in pair for k in range(blocks)],
                        axis=1,
                    )
                )
        out[...] = jnp.concatenate(rows, axis=0).astype(narrow)


def block_matrices(w1, w2):
    lanes = 2 * w1.shape[1] * BS
    return pl.pallas_call(
        block_matrix_kernel,
        out_shape=[shape_of((lanes, lanes), narrow)] * 2,
        compiler_params=params(),
        cost_estimate=cost(1e6, 1e5),
        name="block_matrices",
    )(w1, w2)


FF_TILE = 256
WEIGHT_ROWS = 128


def token_tile(values, side, start, count):
    chans = values[0].shape[2] // 2
    return jnp.concatenate(
        [
            source[0, pl.ds(start, count), side * chans : (side + 1) * chans]
            for source in values
        ],
        axis=1,
    ).astype(wide)


def norm_two(values):
    mean = jnp.mean(values, axis=1, keepdims=True)
    offset = values - mean
    inverse = lax.rsqrt(jnp.mean(offset * offset, axis=1, keepdims=True) + EPS)
    return offset * inverse, inverse


def mlp_kernel(
    tile,
    blks,
    place,
    *refs,
):
    middle, cot = refs[:blks], refs[blks : 2 * blks]
    refs = refs[2 * blks :]
    mlp_body(tile, place, middle, cot, *refs[:3], refs[3:7], refs[7:11], *refs[11:])


def mlp_body(
    tile,
    here,
    middle,
    cot,
    cols,
    gain,
    shift,
    ups,
    downs,
    up_bias,
    down_bias,
    *rest,
):
    before_refs = rest[:-13]
    mixed_kept, mixed_sent, middle_grad = rest[-13:-10]
    weight_grads, (bias_grad, small) = rest[-10:-6], rest[-6:-4]
    tokens_in, grads_in, branch, grad_sum = rest[-4:]
    first_core = here[1] == 0
    step = pl.program_id(0)
    share = middle[0].shape[1]
    pieces = share // tile

    @pl.when(step == 0)
    def _():
        small[...] = before_refs[5][...] if before_refs else jnp.zeros(small.shape, wide)
        for side in range(2):

            @pl.loop(0, pieces)
            def _(piece):
                start = pl.multiple_of(piece * tile, 16)
                place = pl.ds(pl.multiple_of(side * share + piece * tile, 16), tile)
                normed, _ = norm_two(token_tile(middle, side, start, tile))
                tokens_in[place, :] = (normed * gain[...] + shift[...]).astype(narrow)
                weight = cols[place, 1:2]
                grad = (token_tile(cot, side, start, tile) * weight).astype(narrow)
                grads_in[place, :] = grad
                small[0:1] += jnp.sum(grad.astype(wide), axis=0, keepdims=True)
                branch[place, :] = jnp.zeros((tile, C), wide)
                grad_sum[place, :] = jnp.zeros((tile, C), wide)

    up_tile = jnp.concatenate(
        [
            jnp.where(first_core, ups[k][0, j], ups[2 + k][0, j])
            for j in range(ups[0].shape[1])
            for k in range(2)
        ],
        axis=0,
    )
    down_tile = jnp.concatenate(
        [jnp.where(first_core, downs[2 + k][0, 0], downs[k][0, 0]) for k in range(2)], axis=0
    )
    tokens, grads = tokens_in[...], grads_in[...]
    before = dot(tokens, up_tile) + up_bias[...]
    cumulative, density = normal_parts(before)
    hidden = (before * cumulative).astype(narrow)
    before_grad = (dot_nt(grads, down_tile) * (cumulative + before * density)).astype(narrow)
    branch[...] += dot(hidden, down_tile)
    grad_sum[...] += dot_nt(before_grad, up_tile)
    rows = up_tile.shape[1] // 2
    for which, total in enumerate((dot_tn(before_grad, tokens), dot_tn(hidden, grads))):
        first, second = total[:rows], total[rows:]
        parts = (
            jnp.where(first_core, first, second),
            jnp.where(first_core, second, first),
        )
        for k, part in enumerate(parts):
            if before_refs:
                part = part + before_refs[2 * which + k][0].astype(wide)
            weight_grads[2 * which + k][0] = part.astype(narrow)
    bias_total = jnp.sum(before_grad.astype(wide), axis=0, keepdims=True)
    bias_grad[...] = bias_total + before_refs[4][...] if before_refs else bias_total

    @pl.when(step == pl.num_programs(0) - 1)
    def _():
        for side in range(2):

            @pl.loop(0, pieces)
            def _(piece):
                start = pl.multiple_of(piece * tile, 16)
                place = pl.ds(pl.multiple_of(side * share + piece * tile, 16), tile)
                values = token_tile(middle, side, start, tile)
                normed, inverse = norm_two(values)
                result = (
                    values + cols[place, 0:1] + (branch[place, :] + down_bias[...])
                ).astype(narrow)
                grad = grad_sum[place, :]
                small[1:2] += jnp.sum(grad * normed, axis=0, keepdims=True)
                small[2:3] += jnp.sum(grad, axis=0, keepdims=True)
                scaled = grad * gain[...]
                back = inverse * (
                    scaled
                    - jnp.mean(scaled, axis=1, keepdims=True)
                    - normed * jnp.mean(scaled * normed, axis=1, keepdims=True)
                )
                whole = token_tile(cot, side, start, tile) * cols[place, 1:2] + back
                whole = whole.astype(narrow)
                chans = middle[0].shape[2] // 2

                def put(out):
                    for b in range(len(middle)):
                        out[b, pl.ds(start, tile), :] = result[:, b * chans : (b + 1) * chans]

                pl.when(here[1] == side)(lambda: put(mixed_kept))
                pl.when(here[1] != side)(lambda: put(mixed_sent))
                for b in range(len(middle)):
                    lanes = slice(side * chans, (side + 1) * chans)
                    middle_grad[b, pl.ds(start, tile), lanes] = whole[
                        :, b * chans : (b + 1) * chans
                    ]


def mlp(middle, cot, cols, gain, shift, weights, up_bias, down_bias, before):
    blks, share, lanes = middle.shape
    count = 2 * share
    ff_here = weights[0].shape[3]
    per = ff_here // FF_TILE if ff_here % FF_TILE == 0 else 1
    width = ff_here // per
    tile = share // 4 if share % 64 == 0 else share // 2
    by_source = [
        pl.BlockSpec((1, share, lanes), lambda i, at, b=b: (b, 0, 0)) for b in range(blks)
    ]
    by_ring = [
        pl.BlockSpec((1, share, lanes), lambda i, at, b=b: ((at[0] + blks - b) % blks, 0, 0))
        for b in range(blks)
    ]
    grad_out = pl.BlockSpec((1, width // 2, C), lambda i, at: (i // per, i % per, 0))
    bias_out = pl.BlockSpec((1, width), lambda i, at: (0, i))
    groups = weights[0].shape[1]
    down_weights = weights
    if ff_here != C:
        down_weights = []
        for first in (0, 2):
            whole = jnp.stack(weights[first : first + 2], axis=2).reshape(blks, ff_here, C)
            down_weights += jnp.split(whole[:, None], 2, axis=2)
    return pl.pallas_call(
        functools.partial(mlp_kernel, tile, blks),
        grid_spec=pltpu.PrefetchScalarGridSpec(
            num_scalar_prefetch=1,
            grid=(blks * per,),
            in_specs=by_source
            + by_ring
            + [
                full(cols.shape),
                full(gain.shape),
                full(shift.shape),
                *[
                    pl.BlockSpec(
                        (1, groups, WEIGHT_ROWS, width), lambda i, at: (i // per, 0, 0, i % per)
                    )
                ]
                * 4,
                *[
                    pl.BlockSpec((1, 1, width // 2, C), lambda i, at: (i // per, i % per, 0, 0))
                ]
                * 4,
                bias_out,
                full(down_bias.shape),
            ]
            + ([grad_out] * 4 + [bias_out, full((8, C))] if before else []),
            out_specs=[
                full((blks, share, lanes // 2)),
                full((blks, share, lanes // 2)),
                full(middle.shape),
                *[grad_out] * 4,
                bias_out,
                full((8, C)),
            ],
            scratch_shapes=[
                pltpu.VMEM((count, C), narrow),
                pltpu.VMEM((count, C), narrow),
                pltpu.VMEM((count, C), wide),
                pltpu.VMEM((count, C), wide),
            ],
        ),
        out_shape=[
            shape_of((blks, share, lanes // 2), narrow),
            shape_of((blks, share, lanes // 2), narrow),
            shape_of(middle.shape, narrow),
            *[shape_of((blks, ff_here // 2, C), narrow)] * 4,
            shape_of((1, blks * ff_here), wide),
            shape_of((8, C), wide),
        ],
        compiler_params=params(),
        cost_estimate=cost(1e6, 1e5),
        name="channel_mlp",
    )(
        jnp.stack([lax.axis_index("blk"), lax.axis_index("lon")]).astype(jnp.int32),
        *([middle] * blks),
        *([cot] * blks),
        cols,
        gain,
        shift,
        *weights,
        *down_weights,
        up_bias,
        down_bias,
        *before,
    )


def weight_grads_kernel(pieces, up, down):
    lons = pieces.shape[1]
    for which, out in ((0, up), (1, down)):
        halves = [
            jnp.concatenate([pieces[lat, lon, which] for lat in range(pieces.shape[0])], axis=0)
            for lon in range(lons)
        ]
        rows = halves[0].shape[0]
        group = FF_TILE // 2 if 2 * rows % FF_TILE == 0 else rows
        tiles = [half[k : k + group] for k in range(0, rows, group) for half in halves]
        grad = jnp.concatenate(tiles, axis=0).astype(wide)
        out[...] = jnp.transpose(grad) if which == 0 else grad


def weight_grads(pieces, lons, ff_here):
    pieces = pieces.reshape((-1, lons) + pieces.shape[1:])
    return pl.pallas_call(
        weight_grads_kernel,
        out_shape=[shape_of((C, ff_here), wide), shape_of((ff_here, C), wide)],
        compiler_params=params(),
        cost_estimate=cost(1e6, 1e5),
        name="weight_grads",
    )(pieces)


def swap_first(values, axes):
    return lax.all_to_all(values, axes, split_axis=0, concat_axis=0, tiled=True)


def shifted(values, axis, by):
    size = lax.axis_size(axis)
    return lax.ppermute(values, axis, [(i, (i + by) % size) for i in range(size)])


def other_core(values):
    return lax.ppermute(values, "lon", [(0, 1), (1, 0)])


def pick(values, index):
    return lax.dynamic_index_in_dim(values, index, 0, keepdims=False)


def ring(values, axis):
    return [values] + [shifted(values, axis, by) for by in range(1, lax.axis_size(axis))]


def send(values, axis):
    size, here = lax.axis_size(axis), lax.axis_index(axis)
    pieces = [pick(values, here)]
    for by in range(1, size):
        pieces.append(shifted(pick(values, (here + by) % size), axis, by))
    return pieces


def send_across(values, axis):
    size, here = lax.axis_size(axis), lax.axis_index(axis)
    pieces = [pick(values, here)]
    for by in range(1, size):
        turn = [(i, i ^ by) for i in range(size)]
        pieces.append(lax.ppermute(pick(values, here ^ by), axis, turn))
    return pieces


def in_order(halves):
    size, blk = len(halves[0]), lax.axis_index("blk")
    lanes = halves[0][0].shape[1]
    out = jnp.zeros((sum(size * half[0].shape[0] for half in halves), lanes), halves[0][0].dtype)
    first = 0
    for half in halves:
        share = half[0].shape[0]
        for by, piece in enumerate(half):
            place = first + (blk - by) % size * share
            out = lax.dynamic_update_slice_in_dim(out, piece, place, 0)
        first += size * share
    return out


def lat_broadcast(values):
    count = lax.axis_size("lat")
    return swap_first(jnp.broadcast_to(values[None], (count,) + values.shape), "lat")


def grid_broadcast(values):
    count = lax.axis_size("lat") * lax.axis_size("lon")
    return swap_first(jnp.broadcast_to(values[None], (count,) + values.shape), ("lat", "lon"))


def tied(*values):
    return lax.optimization_barrier(values)


def per_device(
    field,
    gain_one,
    shift_one,
    spec_w1,
    spec_b1,
    spec_w2,
    spec_b2,
    gain_two,
    shift_two,
    up_weight,
    up_bias,
    down_weight,
    down_bias,
    presence,
    cotangent,
):
    rows, cols = presence.shape
    chans = gain_one.shape[0]
    lats, lons, blks = (lax.axis_size(name) for name in ("lat", "lon", "blk"))
    blk, lon = lax.axis_index("blk"), lax.axis_index("lon")
    grid_axes = ("lat", "lon")
    group = lats * lons
    half = rows // lons
    blocks = spec_w1.shape[1]
    mode_total = (W // 2 + group) // group * group
    lanes = 2 * chans
    ff_here = up_bias.shape[0]
    ahead, ahead_rest = split_table(column_table(mode_total, False))
    doubled, _ = split_table(column_table(mode_total, True))
    turn, turn_rest = split_table(row_table(rows * lats, group))
    gain_row, shift_row = gain_one[None, :], shift_one[None, :]

    weight_own = jnp.where(lon == 0, up_weight, down_weight.reshape(up_weight.shape))
    weight_own = weight_own.reshape(-1, 2, WEIGHT_ROWS, ff_here)
    weights = [lax.all_gather(weight_own[:, k], "blk", axis=0, tiled=False) for k in range(2)]

    field_cols, sums_part = from_flat(field, rows, chans, True)
    row_params = jnp.concatenate([up_bias.astype(wide), down_bias, gain_two, shift_two])
    param_count = row_params.shape[0]
    row_params = jnp.pad(row_params, (0, -param_count % (2 * SLOTS))).reshape(-1, 2, SLOTS)
    sums_ring = ring(jnp.concatenate([sums_part, row_params]), "blk")
    sums_cols = sum(piece[:rows] for piece in sums_ring)
    seen = presence.reshape(rows, 45, 2).transpose(0, 2, 1)
    seen = jnp.pad(seen, ((0, 0), (0, 0), (0, 3))).reshape(rows, 1, SLOTS).astype(wide)
    field_rows = swap_first(field_cols.reshape(2, half, SLOTS, chans), "lon")
    scalars = jnp.concatenate([sums_cols, seen], axis=1).reshape(2, half, 3, SLOTS)
    scalars = swap_first(scalars, "lon")
    sums_rows = scalars[:, :, :2]

    modes_a, modes_b = spread(
        (field_rows, sums_rows, gain_row, shift_row),
        [
            pl.BlockSpec((2, STEP, SLOTS, chans), lambda i: (0, i, 0, 0)),
            pl.BlockSpec((2, STEP, 2, SLOTS), lambda i: (0, i, 0, 0)),
            full(gain_row.shape),
            full(shift_row.shape),
        ],
        spread_norm_kernel,
        (ahead, ahead_rest),
        group,
        lanes,
        wide,
        "spread_norm",
    )
    cotangent, modes_a, modes_b, weights[0] = tied(cotangent, modes_a, modes_b, weights[0])
    modes_a = swap_first(modes_a, grid_axes)
    cot_cols = from_flat(cotangent, rows, chans, False).reshape(2, half, SLOTS, chans)
    cot_own, cot_other = pick(cot_cols, lon), other_core(pick(cot_cols, 1 - lon))
    cot_pairs = jnp.concatenate(
        [jnp.where(lon == 0, cot_own, cot_other), jnp.where(lon == 0, cot_other, cot_own)], axis=2
    )
    padded = half * SLOTS
    halves = [
        (first * SLOTS, -(-count * SLOTS // (blks * 16)) * 16) for first, count in TOKEN_HALVES
    ]
    tokens = blks * sum(share for _, share in halves)
    cot_pairs = jnp.pad(cot_pairs.reshape(padded, lanes), ((0, tokens - padded), (0, 0)))
    w1, w2 = block_matrices(spec_w1, spec_w2)
    b1, b2 = spec_b1.reshape(1, lanes), spec_b2.reshape(1, lanes)
    modes_b, cot_pairs, w1, w2, weights[1] = tied(modes_b, cot_pairs, w1, w2, weights[1])
    modes_b = swap_first(modes_b, grid_axes)
    cot_rings = [
        send(cot_pairs[first : first + blks * share].reshape(blks, share, lanes), "blk")
        for first, share in halves
    ]
    shrunk_a, *kept_a = spectral(modes_a, turn, turn_rest, w1, b1, w2, b2)
    modes_b, shrunk_a, cot_rings[0] = tied(modes_b, shrunk_a, cot_rings[0])
    shrunk_a = swap_first(shrunk_a, grid_axes)
    weights_other = [other_core(part) for part in weights]
    shrunk_b, *kept_b = spectral(modes_b, turn, turn_rest, w1, b1, w2, b2)
    cot_b = cot_rings[1]
    shrunk_b, shrunk_a, cot_b[1] = tied(shrunk_b, shrunk_a, cot_b[1])
    shrunk_b = swap_first(shrunk_b, grid_axes)
    per_token = jnp.stack(
        [scalars[:, :, 0] * (1.0 / C), (1.0 + scalars[:, :, 2]) * 0.25], axis=-1
    ).reshape(2, padded, 2)
    per_token = jnp.pad(per_token, ((0, 0), (0, tokens - padded), (0, 0)))
    per_token = [
        lax.dynamic_slice_in_dim(per_token, first + blk * share, share, 1).reshape(2 * share, 2)
        for first, share in halves
    ]
    params_ring = jnp.stack([piece[rows:].reshape(-1)[:param_count] for piece in sums_ring])
    params_all = jnp.concatenate([params_ring[:1], params_ring[:0:-1]])
    params_all = jnp.concatenate([params_all, params_all])
    params_all = lax.dynamic_slice_in_dim(params_all, blks - blk, blks, 0)
    bias_all = params_all[:, :ff_here].reshape(1, -1)
    token_params = [
        params_all[:, ff_here + i * chans : ff_here + (i + 1) * chans].reshape(1, C)
        for i in range(3)
    ]
    shrunk_b, shrunk_a, per_token, bias_all, cot_rings, token_params = tied(
        shrunk_b, shrunk_a, per_token, bias_all, cot_rings, token_params
    )

    middles = []
    for (first, share), spans in zip(halves, TOKEN_HALVES):
        middle = collect(
            (shrunk_a, shrunk_b),
            field_rows,
            sums_rows,
            gain_row,
            shift_row,
            doubled,
            spans,
            blks * share,
        )
        middle, shrunk_b = tied(middle, shrunk_b)
        middles.append(swap_first(middle.reshape(blks, share, lanes), "blk"))
    before, mixed_parts, grad_parts = (), [], []
    for middle, cot_ring, scalar in zip(middles, cot_rings, per_token):
        kept, sent, middle_grad, *before = mlp(
            middle,
            jnp.stack(cot_ring),
            scalar,
            token_params[1],
            token_params[2],
            [*weights, *weights_other],
            bias_all,
            token_params[0],
            before,
        )
        if grad_parts:
            middle_grad, before, grad_parts[0] = tied(middle_grad, before, grad_parts[0])
        mixed_parts.append((kept, sent))
        grad_parts.append(swap_first(middle_grad, "blk"))
    up_kept, up_sent, down_kept, down_sent, bias_part, small_part = before

    ff_half = ff_here // 2
    summed = jnp.stack(
        [
            (kept.astype(wide) + other_core(sent).astype(wide)).astype(narrow)
            for kept, sent in ((up_kept, up_sent), (down_kept, down_sent))
        ]
    ).reshape(2, blks, lats, ff_half // lats, C)
    summed = summed.transpose(2, 1, 0, 3, 4).reshape(-1, C)
    summed = lax.psum_scatter(summed, "lat", scatter_dimension=0, tiled=True)
    total = lax.psum_scatter(summed, "blk", scatter_dimension=0, tiled=True)
    total = total.reshape(2, ff_half // lats, C)
    mixed_rows = []
    for kept, sent in mixed_parts:
        sent = other_core(sent)
        mixed_rows.append(
            jnp.concatenate(
                [jnp.where(lon == 0, kept, sent), jnp.where(lon == 0, sent, kept)], axis=2
            )
        )
    owned = small_part[:3].reshape(3, blks, chans).transpose(1, 0, 2).reshape(blks, -1)
    owned = jnp.concatenate([owned, bias_part.reshape(blks, -1)], axis=1)
    owned = send(owned[:, None, :], "blk")
    grad_parts[1], mixed_rows, owned = tied(grad_parts[1], mixed_rows, owned)
    middle_grad = jnp.concatenate([part.reshape(-1, lanes) for part in grad_parts])

    back_a, back_b = spread(
        (middle_grad,),
        [pl.BlockSpec((STEP * SLOTS, lanes), lambda i: (i, 0))],
        spread_kernel,
        (doubled,),
        group,
        lanes,
        narrow,
        "spread_grad",
    )
    ring_a, ring_b = [send(mixed, "blk") for mixed in mixed_rows]
    back_a = swap_first(back_a, grid_axes)
    back_b, ring_a[1], ring_a[-1] = tied(back_b, ring_a[1], ring_a[-1])
    back_b = swap_first(back_b, grid_axes)
    back_a, *spec_sums = spectral_back(back_a, *kept_a, turn, w1, b1, w2, b2)
    back_a, back_b = tied(back_a, back_b)
    back_a = swap_first(back_a, grid_axes)
    back_b, spec_grads, spec_small = spectral_back(
        back_b, *kept_b, turn, w1, b1, w2, b2, tuple(spec_sums)
    )
    back_b, back_a, total, ring_a, ring_b[1] = tied(back_b, back_a, total, ring_a, ring_b[1])
    back_b = swap_first(back_b, grid_axes)
    total = lax.all_gather(total, grid_axes, axis=0, tiled=False)
    back_a, back_b, ring_b[-1], total, spec_grads = tied(
        back_a, back_b, ring_b[-1], total, spec_grads
    )

    vector = jnp.concatenate([spec_small[:2].reshape(-1), sum(owned).reshape(-1)])
    vector_size, vector_rows = vector.shape[0], -(-vector.shape[0] // (BS * group))
    vector = jnp.pad(vector, (0, group * vector_rows * BS - vector_size))
    shared = jnp.concatenate(
        [spec_grads.reshape(group, -1, BS), vector.reshape(group, vector_rows, BS)], axis=1
    )
    shared = jnp.sum(swap_first(shared, grid_axes), axis=0)

    base, part_sums, one_small = collect_back(
        (back_a, back_b), middle_grad, field_rows, sums_rows, gain_row, ahead
    )
    base, part_sums, total, ring_b, shared = tied(base, part_sums, total, ring_b, shared)
    grad_sums = swap_first(part_sums, "lon").reshape(rows, 2, SLOTS)
    base, grad_sums = tied(base, grad_sums)
    base = swap_first(base, "lon").reshape(rows, SLOTS, chans)
    mixed = in_order((ring_a, ring_b))
    base, mixed, one_small, total, shared = tied(base, mixed, one_small, total, shared)
    mixed = to_flat(mixed)
    up_grad, down_grad = weight_grads(total, lons, ff_here)
    own_rows = shared.shape[0]
    shared = grid_broadcast(jnp.concatenate([shared, one_small[:2].reshape(-1, BS)]))
    base, grad_sums, mixed, up_grad, down_grad = tied(
        base, sum(ring(grad_sums, "blk")), mixed, up_grad, down_grad
    )
    input_grad = final_flat(base, field_cols, sums_cols, grad_sums)

    one_small = jnp.sum(shared[:, own_rows:], axis=0).reshape(-1)
    vector = shared[:, own_rows - vector_rows : own_rows].reshape(-1)
    spec_grads = shared[:, : own_rows - vector_rows].reshape(2, 2, blocks, BS, BS)
    pieces, at = [one_small[:chans], one_small[chans:]], 0
    for size in (lanes, lanes, chans, chans, chans, ff_here):
        pieces.append(vector[at : at + size])
        at += size
    gain_one_grad, shift_one_grad, b1_grad, b2_grad = pieces[:4]
    down_bias_grad, gain_two_grad, shift_two_grad, up_bias_grad = pieces[4:]
    return (
        mixed,
        input_grad,
        gain_one_grad,
        shift_one_grad,
        spec_grads[0],
        b1_grad.reshape(spec_b1.shape),
        spec_grads[1],
        b2_grad.reshape(spec_b2.shape),
        gain_two_grad,
        shift_two_grad,
        up_grad,
        up_bias_grad,
        down_grad,
        down_bias_grad,
    )


def solution(mesh):
    placed = (
        P("lon", "blk", "lat"),
        P("blk"),
        P("blk"),
        P(None, "blk", None, None),
        P(None, "blk", None),
        P(None, "blk", None, None),
        P(None, "blk", None),
        P("blk"),
        P("blk"),
        P(None, "blk"),
        P("blk"),
        P("blk", None),
        P("blk"),
        P("lat", "lon"),
        P("lon", "blk", "lat"),
    )
    return jax.shard_map(
        per_device,
        mesh=mesh,
        in_specs=placed,
        out_specs=(
            P("lon", "blk", "lat"),
            P("lon", "blk", "lat"),
            P("blk"),
            P("blk"),
            P(None, "blk", None, None),
            P(None, "blk", None),
            P(None, "blk", None, None),
            P(None, "blk", None),
            P("blk"),
            P("blk"),
            P(None, "blk"),
            P("blk"),
            P("blk", None),
            P("blk"),
        ),
        check_vma=False,
    )
```

time: 2480 us -> 764 us (0.31)
  waiting for transfers between devices: 777 us -> 174 us
  matrix products: 431 us -> 0 us
  local copies, waits for them, and re-layouts: 486 us -> 72.8 us
  blocking collectives: 420 us -> 10 us
  Pallas kernels: 0 us -> 310 us
  other arithmetic: 238 us -> 36.4 us
  starting transfers between devices: 94.2 us -> 136 us
    all_to_all x13 -> x16, waiting for transfers between devices: 745 us -> 52.2 us  [swap_first(): return lax.all_to_all(values, axes, split_axis=0, concat_axis=0, tiled=True)]
    dot_general x54 -> x0, matrix products: 431 us -> none  [the longest x16 134 us: along_rows(): return jnp.einsum('kh,hslc->kslc', table, values, precision=HIGH)]
    pallas_call x0 -> x17, Pallas kernels: none -> 310 us  [the longest x2 110 us: mlp(): pl.pallas_call(functools.partial(mlp_kernel, tile, blks), grid_spec=pltpu...]
    psum x4 -> x0, blocking collectives: 200 us -> none  [the longest x3 180 us: row_totals(): return lax.psum((first_sum, second_sum), 'blk')]
    reshape x24 -> x19, local copies, waits for them, and re-layouts: 203 us -> 6.84 us  [the longest x3 2.01 us: per_device(): params_all[:, ff_here + i * chans:ff_here + (i + 1) * chans].reshape(1, C)]
    all_gather x1 -> x0, blocking collectives: 177 us -> none  [per_device(): lax.all_gather(up_bias, 'blk', axis=0, tiled=True)]
    all_to_all x18 -> x0, local copies, waits for them, and re-layouts: 137 us -> none  [the longest x4 41 us: to_channels(): lax.all_to_all(values, 'blk', split_axis=2, concat_axis=0, tiled=True)]
    convert_element_type x5 -> x3, other arithmetic: 138 us -> 2.77 us  [the longest x2 2.76 us: per_device(): (kept.astype(wide) + other_core(sent).astype(wide)).astype(narrow)]
  transfers between devices with their start and end apart: 19 -> 49, of which waited for: 11 -> 22; matrix products, arithmetic and copies ran while one was open for 32% -> 11% of each run, Pallas kernels for 0% -> 40%
where the time goes in v1:
time: 764 us; the launch traced here: 754 us
  Pallas kernels  310 us (41%)
  waiting for transfers between devices  174 us (23%)
  starting transfers between devices  136 us (18%)
  local copies, waits for them, and re-layouts  72.8 us (10%)
  other arithmetic  36.4 us (5%)
  between operations  14.8 us (2%)
  blocking collectives  10 us (1%)
    pallas_call x2, Pallas kernels, mlp(): pl.pallas_call(functools.partial(mlp_kernel, tile, blks), grid_spec=pltpu...  110 us
    all_to_all x16, starting transfers between devices, swap_first(): return lax.all_to_all(values, axes, split_axis=0, concat_axis=0, tiled=True)  99.8 us
    ppermute x21, waiting for transfers between devices, shifted(): lax.ppermute(values, axis, [(i, (i + by) % size) for i in range(size)])  77.3 us
    all_to_all x16, waiting for transfers between devices, swap_first(): return lax.all_to_all(values, axes, split_axis=0, concat_axis=0, tiled=True)  52.2 us
    pallas_call x2, Pallas kernels, spectral_back(): pl.pallas_call(spectral_back_kernel, grid=(share,), in_specs=[mode_block,...  36.5 us
    pallas_call x2, Pallas kernels, spectral(): pl.pallas_call(spectral_kernel, grid=(share,), in_specs=[mode_block] + [f...  36.3 us
    ppermute x21, starting transfers between devices, shifted(): lax.ppermute(values, axis, [(i, (i + by) % size) for i in range(size)])  32.4 us
    pallas_call x1, Pallas kernels, collect_back(): pl.pallas_call(collect_back_kernel, grid=(45 // STEP,), in_specs=[*[full(...  27.6 us
  transfers between devices with their start and end apart: 49, of which 22 were waited for; matrix products, arithmetic and copies ran while one was open for 11% of the time, Pallas kernels for 40%

profile of v1, /device:TPU:1, one launch (start us, length us, event | category | flops | bytes accessed | tf_op | source)
XLA Modules:
  0.0 753.8 jit_solution(5781933035152659475)
XLA Ops:
  10.1 10.0 %from_flat.2 = (bf16[90,96,192]{2,1,0:T(8,128)(2,1)}, f32[90,2,96]{2,1,0:T(2,128)}) custom-call(bf16[1,1,1555200]{2,1,0:T(2,128)(2,1)} %flat.1), custom_call_target="tpu_custom_call" | custom-call | flops 1000000 | bytes 100000 | tf_op jit(solution)/shard_map/from_flat/pallas_call | solution.py:236
  26.9 3.3 collective-permute-done
  30.2 7.0 collective-permute-done.1
  38.9 5.6 all_to_all.90
  44.5 6.1 all-to-all-start
  51.3 3.6 all-to-all-done.field
  54.9 15.6 %spread_norm.1 = (f32[8,6,48,384]{3,2,1,0:T(8,128)}, f32[8,6,48,384]{3,2,1,0:T(8,128)}) custom-call(bf16[2,45,96,192]{3,2,1,0:T(8,128)(2,1)} %all-to-all-done.field, f32[2,45,2,96]{3,2,1,0:T(2,128)} %copy.172.sums, f32[1,192]{1,0:T(1,128)} %bitcast.140, f32[1,192]{1,0:T(1,128)} %bitcast.144, bf16[192,192]{1,0:T(8,128)(2,1)} %constant.182.clone.table, ...), custom_call_target="tpu_custom_call" | custom-call | flops 1000000 | bytes 100000 | tf_op jit(solution)/shard_map/spread_norm/pallas_call | solution.py:399
  71.0 4.4 all-to-all-start.3
  75.3 8.6 %from_flat.3 = bf16[90,96,192]{2,1,0:T(8,128)(2,1)} custom-call(bf16[1,1,1555200]{2,1,0:T(2,128)(2,1)} %flat.2), custom_call_target="tpu_custom_call" | custom-call | flops 1000000 | bytes 100000 | tf_op jit(solution)/shard_map/from_flat/pallas_call | solution.py:236
  83.9 3.1 dynamic-slice_bitcast_fusion
  88.9 2.8 collective-permute-done.3
  91.7 2.6 bitcast_select_fusion.1
  97.6 24.8 %all-gather.9.cloned.1.call-done = bf16[12,1,128,768]{3,2,1,0:T(8,128)(2,1)} async-done(((bf16[3,1,128,768]{3,2,1,0:T(8,128)(2,1)}), bf16[12,1,128,768]{3,2,1,0:T(8,128)(2,1)}) %all-gather.9.cloned.1.call-update) | async-done | bytes 2359312 | tf_op jit(solution)/shard_map/all_gather | solution.py:1041
  124.2 4.4 all-to-all-start.2
  132.3 3.0 collective-permute-start.5
  136.8 18.2 %spectral.2 = (bf16[8,6,48,384]{3,2,1,0:T(8,128)(2,1)}, bf16[6,384,384]{2,1,0:T(8,128)(2,1)}, bf16[6,384,384]{2,1,0:T(8,128)(2,1)}) custom-call(f32[8,6,48,384]{3,2,1,0:T(8,128)} %copy-done.5, bf16[768,384]{1,0:T(8,128)(2,1)} %constant.185.clone.table, bf16[768,384]{1,0:T(8,128)(2,1)} %constant.186.clone.table_rest, bf16[384,384]{1,0:T(8,128)(2,1)} %get-tuple-element.158.w1, ...), custom_call_target="tpu_custom_call" | custom-call | flops 1000000 | bytes 100000 | tf_op jit(solution)/shard_map/spectral/pallas_call | solution.py:567
  155.0 10.0 %collective-permute-done.5 = bf16[576,384]{1,0:T(8,128)(2,1)} collective-permute-done((bf16[576,384]{1,0:T(8,128)(2,1)}, bf16[576,384]{1,0:T(8,128)(2,1)}, u32[]{:S(2)}, u32[]{:S(2)}) %collective-permute-start.5) | collective-permute-done | bytes 442400 | tf_op jit(solution)/shard_map/ppermute | solution.py:946
  169.0 7.0 all-to-all-start.4
  178.4 4.9 collective-permute-start.7
  185.4 18.1 %spectral.3 = (bf16[8,6,48,384]{3,2,1,0:T(8,128)(2,1)}, bf16[6,384,384]{2,1,0:T(8,128)(2,1)}, bf16[6,384,384]{2,1,0:T(8,128)(2,1)}) custom-call(f32[8,6,48,384]{3,2,1,0:T(8,128)} %copy-done.4, bf16[768,384]{1,0:T(8,128)(2,1)} %constant.185.clone.table, bf16[768,384]{1,0:T(8,128)(2,1)} %constant.186.clone.table_rest, bf16[384,384]{1,0:T(8,128)(2,1)} %get-tuple-element.158.w1, ...), custom_call_target="tpu_custom_call" | custom-call | flops 1000000 | bytes 100000 | tf_op jit(solution)/shard_map/spectral/pallas_call | solution.py:567
  204.3 4.5 all-to-all-start.5
  222.4 15.6 %collective-permute-done.8 = bf16[512,384]{1,0:T(8,128)(2,1)S(1)} collective-permute-done((bf16[512,384]{1,0:T(8,128)(2,1)}, bf16[512,384]{1,0:T(8,128)(2,1)S(1)}, u32[]{:S(2)}, u32[]{:S(2)}) %collective-permute-start.8) | collective-permute-done | bytes 393248 | tf_op jit(solution)/shard_map/ppermute | solution.py:946
  239.2 10.8 %collect_norm.2 = bf16[2304,384]{1,0:T(8,128)(2,1)} custom-call(bf16[8,6,48,384]{3,2,1,0:T(8,128)(2,1)} %copy-done.2, bf16[8,6,48,384]{3,2,1,0:T(8,128)(2,1)} %copy-done.3, bf16[2,45,96,192]{3,2,1,0:T(8,128)(2,1)} %all-to-all-done.field, f32[2,45,2,96]{3,2,1,0:T(2,128)} %copy.172.sums, f32[1,192]{1,0:T(1,128)} %bitcast.141, f32[1,192]{1,0:T(1,128)} %bitcast.145, ...), custom_call_target="tpu_custom_call" | custom-call | flops 1000000 | bytes 100000 | tf_op jit(solution)/shard_map/collect_norm/pallas_call | solution.py:449
  250.0 10.0 %all-to-all-start.7 = ((bf16[4,576,384]{2,1,0:T(8,128)(2,1)}), bf16[4,576,384]{2,1,0:T(8,128)(2,1)S(1)}, u32[]{:S(2)}, u32[]{:S(2)}) async-start(bf16[4,576,384]{2,1,0:T(8,128)(2,1)} %bitcast.115), calls=%async_computation.7 | async-start | bytes 3538944 | tf_op jit(solution)/shard_map/all_to_all | solution.py:941
  260.7 10.8 %collect_norm.3 = bf16[2048,384]{1,0:T(8,128)(2,1)} custom-call(bf16[8,6,48,384]{3,2,1,0:T(8,128)(2,1)} %copy-done.2, bf16[8,6,48,384]{3,2,1,0:T(8,128)(2,1)} %copy-done.3, bf16[2,45,96,192]{3,2,1,0:T(8,128)(2,1)} %all-to-all-done.field, f32[2,45,2,96]{3,2,1,0:T(2,128)} %copy.172.sums, f32[1,192]{1,0:T(1,128)} %bitcast.142, f32[1,192]{1,0:T(1,128)} %bitcast.146, ...), custom_call_target="tpu_custom_call" | custom-call | flops 1000000 | bytes 100000 | tf_op jit(solution)/shard_map/collect_norm/pallas_call | solution.py:449
  271.5 29.2 %all-to-all-done.7.refs_0_.refs_1_.refs_2_.refs_3_ = bf16[4,576,384]{2,1,0:T(8,128)(2,1)S(1)} async-done(((bf16[4,576,384]{2,1,0:T(8,128)(2,1)}), bf16[4,576,384]{2,1,0:T(8,128)(2,1)S(1)}, u32[]{:S(2)}, u32[]{:S(2)}) %all-to-all-start.7) | async-done | bytes 1769504 | tf_op jit(solution)/shard_map/all_to_all | solution.py:941
  300.7 14.6 %all-to-all-start.6 = ((bf16[4,512,384]{2,1,0:T(8,128)(2,1)}), bf16[4,512,384]{2,1,0:T(8,128)(2,1)S(1)}, u32[]{:S(2)}, u32[]{:S(2)}) async-start(bf16[4,512,384]{2,1,0:T(8,128)(2,1)} %bitcast.116), calls=%async_computation.6 | async-start | bytes 3145728 | tf_op jit(solution)/shard_map/all_to_all | solution.py:941
  315.9 2.9 pad_maximum_fusion.3.refs_4_.refs_5_.refs_6_.refs_7_
  318.8 58.0 %channel_mlp.2 = (bf16[4,576,192]{2,1,0:T(8,128)(2,1)}, bf16[4,576,192]{2,1,0:T(8,128)(2,1)}, bf16[4,576,384]{2,1,0:T(8,128)(2,1)}, bf16[4,384,768]{2,1,0:T(8,12...) custom-call(s32[2]{0:T(128)} %pad_add_fusion.place, ...), custom_call_target="tpu_custom_call" | custom-call | flops 1000000 | bytes 100000 | tf_op jit(solution)/shard_map/channel_mlp/pallas_call | solution.py:849
  376.9 4.5 all-to-all-start.8
  381.4 2.7 pad_maximum_fusion.5.refs_4_.refs_5_.refs_6_.refs_7_
  384.1 52.3 %channel_mlp.3 = (bf16[4,512,192]{2,1,0:T(8,128)(2,1)}, bf16[4,512,192]{2,1,0:T(8,128)(2,1)}, bf16[4,512,384]{2,1,0:T(8,128)(2,1)}, bf16[4,384,768]{2,1,0:T(8,12...) custom-call(s32[2]{0:T(128)} %pad_add_fusion.place, ...), custom_call_target="tpu_custom_call" | custom-call | flops 1000000 | bytes 100000 | tf_op jit(solution)/shard_map/channel_mlp/pallas_call | solution.py:849
  438.4 4.3 collective-permute-done.19
  447.1 2.6 copy.171
  449.7 4.8 all-to-all-start.9
  457.3 2.6 copy.151
  467.9 3.2 broadcast_select_fusion.1
  477.9 3.5 pad_maximum_fusion.4
  483.3 8.0 %collective-permute-done.15 = f32[1,1344]{1,0:T(1,128)S(1)} collective-permute-done((f32[1,1344]{1,0:T(1,128)S(1)}, f32[1,1344]{1,0:T(1,128)S(1)}, u32[]{:S(2)}, u32[]{:S(2)}) %collective-permute-start.15) | collective-permute-done | bytes 5408 | tf_op jit(solution)/shard_map/ppermute | solution.py:946
  493.4 8.0 %spread_grad.1 = (bf16[8,6,48,384]{3,2,1,0:T(8,128)(2,1)}, bf16[8,6,48,384]{3,2,1,0:T(8,128)(2,1)}) custom-call(bf16[4352,384]{1,0:T(8,128)(2,1)} %pad_maximum_fusion.1.grad, bf16[192,192]{1,0:T(8,128)(2,1)} %constant.184.clone.table), custom_call_target="tpu_custom_call" | custom-call | flops 1000000 | bytes 100000 | tf_op jit(solution)/shard_map/spread_grad/pallas_call | solution.py:399
  501.5 5.4 all-to-all-start.10
  508.4 2.9 collective-permute-start.18
  511.3 10.4 %collective-permute-done.17 = bf16[576,384]{1,0:T(8,128)(2,1)S(1)} collective-permute-done((bf16[576,384]{1,0:T(8,128)(2,1)S(1)}, bf16[576,384]{1,0:T(8,128)(2,1)S(1)}, u32[]{:S(2)}, u32[]{:S(2)}) %collective-permute-start.17) | collective-permute-done | bytes 442400 | tf_op jit(solution)/shard_map/ppermute | solution.py:946
  521.6 7.7 %collective-permute-done.18 = bf16[576,384]{1,0:T(8,128)(2,1)S(1)} collective-permute-done((bf16[576,384]{1,0:T(8,128)(2,1)S(1)}, bf16[576,384]{1,0:T(8,128)(2,1)S(1)}, u32[]{:S(2)}, u32[]{:S(2)}) %collective-permute-start.18) | collective-permute-done | bytes 442400 | tf_op jit(solution)/shard_map/ppermute | solution.py:946
  530.1 5.0 all-to-all-start.11
  535.6 17.9 %spectral_back.2 = (bf16[8,6,48,384]{3,2,1,0:T(8,128)(2,1)}, f32[8,384]{1,0:T(8,128)}, f32[384,384]{1,0:T(8,128)}, f32[384,384]{1,0:T(8,128)}) custom-call(bf16[8,6,48,384]{3,2,1,0:T(8,128)(2,1)} %copy-done.8, bf16[6,384,384]{2,1,0:T(8,128)(2,1)} %get-tuple-element.217.low, bf16[6,384,384]{2,1,0:T(8,128)(2,1)} %get-tuple-element.218.act, ...), custom_call_target="tpu_custom_call" | custom-call | flops 1000000 | bytes 100000 | tf_op jit(solution)/shard_map/spectral_back/pallas_call | solution.py:638
  554.7 7.0 all-to-all-start.12
  563.5 2.6 dynamic-slice_bitcast_fusion.9
  566.4 18.5 %spectral_back.3 = (bf16[8,6,48,384]{3,2,1,0:T(8,128)(2,1)}, f32[768,96]{1,0:T(8,128)}, f32[8,384]{1,0:T(8,128)}) custom-call(bf16[8,6,48,384]{3,2,1,0:T(8,128)(2,1)} %copy-done.7, bf16[6,384,384]{2,1,0:T(8,128)(2,1)} %get-tuple-element.224.low, bf16[6,384,384]{2,1,0:T(8,128)(2,1)} %get-tuple-element.225.act, bf16[768,384]{1,0:T(8,128)(2,1)} %constant.185.clone.table, ...), custom_call_target="tpu_custom_call" | custom-call | flops 1000000 | bytes 100000 | tf_op jit(solution)/shard_map/spectral_back/pallas_call | solution.py:638
  585.7 7.2 collective-permute-done.21
  592.9 4.9 all-to-all-start.13
  602.5 6.2 collective-permute-done.23
  608.7 12.8 %all-to-all-done.13.modes_b = bf16[8,6,48,384]{3,2,1,0:T(8,128)(2,1)} async-done(((bf16[8,6,48,384]{3,2,1,0:T(8,128)(2,1)}), bf16[8,6,48,384]{3,2,1,0:T(8,128)(2,1)}, u32[]{:S(2)}, u32[]{:S(2)}) %all-to-all-start.13) | async-done | bytes 1769504 | tf_op jit(solution)/shard_map/all_to_all | solution.py:941
  621.5 10.3 %all-gather.11.cloned.1.call-done = bf16[16,96,768]{2,1,0:T(8,128)(2,1)} async-done(((bf16[2,96,768]{2,1,0:T(8,128)(2,1)}), bf16[16,96,768]{2,1,0:T(8,128)(2,1)}) %all-gather.11.cloned.1.call-update) | async-done | bytes 2359312 | tf_op jit(solution)/shard_map/all_gather | solution.py:1201
  635.8 4.5 all-to-all-start.14
  643.6 27.6 %collect_back.1 = (f32[2,45,96,192]{3,2,1,0:T(8,128)}, f32[2,45,2,96]{3,2,1,0:T(2,128)}, f32[8,192]{1,0:T(8,128)}) custom-call(bf16[8,6,48,384]{3,2,1,0:T(8,128)(2,1)} %copy-done.10, bf16[8,6,48,384]{3,2,1,0:T(8,128)(2,1)} %all-to-all-done.13.modes_b, bf16[4352,384]{1,0:T(8,128)(2,1)} %pad_maximum_fusion.1.grad, ...), custom_call_target="tpu_custom_call" | custom-call | flops 1000000 | bytes 100000 | tf_op jit(solution)/shard_map/collect_back/pallas_call | solution.py:504
  672.2 4.5 all_to_all.91
  678.2 2.4 collective-permute-start.27
  680.5 8.3 %all-to-all-start.16 = ((f32[2,45,96,192]{3,2,1,0:T(8,128)}), f32[2,45,96,192]{3,2,1,0:T(8,128)}, u32[]{:S(2)}, u32[]{:S(2)}) async-start(f32[2,45,96,192]{3,2,1,0:T(8,128)} %get-tuple-element.257), calls=%async_computation.18 | async-start | bytes 17694720 | tf_op jit(solution)/shard_map/all_to_all | solution.py:941
  693.1 3.2 all-to-all-done.16
  698.1 4.5 all-to-all-start.17
  702.6 11.9 %to_flat.1 = bf16[1,1,1555200]{2,1,0:T(2,128)(2,1)} custom-call(bf16[4352,384]{1,0:T(8,128)(2,1)} %copy-done.6), custom_call_target="tpu_custom_call" | custom-call | flops 1000000 | bytes 100000 | tf_op jit(solution)/shard_map/to_flat/pallas_call | solution.py:284
  714.5 4.2 weight_grads.1
  720.5 17.7 %final_flat.1 = f32[1,1,1555200]{2,1,0:T(1,128)} custom-call(f32[90,96,192]{2,1,0:T(8,128)} %bitcast.55.base, bf16[90,96,192]{2,1,0:T(8,128)(2,1)} %get-tuple-element.148.field, f32[90,2,96]{2,1,0:T(2,128)} %copy-done.12, f32[90,2,96]{2,1,0:T(2,128)} %add_add_fusion.grad_sums), custom_call_target="tpu_custom_call" | custom-call | flops 1000000 | bytes 100000 | tf_op jit(solution)/shard_map/final_flat/pallas_call | solution.py:341
  (255 shorter events, 115.7 us)
Async XLA Ops:
  7.2 63.8 %all-gather.7.cloned.1.call-start = ((), (), s32[]{:S(2)}) async-start(), calls=%async_computation.22 | async-start | bytes 2949120 | tf_op jit(solution)/shard_map/all_gather | solution.py:1041
  9.8 112.6 %all-gather.9.cloned.1.call-start = ((), (), s32[]{:S(2)}) async-start(), calls=%async_computation.23 | async-start | bytes 2949120 | tf_op jit(solution)/shard_map/all_gather | solution.py:1041
  10.1 16.5 %copy-start.25 = (s32[90,90]{1,0:T(8,128)S(1)}, s32[90,90]{1,0:T(8,128)}, u32[]{:S(2)}) copy-start(s32[90,90]{1,0:T(8,128)} %param.33) | copy-start | bytes 97204
  21.0 9.2 %collective-permute-start = (f32[97,2,96]{2,1,0:T(2,128)S(1)}, f32[97,2,96]{2,1,0:T(2,128)S(1)}, u32[]{:S(2)}, u32[]{:S(2)}) collective-permute-start(f32[97,2,96]{2,1,0:T(2,128)S(1)} %constant_dynamic-update-slice_fusion.8), channel_id=1, source_target_pairs={{0,1},{1,2},{2,3},{3,0},{4,5},{5,6},{6,7},{7,4},{8,9},{9,10},{10,1... | collective-permute-start | bytes 223496 | tf_op jit(solution)/shard_map/ppermute | solution.py:946
  23.1 14.0 %collective-permute-start.1 = (f32[97,2,96]{2,1,0:T(2,128)S(1)}, f32[97,2,96]{2,1,0:T(2,128)S(1)}, u32[]{:S(2)}, u32[]{:S(2)}) collective-permute-start(f32[97,2,96]{2,1,0:T(2,128)S(1)} %constant_dynamic-update-slice_fusion.8), channel_id=1, source_target_pairs={{0,2},{1,3},{2,0},{3,1},{4,6},{5,7},{6,4},{7,5},{8,10},{9,11},{10,... | collective-permute-start | bytes 223496 | tf_op jit(solution)/shard_map/ppermute | solution.py:946
  25.5 11.7 %collective-permute-start.2 = (f32[97,2,96]{2,1,0:T(2,128)S(1)}, f32[97,2,96]{2,1,0:T(2,128)S(1)}, u32[]{:S(2)}, u32[]{:S(2)}) collective-permute-start(f32[97,2,96]{2,1,0:T(2,128)S(1)} %constant_dynamic-update-slice_fusion.8), channel_id=1, source_target_pairs={{0,3},{1,0},{2,1},{3,2},{4,7},{5,4},{6,5},{7,6},{8,11},{9,8},{10,9... | collective-permute-start | bytes 223496 | tf_op jit(solution)/shard_map/ppermute | solution.py:946
  30.2 14.3 %copy-start.22 = (f32[97,2,96]{2,1,0:T(2,128)}, f32[97,2,96]{2,1,0:T(2,128)S(1)}, u32[]{:S(2)}) copy-start(f32[97,2,96]{2,1,0:T(2,128)S(1)} %collective-permute-done) | copy-start | bytes 223492
  44.5 10.4 %all-to-all-start = ((bf16[2,45,96,192]{3,2,1,0:T(8,128)(2,1)}), bf16[2,45,96,192]{3,2,1,0:T(8,128)(2,1)}, u32[]{:S(2)}, u32[]{:S(2)}) async-start(bf16[2,45,96,192]{3,2,1,0:T(8,128)(2,1)} %bitcast.106), calls=%async_computation | async-start | bytes 8847360 | tf_op jit(solution)/shard_map/all_to_all | solution.py:941
  71.0 51.5 %all-to-all-start.3 = ((f32[8,6,48,384]{3,2,1,0:T(8,128)}), f32[8,6,48,384]{3,2,1,0:T(8,128)S(1)}, u32[]{:S(2)}, u32[]{:S(2)}) async-start(f32[8,6,48,384]{3,2,1,0:T(8,128)} %get-tuple-element.157), calls=%async_computation.3 | async-start | bytes 7077888 | tf_op jit(solution)/shard_map/all_to_all | solution.py:941
  87.0 4.7 collective-permute-start.3
  124.2 43.0 %all-to-all-start.2 = ((f32[8,6,48,384]{3,2,1,0:T(8,128)}), f32[8,6,48,384]{3,2,1,0:T(8,128)S(1)}, u32[]{:S(2)}, u32[]{:S(2)}) async-start(f32[8,6,48,384]{3,2,1,0:T(8,128)} %get-tuple-element.156), calls=%async_computation.2 | async-start | bytes 7077888 | tf_op jit(solution)/shard_map/all_to_all | solution.py:941
  131.3 23.7 %collective-permute-start.4 = (bf16[576,384]{1,0:T(8,128)(2,1)}, bf16[576,384]{1,0:T(8,128)(2,1)}, u32[]{:S(2)}, u32[]{:S(2)}) collective-permute-start(bf16[576,384]{1,0:T(8,128)(2,1)} %get-tuple-element.364), channel_id=1, source_target_pairs={{0,1},{1,2},{2,3},{3,0},{4,5},{5,6},{6,7},{7,4},{8,9},{9,10},{10,1... | collective-permute-start | bytes 1327112 | tf_op jit(solution)/shard_map/ppermute | solution.py:946
  132.3 32.7 %collective-permute-start.5 = (bf16[576,384]{1,0:T(8,128)(2,1)}, bf16[576,384]{1,0:T(8,128)(2,1)}, u32[]{:S(2)}, u32[]{:S(2)}) collective-permute-start(bf16[576,384]{1,0:T(8,128)(2,1)} %get-tuple-element.363), channel_id=1, source_target_pairs={{0,2},{1,3},{2,0},{3,1},{4,6},{5,7},{6,4},{7,5},{8,10},{9,11},{10,... | collective-permute-start | bytes 1327112 | tf_op jit(solution)/shard_map/ppermute | solution.py:946
  135.3 29.7 %collective-permute-start.6 = (bf16[576,384]{1,0:T(8,128)(2,1)}, bf16[576,384]{1,0:T(8,128)(2,1)}, u32[]{:S(2)}, u32[]{:S(2)}) collective-permute-start(bf16[576,384]{1,0:T(8,128)(2,1)} %get-tuple-element.362), channel_id=1, source_target_pairs={{0,3},{1,0},{2,1},{3,2},{4,7},{5,4},{6,5},{7,6},{8,11},{9,8},{10,9... | collective-permute-start | bytes 1327112 | tf_op jit(solution)/shard_map/ppermute | solution.py:946
  169.0 34.5 %all-to-all-start.4 = ((bf16[8,6,48,384]{3,2,1,0:T(8,128)(2,1)}), bf16[8,6,48,384]{3,2,1,0:T(8,128)(2,1)S(1)}, u32[]{:S(2)}, u32[]{:S(2)}) async-start(bf16[8,6,48,384]{3,2,1,0:T(8,128)(2,1)} %get-tuple-element.164), calls=%async_computation.4 | async-start | bytes 3538944 | tf_op jit(solution)/shard_map/all_to_all | solution.py:941
  176.0 7.9 %copy-start.14 = (f32[2,45,3,96]{3,1,2,0:T(8,128)S(1)}, f32[2,45,3,96]{3,1,2,0:T(8,128)}, u32[]{:S(2)}) copy-start(f32[2,45,3,96]{3,1,2,0:T(8,128)} %copy-done.13) | copy-start | bytes 311044
  178.4 25.1 %collective-permute-start.7 = (bf16[512,384]{1,0:T(8,128)(2,1)S(1)}, bf16[512,384]{1,0:T(8,128)(2,1)S(1)}, u32[]{:S(2)}, u32[]{:S(2)}) collective-permute-start(bf16[512,384]{1,0:T(8,128)(2,1)S(1)} %get-tuple-element.373), channel_id=1, source_target_pairs={{0,1},{1,2},{2,3},{3,0},{4,5},{5,6},{6,7},{7,4},{8,9},{9,10},{10,1... | collective-permute-start | bytes 1179656 | tf_op jit(solution)/shard_map/ppermute | solution.py:946
  203.5 12.2 %copy-start.2 = (bf16[8,6,48,384]{3,2,1,0:T(8,128)(2,1)}, bf16[8,6,48,384]{3,2,1,0:T(8,128)(2,1)S(1)}, u32[]{:S(2)}) copy-start(bf16[8,6,48,384]{3,2,1,0:T(8,128)(2,1)S(1)} %all-to-all-done.4.modes_a) | copy-start | bytes 5308420
  203.5 12.2 %slice-start.3 = ((f32[97,2,96]{2,1,0:T(2,128)}), f32[7,2,96]{2,1,0:T(2,128)S(1)}, s32[]{:S(2)}) async-start(f32[97,2,96]{2,1,0:T(2,128)} %copy-done.23), calls=%async_computation.28 | async-start | bytes 14336 | tf_op jit(solution)/shard_map/slice | solution.py:1108
  203.6 13.0 %slice-start.2 = ((f32[97,2,96]{2,1,0:T(2,128)}), f32[7,2,96]{2,1,0:T(2,128)S(1)}, s32[]{:S(2)}) async-start(f32[97,2,96]{2,1,0:T(2,128)} %copy-done.22), calls=%async_computation.27 | async-start | bytes 14336 | tf_op jit(solution)/shard_map/slice | solution.py:1108
  204.3 33.7 %all-to-all-start.5 = ((bf16[8,6,48,384]{3,2,1,0:T(8,128)(2,1)}), bf16[8,6,48,384]{3,2,1,0:T(8,128)(2,1)S(1)}, u32[]{:S(2)}, u32[]{:S(2)}) async-start(bf16[8,6,48,384]{3,2,1,0:T(8,128)(2,1)} %get-tuple-element.165), calls=%async_computation.5 | async-start | bytes 3538944 | tf_op jit(solution)/shard_map/all_to_all | solution.py:941
  217.9 20.1 %collective-permute-start.8 = (bf16[512,384]{1,0:T(8,128)(2,1)}, bf16[512,384]{1,0:T(8,128)(2,1)S(1)}, u32[]{:S(2)}, u32[]{:S(2)}) collective-permute-start(bf16[512,384]{1,0:T(8,128)(2,1)} %get-tuple-element.371), channel_id=1, source_target_pairs={{0,2},{1,3},{2,0},{3,1},{4,6},{5,7},{6,4},{7,5},{8,10},{9,11},{10,... | collective-permute-start | bytes 1179656 | tf_op jit(solution)/shard_map/ppermute | solution.py:946
  217.9 20.1 %collective-permute-start.9 = (bf16[512,384]{1,0:T(8,128)(2,1)}, bf16[512,384]{1,0:T(8,128)(2,1)S(1)}, u32[]{:S(2)}, u32[]{:S(2)}) collective-permute-start(bf16[512,384]{1,0:T(8,128)(2,1)} %get-tuple-element.370), channel_id=1, source_target_pairs={{0,3},{1,0},{2,1},{3,2},{4,7},{5,4},{6,5},{7,6},{8,11},{9,8},{10,9... | collective-permute-start | bytes 1179656 | tf_op jit(solution)/shard_map/ppermute | solution.py:946
  238.0 33.5 %copy-start.18 = (bf16[512,384]{1,0:T(8,128)(2,1)}, bf16[512,384]{1,0:T(8,128)(2,1)S(1)}, u32[]{:S(2)}) copy-start(bf16[512,384]{1,0:T(8,128)(2,1)S(1)} %collective-permute-done.8) | copy-start | bytes 1179652
  238.0 33.5 %copy-start.19 = (bf16[512,384]{1,0:T(8,128)(2,1)}, bf16[512,384]{1,0:T(8,128)(2,1)S(1)}, u32[]{:S(2)}) copy-start(bf16[512,384]{1,0:T(8,128)(2,1)S(1)} %collective-permute-done.9) | copy-start | bytes 1179652
  250.0 50.7 %all-to-all-start.7 = ((bf16[4,576,384]{2,1,0:T(8,128)(2,1)}), bf16[4,576,384]{2,1,0:T(8,128)(2,1)S(1)}, u32[]{:S(2)}, u32[]{:S(2)}) async-start(bf16[4,576,384]{2,1,0:T(8,128)(2,1)} %bitcast.115), calls=%async_computation.7 | async-start | bytes 3538944 | tf_op jit(solution)/shard_map/all_to_all | solution.py:941
  260.0 58.8 %collective-permute-start.10 = (bf16[4,3,128,768]{3,2,1,0:T(8,128)(2,1)}, bf16[4,3,128,768]{3,2,1,0:T(8,128)(2,1)}, u32[]{:S(2)}, u32[]{:S(2)}) collective-permute-start(bf16[4,3,128,768]{3,2,1,0:T(8,128)(2,1)} %bitcast.95), channel_id=1, source_target_pairs={{0,4},{4,0},{1,5},{5,1},{2,6},{6,2},{3,7},{7,3},{8,12},{12,8},{9,1... | collective-permute-start | bytes 7077896 | tf_op jit(solution)/shard_map/ppermute | solution.py:950
  260.7 58.1 %collective-permute-start.11 = (bf16[4,3,128,768]{3,2,1,0:T(8,128)(2,1)}, bf16[4,3,128,768]{3,2,1,0:T(8,128)(2,1)}, u32[]{:S(2)}, u32[]{:S(2)}) collective-permute-start(bf16[4,3,128,768]{3,2,1,0:T(8,128)(2,1)} %bitcast.100), channel_id=1, source_target_pairs={{0,4},{4,0},{1,5},{5,1},{2,6},{6,2},{3,7},{7,3},{8,12},{12,8},{9,1... | collective-permute-start | bytes 7077896 | tf_op jit(solution)/shard_map/ppermute | solution.py:950
  300.7 18.1 %copy-start = (bf16[4,576,384]{2,1,0:T(8,128)(2,1)}, bf16[4,576,384]{2,1,0:T(8,128)(2,1)S(1)}, u32[]{:S(2)}) copy-start(bf16[4,576,384]{2,1,0:T(8,128)(2,1)S(1)} %all-to-all-done.7.refs_0_.refs_1_.refs_2_.refs_3_) | copy-start | bytes 5308420
  300.7 76.2 %all-to-all-start.6 = ((bf16[4,512,384]{2,1,0:T(8,128)(2,1)}), bf16[4,512,384]{2,1,0:T(8,128)(2,1)S(1)}, u32[]{:S(2)}, u32[]{:S(2)}) async-start(bf16[4,512,384]{2,1,0:T(8,128)(2,1)} %bitcast.116), calls=%async_computation.6 | async-start | bytes 3145728 | tf_op jit(solution)/shard_map/all_to_all | solution.py:941
  376.9 59.6 %all-to-all-start.8 = ((bf16[4,576,384]{2,1,0:T(8,128)(2,1)}), bf16[4,576,384]{2,1,0:T(8,128)(2,1)S(1)}, u32[]{:S(2)}, u32[]{:S(2)}) async-start(bf16[4,576,384]{2,1,0:T(8,128)(2,1)} %get-tuple-element.206), calls=%async_computation.8 | async-start | bytes 3538944 | tf_op jit(solution)/shard_map/all_to_all | solution.py:941
  381.4 153.7 %reduce-scatter.3.cloned.1.call-start = ((), (), s32[]{:S(2)}) async-start(), calls=%async_computation.20 | async-start | bytes 5898240 | tf_op jit(solution)/shard_map/reduce_scatter | solution.py:1162
  436.5 9.6 %copy-start.11 = (bf16[4,384,768]{2,1,0:T(8,128)(2,1)S(1)}, bf16[4,384,768]{2,1,0:T(8,128)(2,1)}, u32[]{:S(2)}) copy-start(bf16[4,384,768]{2,1,0:T(8,128)(2,1)} %get-tuple-element.233) | copy-start | bytes 7077892
  436.5 6.2 collective-permute-start.19
  438.3 7.7 %collective-permute-start.20 = (bf16[4,384,768]{2,1,0:T(8,128)(2,1)}, bf16[4,384,768]{2,1,0:T(8,128)(2,1)S(1)}, u32[]{:S(2)}, u32[]{:S(2)}) collective-permute-start(bf16[4,384,768]{2,1,0:T(8,128)(2,1)} %get-tuple-element.234), channel_id=1, source_target_pairs={{0,4},{4,0},{1,5},{5,1},{2,6},{6,2},{3,7},{7,3},{8,12},{12,8},{9,1... | collective-permute-start | bytes 7077896 | tf_op jit(solution)/shard_map/ppermute | solution.py:950
  449.7 41.7 %all-to-all-start.9 = ((bf16[4,512,384]{2,1,0:T(8,128)(2,1)}), bf16[4,512,384]{2,1,0:T(8,128)(2,1)S(1)}, u32[]{:S(2)}, u32[]{:S(2)}) async-start(bf16[4,512,384]{2,1,0:T(8,128)(2,1)} %get-tuple-element.208), calls=%async_computation.9 | async-start | bytes 3145728 | tf_op jit(solution)/shard_map/all_to_all | solution.py:941
  456.6 3.3 collective-permute-start.13
  459.9 5.7 collective-permute-start.12
  472.6 10.7 %collective-permute-start.14 = (f32[1,1344]{1,0:T(1,128)S(1)}, f32[1,1344]{1,0:T(1,128)S(1)}, u32[]{:S(2)}, u32[]{:S(2)}) collective-permute-start(f32[1,1344]{1,0:T(1,128)S(1)} %get-tuple-element.384), channel_id=1, source_target_pairs={{0,1},{1,2},{2,3},{3,0},{4,5},{5,6},{6,7},{7,4},{8,9},{9,10},{10,1... | collective-permute-start | bytes 16136 | tf_op jit(solution)/shard_map/ppermute | solution.py:946
  474.4 16.9 %collective-permute-start.15 = (f32[1,1344]{1,0:T(1,128)S(1)}, f32[1,1344]{1,0:T(1,128)S(1)}, u32[]{:S(2)}, u32[]{:S(2)}) collective-permute-start(f32[1,1344]{1,0:T(1,128)S(1)} %get-tuple-element.385), channel_id=1, source_target_pairs={{0,2},{1,3},{2,0},{3,1},{4,6},{5,7},{6,4},{7,5},{8,10},{9,11},{10,... | collective-permute-start | bytes 16136 | tf_op jit(solution)/shard_map/ppermute | solution.py:946
  476.5 14.8 %collective-permute-start.16 = (f32[1,1344]{1,0:T(1,128)S(1)}, f32[1,1344]{1,0:T(1,128)S(1)}, u32[]{:S(2)}, u32[]{:S(2)}) collective-permute-start(f32[1,1344]{1,0:T(1,128)S(1)} %get-tuple-element.382), channel_id=1, source_target_pairs={{0,3},{1,0},{2,1},{3,2},{4,7},{5,4},{6,5},{7,6},{8,11},{9,8},{10,9... | collective-permute-start | bytes 16136 | tf_op jit(solution)/shard_map/ppermute | solution.py:946
  501.5 28.6 %all-to-all-start.10 = ((bf16[8,6,48,384]{3,2,1,0:T(8,128)(2,1)}), bf16[8,6,48,384]{3,2,1,0:T(8,128)(2,1)S(1)}, u32[]{:S(2)}, u32[]{:S(2)}) async-start(bf16[8,6,48,384]{3,2,1,0:T(8,128)(2,1)} %get-tuple-element.216), calls=%async_computation.10 | async-start | bytes 3538944 | tf_op jit(solution)/shard_map/all_to_all | solution.py:941
  508.0 13.6 %collective-permute-start.17 = (bf16[576,384]{1,0:T(8,128)(2,1)S(1)}, bf16[576,384]{1,0:T(8,128)(2,1)S(1)}, u32[]{:S(2)}, u32[]{:S(2)}) collective-permute-start(bf16[576,384]{1,0:T(8,128)(2,1)S(1)} %get-tuple-element.361), channel_id=1, source_target_pairs={{0,1},{1,2},{2,3},{3,0},{4,5},{5,6},{6,7},{7,4},{8,9},{9,10},{10,1... | collective-permute-start | bytes 1327112 | tf_op jit(solution)/shard_map/ppermute | solution.py:946
  508.4 20.9 %collective-permute-start.18 = (bf16[576,384]{1,0:T(8,128)(2,1)S(1)}, bf16[576,384]{1,0:T(8,128)(2,1)S(1)}, u32[]{:S(2)}, u32[]{:S(2)}) collective-permute-start(bf16[576,384]{1,0:T(8,128)(2,1)S(1)} %get-tuple-element.360), channel_id=1, source_target_pairs={{0,3},{1,0},{2,1},{3,2},{4,7},{5,4},{6,5},{7,6},{8,11},{9,8},{10,9... | collective-permute-start | bytes 1327112 | tf_op jit(solution)/shard_map/ppermute | solution.py:946
  521.6 7.7 %copy-start.16 = (bf16[576,384]{1,0:T(8,128)(2,1)}, bf16[576,384]{1,0:T(8,128)(2,1)S(1)}, u32[]{:S(2)}) copy-start(bf16[576,384]{1,0:T(8,128)(2,1)S(1)} %collective-permute-done.17) | copy-start | bytes 1327108
  530.1 24.6 %all-to-all-start.11 = ((bf16[8,6,48,384]{3,2,1,0:T(8,128)(2,1)}), bf16[8,6,48,384]{3,2,1,0:T(8,128)(2,1)S(1)}, u32[]{:S(2)}, u32[]{:S(2)}) async-start(bf16[8,6,48,384]{3,2,1,0:T(8,128)(2,1)} %get-tuple-element.222), calls=%async_computation.11 | async-start | bytes 3538944 | tf_op jit(solution)/shard_map/all_to_all | solution.py:941
  535.0 57.8 %reduce-scatter.5.cloned.1.call-start = ((), (), s32[]{:S(2)}) async-start(), calls=%async_computation.21 | async-start | bytes 1474560 | tf_op jit(solution)/shard_map/reduce_scatter | solution.py:1163
  554.7 11.3 %copy-start.7 = (bf16[8,6,48,384]{3,2,1,0:T(8,128)(2,1)}, bf16[8,6,48,384]{3,2,1,0:T(8,128)(2,1)S(1)}, u32[]{:S(2)}) copy-start(bf16[8,6,48,384]{3,2,1,0:T(8,128)(2,1)S(1)} %all-to-all-done.11.modes) | copy-start | bytes 5308420
  554.7 38.2 %all-to-all-start.12 = ((bf16[8,6,48,384]{3,2,1,0:T(8,128)(2,1)}), bf16[8,6,48,384]{3,2,1,0:T(8,128)(2,1)S(1)}, u32[]{:S(2)}, u32[]{:S(2)}) async-start(bf16[8,6,48,384]{3,2,1,0:T(8,128)(2,1)} %get-tuple-element.230), calls=%async_computation.12 | async-start | bytes 3538944 | tf_op jit(solution)/shard_map/all_to_all | solution.py:941
  561.7 70.1 %all-gather.11.cloned.1.call-start = ((), (), s32[]{:S(2)}) async-start(), calls=%async_computation.24 | async-start | bytes 2654208 | tf_op jit(solution)/shard_map/all_gather | solution.py:1201
  561.7 31.2 %collective-permute-start.21 = (bf16[576,384]{1,0:T(8,128)(2,1)}, bf16[576,384]{1,0:T(8,128)(2,1)}, u32[]{:S(2)}, u32[]{:S(2)}) collective-permute-start(bf16[576,384]{1,0:T(8,128)(2,1)} %get-tuple-element.358), channel_id=1, source_target_pairs={{0,2},{1,3},{2,0},{3,1},{4,6},{5,7},{6,4},{7,5},{8,10},{9,11},{10,... | collective-permute-start | bytes 1327112 | tf_op jit(solution)/shard_map/ppermute | solution.py:946
  566.0 18.9 %collective-permute-start.22 = (bf16[512,384]{1,0:T(8,128)(2,1)}, bf16[512,384]{1,0:T(8,128)(2,1)S(1)}, u32[]{:S(2)}, u32[]{:S(2)}) collective-permute-start(bf16[512,384]{1,0:T(8,128)(2,1)} %get-tuple-element.369), channel_id=1, source_target_pairs={{0,1},{1,2},{2,3},{3,0},{4,5},{5,6},{6,7},{7,4},{8,9},{9,10},{10,1... | collective-permute-start | bytes 1179656 | tf_op jit(solution)/shard_map/ppermute | solution.py:946
  584.9 14.4 %copy-start.29 = (f32[1,1344]{1,0:T(1,128)S(1)}, f32[1,1344]{1,0:T(1,128)}, u32[]{:S(2)}) copy-start(f32[1,1344]{1,0:T(1,128)} %copy-done.28) | copy-start | bytes 16132
  584.9 14.4 %copy-start.31 = (f32[1,1344]{1,0:T(1,128)S(1)}, f32[1,1344]{1,0:T(1,128)}, u32[]{:S(2)}) copy-start(f32[1,1344]{1,0:T(1,128)} %copy-done.30) | copy-start | bytes 16132
  592.9 28.6 %all-to-all-start.13 = ((bf16[8,6,48,384]{3,2,1,0:T(8,128)(2,1)}), bf16[8,6,48,384]{3,2,1,0:T(8,128)(2,1)}, u32[]{:S(2)}, u32[]{:S(2)}) async-start(bf16[8,6,48,384]{3,2,1,0:T(8,128)(2,1)} %get-tuple-element.239), calls=%async_computation.15 | async-start | bytes 3538944 | tf_op jit(solution)/shard_map/all_to_all | solution.py:941
  597.8 10.9 %collective-permute-start.23 = (bf16[512,384]{1,0:T(8,128)(2,1)}, bf16[512,384]{1,0:T(8,128)(2,1)}, u32[]{:S(2)}, u32[]{:S(2)}) collective-permute-start(bf16[512,384]{1,0:T(8,128)(2,1)} %get-tuple-element.368), channel_id=1, source_target_pairs={{0,3},{1,0},{2,1},{3,2},{4,7},{5,4},{6,5},{7,6},{8,11},{9,8},{10,9... | collective-permute-start | bytes 1179656 | tf_op jit(solution)/shard_map/ppermute | solution.py:946
  597.8 74.4 %collective-permute-start.24 = (bf16[512,384]{1,0:T(8,128)(2,1)}, bf16[512,384]{1,0:T(8,128)(2,1)}, u32[]{:S(2)}, u32[]{:S(2)}) collective-permute-start(bf16[512,384]{1,0:T(8,128)(2,1)} %get-tuple-element.366), channel_id=1, source_target_pairs={{0,2},{1,3},{2,0},{3,1},{4,6},{5,7},{6,4},{7,5},{8,10},{9,11},{10,... | collective-permute-start | bytes 1179656 | tf_op jit(solution)/shard_map/ppermute | solution.py:946
  635.8 35.4 %all-to-all-start.14 = ((f32[8,99,96]{1,2,0:T(8,128)}), f32[8,99,96]{1,2,0:T(8,128)}, u32[]{:S(2)}, u32[]{:S(2)}) async-start(f32[8,99,96]{1,2,0:T(8,128)} %pad_maximum_fusion.7), calls=%async_computation.16 | async-start | bytes 786432 | tf_op jit(solution)/shard_map/all_to_all | solution.py:941
  676.7 42.1 %collective-permute-start.25 = (f32[90,2,96]{2,1,0:T(2,128)S(1)}, f32[90,2,96]{2,1,0:T(2,128)}, u32[]{:S(2)}, u32[]{:S(2)}) collective-permute-start(f32[90,2,96]{2,1,0:T(2,128)S(1)} %bitcast.131), channel_id=1, source_target_pairs={{0,1},{1,2},{2,3},{3,0},{4,5},{5,6},{6,7},{7,4},{8,9},{9,10},{10,1... | collective-permute-start | bytes 207368 | tf_op jit(solution)/shard_map/ppermute | solution.py:946
  676.7 42.1 %collective-permute-start.26 = (f32[90,2,96]{2,1,0:T(2,128)S(1)}, f32[90,2,96]{2,1,0:T(2,128)}, u32[]{:S(2)}, u32[]{:S(2)}) collective-permute-start(f32[90,2,96]{2,1,0:T(2,128)S(1)} %bitcast.132), channel_id=1, source_target_pairs={{0,2},{1,3},{2,0},{3,1},{4,6},{5,7},{6,4},{7,5},{8,10},{9,11},{10,... | collective-permute-start | bytes 207368 | tf_op jit(solution)/shard_map/ppermute | solution.py:946
  678.2 40.6 %collective-permute-start.27 = (f32[90,2,96]{2,1,0:T(2,128)S(1)}, f32[90,2,96]{2,1,0:T(2,128)}, u32[]{:S(2)}, u32[]{:S(2)}) collective-permute-start(f32[90,2,96]{2,1,0:T(2,128)S(1)} %bitcast.133), channel_id=1, source_target_pairs={{0,3},{1,0},{2,1},{3,2},{4,7},{5,4},{6,5},{7,6},{8,11},{9,8},{10,9... | collective-permute-start | bytes 207368 | tf_op jit(solution)/shard_map/ppermute | solution.py:946
  680.5 15.8 %all-to-all-start.16 = ((f32[2,45,96,192]{3,2,1,0:T(8,128)}), f32[2,45,96,192]{3,2,1,0:T(8,128)}, u32[]{:S(2)}, u32[]{:S(2)}) async-start(f32[2,45,96,192]{3,2,1,0:T(8,128)} %get-tuple-element.257), calls=%async_computation.18 | async-start | bytes 17694720 | tf_op jit(solution)/shard_map/all_to_all | solution.py:941
  693.1 9.5 %copy-start.6 = (bf16[4352,384]{1,0:T(8,128)(2,1)}, bf16[4352,384]{1,0:T(8,128)(2,1)S(1)}, u32[]{:S(2)}) copy-start(bf16[4352,384]{1,0:T(8,128)(2,1)S(1)} %constant_dynamic-update-slice_fusion.pairs) | copy-start | bytes 10027012
  698.1 40.1 %all-to-all-start.17 = ((f32[8,103,96]{1,2,0:T(8,128)}), f32[8,103,96]{1,2,0:T(8,128)}, u32[]{:S(2)}, u32[]{:S(2)}) async-start(f32[8,103,96]{1,2,0:T(8,128)} %broadcast_in_dim.19), calls=%async_computation.19 | async-start | bytes 786432 | tf_op jit(solution)/shard_map/all_to_all | solution.py:941
  (27 other events, 88.1 us)
Sparse Core Ops, SparseCore 0:
  10.2 60.7 all-gather.6
  73.1 49.2 all-gather.8
  449.8 58.3 reduce-scatter.2
  537.9 28.5 reduce-scatter.4
  593.0 38.7 all-gather.10

commit v2 on v1

--- a/solution.py
+++ b/solution.py
@@ -193,6 +193,10 @@
 
 def full(shape):
     return pl.BlockSpec(shape, lambda *_: (0,) * len(shape))
+
+
+def once(shape, index):
+    return pl.BlockSpec(shape, index, pipeline_mode=pl.Buffered(1))
 
 
 def shape_of(shape, kind):
@@ -259,11 +263,29 @@
 PAIR_ROWS = 9
 
 
-def to_flat_kernel(pairs, flat, scratch):
-    chans = pairs.shape[1] // 2
+def place_pieces(blk, pieces, out):
+    first, size = 0, len(pieces) // 2
+    for half in (pieces[:size], pieces[size:]):
+        share = half[0].shape[0]
+        for by, piece in enumerate(half):
+            place = first + lax.rem(blk + size - by, size) * share
+            out[pl.ds(pl.multiple_of(place, 16), share), :] = piece[...]
+        first += size * share
+
+
+def to_flat_kernel(blk, *refs):
+    *pieces, flat, rows, scratch = refs
+    chans = rows.shape[1] // 2
     second = pl.program_id(0) == 1
+    step = pl.program_id(1)
+
+    @pl.when(jnp.logical_not(second) & (step == 0))
+    def _():
+        place_pieces(blk[0], pieces, rows)
+
     for q in range(PAIR_ROWS):
-        pair = pairs[q * SLOTS : (q + 1) * SLOTS, :].astype(wide)
+        start = pl.multiple_of((step * PAIR_ROWS + q) * SLOTS, SLOTS)
+        pair = rows[pl.ds(start, SLOTS), :].astype(wide)
         write_flat(scratch, q, jnp.where(second, pair[:, chans:], pair[:, :chans]))
     flat[0] = scratch[...].reshape(1, scratch.shape[0] * 128).astype(flat.dtype)
 
@@ -274,24 +296,33 @@
     return kept.reshape(1, 1, rows * 90 * chans)
 
 
-def to_flat(pairs):
-    chans = pairs.shape[1] // 2
+def to_flat(halves):
+    pieces = [piece for half in halves for piece in half]
+    chans = pieces[0].shape[1] // 2
     if chans != 192:
+        pairs = in_order(halves)
         grid = pairs[: 45 * SLOTS].reshape(45, SLOTS, 2, chans).transpose(2, 0, 1, 3)
         return plain_flat(grid.reshape(90, SLOTS, chans))
     block = PAIR_ROWS * 90 * chans
     steps = 45 // PAIR_ROWS
+    tokens = sum(piece.shape[0] for piece in pieces)
     return pl.pallas_call(
         to_flat_kernel,
-        grid=(2, steps),
-        in_specs=[pl.BlockSpec((PAIR_ROWS * SLOTS, 2 * chans), lambda h, i: (i, 0))],
-        out_specs=pl.BlockSpec((1, 1, block), lambda h, i: (0, 0, h * steps + i)),
-        out_shape=shape_of((1, 1, 90 * 90 * chans), pairs.dtype),
-        scratch_shapes=[pltpu.VMEM((block // 128, 128), wide)],
+        grid_spec=pltpu.PrefetchScalarGridSpec(
+            num_scalar_prefetch=1,
+            grid=(2, steps),
+            in_specs=[once(piece.shape, lambda *_: (0, 0)) for piece in pieces],
+            out_specs=pl.BlockSpec((1, 1, block), lambda h, i, at: (0, 0, h * steps + i)),
+            scratch_shapes=[
+                pltpu.VMEM((tokens, 2 * chans), narrow),
+                pltpu.VMEM((block // 128, 128), wide),
+            ],
+        ),
+        out_shape=shape_of((1, 1, 90 * 90 * chans), narrow),
         compiler_params=params(),
         cost_estimate=cost(1e6, 1e5),
         name="to_flat",
-    )(pairs)
+    )(lax.axis_index("blk").astype(jnp.int32).reshape(1), *pieces)
 
 
 def final_tile(base, field, sums, grad_sums):
@@ -306,48 +337,57 @@
     return base - cols[:, 1:2] - (field.astype(wide) - cols[:, 0:1]) * cols[:, 2:3]
 
 
-def final_kernel(base, field, sums, grad_sums, flat, scratch):
-    for q in range(FLAT_ROWS):
-        write_flat(scratch, q, final_tile(base[q], field[q], sums[q], grad_sums[q]))
-    flat[0] = scratch[...].reshape(1, scratch.shape[0] * 128)
-
-
-def final_grid_kernel(base, field, sums, grad_sums, out):
-    for q in range(FLAT_ROWS):
-        out[q] = final_tile(base[q], field[q], sums[q], grad_sums[q])
-
-
-def final_flat(base, field, sums, grad_sums):
-    rows, _, chans = base.shape
-    block = FLAT_ROWS * 90 * chans
-    tiles = pl.BlockSpec((FLAT_ROWS, SLOTS, chans), lambda i: (i, 0, 0))
-    pairs = pl.BlockSpec((FLAT_ROWS, 2, SLOTS), lambda i: (i, 0, 0))
-    common = dict(
-        grid=(rows // FLAT_ROWS,),
-        in_specs=[tiles, tiles, pairs, pairs],
+FINAL_ROWS = 15
+
+
+def final_kernel(place, kept, other, field, sums, grad_sums, flat, *scratch):
+    own = pl.program_id(0) // (45 // FINAL_ROWS) == place[0]
+    for q in range(FINAL_ROWS):
+        base = jnp.where(own, kept[q], other[q])
+        tile = final_tile(base, field[q], sums[q], grad_sums[q])
+        if scratch:
+            write_flat(scratch[0], q, tile)
+        else:
+            flat[q] = tile
+    if scratch:
+        flat[0] = scratch[0][...].reshape(1, scratch[0].shape[0] * 128)
+
+
+def final_flat(kept, other, field, sums, grad_sums):
+    rows, _, chans = field.shape
+    steps = 45 // FINAL_ROWS
+    block = FINAL_ROWS * 90 * chans
+
+    def half_of(which):
+        def index(i, at):
+            first = steps * (at[0] if which == 0 else 1 - at[0])
+            return (jnp.clip(i - first, 0, steps - 1), 0, 0)
+
+        return pl.BlockSpec((FINAL_ROWS, SLOTS, chans), index)
+
+    tiles = pl.BlockSpec((FINAL_ROWS, SLOTS, chans), lambda i, at: (i, 0, 0))
+    pairs = pl.BlockSpec((FINAL_ROWS, 2, SLOTS), lambda i, at: (i, 0, 0))
+    simple = chans != 192
+    out = pl.pallas_call(
+        final_kernel,
+        grid_spec=pltpu.PrefetchScalarGridSpec(
+            num_scalar_prefetch=1,
+            grid=(2 * steps,),
+            in_specs=[half_of(0), half_of(1), tiles, pairs, pairs],
+            out_specs=tiles if simple else pl.BlockSpec((1, 1, block), lambda i, at: (0, 0, i)),
+            scratch_shapes=[] if simple else [pltpu.VMEM((block // 128, 128), wide)],
+        ),
+        out_shape=shape_of(field.shape if simple else (1, 1, rows * 90 * chans), wide),
         compiler_params=params(),
         cost_estimate=cost(1e6, 1e5),
         name="final_flat",
-    )
-    if chans != 192:
-        return plain_flat(
-            pl.pallas_call(
-                final_grid_kernel,
-                out_specs=tiles,
-                out_shape=shape_of(base.shape, wide),
-                **common,
-            )(base, field, sums, grad_sums)
-        )
-    return pl.pallas_call(
-        final_kernel,
-        out_specs=pl.BlockSpec((1, 1, block), lambda i: (0, 0, i)),
-        out_shape=shape_of((1, 1, rows * 90 * chans), wide),
-        scratch_shapes=[pltpu.VMEM((block // 128, 128), wide)],
-        **common,
-    )(base, field, sums, grad_sums)
+    )(lax.axis_index("lon").astype(jnp.int32).reshape(1), kept, other, field, sums, grad_sums)
+    return plain_flat(out) if simple else out
 
 
 STEP = 9
+TOKEN_STEP = 8
+TOKEN_HALVES = ((0, 24), (24, 21))
 
 
 def spread_norm_kernel(field, sums, gain, shift, table, table_rest, out_a, out_b, *scratch):
@@ -367,17 +407,22 @@
     finish_spread(step, scratch, (out_a, out_b))
 
 
-def spread_kernel(grad, table, out_a, out_b, *scratch):
+def spread_kernel(first, second, table, out_a, out_b, *scratch):
     step = pl.program_id(0)
-    for q in range(STEP):
-        pair = grad[q * SLOTS : (q + 1) * SLOTS, :]
+    from_first = step < TOKEN_HALVES[0][1] // TOKEN_STEP
+    for q in range(TOKEN_STEP):
+        row = step * TOKEN_STEP + q
+        rows = slice(q * SLOTS, (q + 1) * SLOTS)
+        pair = jnp.where(from_first, first[rows, :], second[rows, :])
         chans = pair.shape[1] // 2
         modes = dot(table[...], jnp.concatenate([pair[:, :chans], pair[:, chans:]], axis=0))
         count = modes.shape[0] // 2
-        store_modes(
-            scratch, step * STEP + q, jnp.concatenate([modes[:count], modes[count:]], axis=1)
-        )
-    finish_spread(step, scratch, (out_a, out_b))
+        modes = jnp.concatenate([modes[:count], modes[count:]], axis=1)
+        store_modes(scratch, row, jnp.where(row < 45, modes, 0.0))
+
+    @pl.when(step == pl.num_programs(0) - 1)
+    def _():
+        flush_modes(scratch, (out_a, out_b))
 
 
 def finish_spread(step, scratch, out):
@@ -393,12 +438,12 @@
         flush_modes(scratch, out)
 
 
-def spread(inputs, in_specs, kernel, tables, group, lanes, kind, name):
+def spread(inputs, in_specs, kernel, tables, group, lanes, kind, steps, name):
     mode_total = tables[0].shape[0] // 2
     outs = [(group, count, ROW_PAD, lanes) for count in mode_parts(mode_total // group)]
     return pl.pallas_call(
         kernel,
-        grid=(45 // STEP,),
+        grid=(steps,),
         in_specs=in_specs + [full(table.shape) for table in tables],
         out_specs=[full(out) for out in outs],
         out_shape=[shape_of(out, kind) for out in outs],
@@ -407,10 +452,6 @@
         cost_estimate=cost(1e6, 1e5),
         name=name,
     )(*inputs, *tables)
-
-
-TOKEN_STEP = 8
-TOKEN_HALVES = ((0, 24), (24, 21))
 
 
 def collect_kernel(first, modes_a, modes_b, field, sums, gain, shift, table, out, *scratch):
@@ -434,10 +475,10 @@
 
 
 def spatial_rows(scratch, row, table, lanes):
-    count = table.shape[0] // 2
+    count = table.shape[1] // 2
     pair = load_modes(scratch, row, count, lanes).astype(narrow)
     stacked = jnp.concatenate([pair[:, : lanes // 2], pair[:, lanes // 2 :]], axis=0)
-    spatial = dot_tn(table[...], stacked)
+    spatial = dot(table[...], stacked)
     return spatial[:SLOTS], spatial[SLOTS:]
 
 
@@ -445,7 +486,7 @@
     chans = field.shape[3]
     first, count = rows
     skip = first // TOKEN_STEP
-    mode_total = table.shape[0] // 2
+    mode_total = table.shape[1] // 2
     return pl.pallas_call(
         functools.partial(collect_kernel, first),
         grid=(-(-count // TOKEN_STEP),),
@@ -466,7 +507,9 @@
     )(*modes, field, sums, gain, shift, table)
 
 
-def collect_back_kernel(modes_a, modes_b, grad, field, sums, gain, table, base, parts, small, *scratch):
+def collect_back_kernel(
+    place, modes_a, modes_b, grad, field, sums, gain, table, kept, sent, parts, small, *scratch
+):
     step = pl.program_id(0)
 
     @pl.when(step == 0)
@@ -481,52 +524,57 @@
         cols = norm_columns(sums[:, q])
         pair = grad[q * SLOTS : (q + 1) * SLOTS, :].astype(wide)
         chans = pair.shape[1] // 2
+        bases = []
         for side in range(2):
             inverse = cols[:, 2 * side + 1 : 2 * side + 2]
             normed = (field[side, q].astype(wide) - cols[:, 2 * side : 2 * side + 1]) * inverse
             middle = pair[:, side * chans : (side + 1) * chans]
             total = middle + spatial[side]
             scaled = total * gain[...]
-            base[side, q] = middle + inverse * scaled
+            bases.append(middle + inverse * scaled)
             turned = scaled * normed
             parts[side, q] = jnp.concatenate(
                 [token_sums(scaled)[:1], token_sums(turned)[:1]], axis=0
             )
             gain_sum = gain_sum + jnp.sum(total * normed, axis=0, keepdims=True)
             shift_sum = shift_sum + jnp.sum(total, axis=0, keepdims=True)
+        kept[q] = jnp.where(place[0] == 0, bases[0], bases[1])
+        sent[q] = jnp.where(place[0] == 0, bases[1], bases[0])
     small[0:1] += gain_sum
     small[1:2] += shift_sum
 
 
 def collect_back(modes, grad, field, sums, gain, table):
     chans = field.shape[3]
-    mode_total = table.shape[0] // 2
+    mode_total = table.shape[1] // 2
+    half_rows = pl.BlockSpec((STEP, SLOTS, chans), lambda i, at: (i, 0, 0))
+    pair_sums = pl.BlockSpec((2, STEP, 2, SLOTS), lambda i, at: (0, i, 0, 0))
     return pl.pallas_call(
         collect_back_kernel,
-        grid=(45 // STEP,),
-        in_specs=[
-            *[full(part.shape) for part in modes],
-            pl.BlockSpec((STEP * SLOTS, 2 * chans), lambda i: (i, 0)),
-            pl.BlockSpec((2, STEP, SLOTS, chans), lambda i: (0, i, 0, 0)),
-            pl.BlockSpec((2, STEP, 2, SLOTS), lambda i: (0, i, 0, 0)),
-            full(gain.shape),
-            full(table.shape),
-        ],
-        out_specs=[
-            pl.BlockSpec((2, STEP, SLOTS, chans), lambda i: (0, i, 0, 0)),
-            pl.BlockSpec((2, STEP, 2, SLOTS), lambda i: (0, i, 0, 0)),
-            full((8, chans)),
-        ],
+        grid_spec=pltpu.PrefetchScalarGridSpec(
+            num_scalar_prefetch=1,
+            grid=(45 // STEP,),
+            in_specs=[
+                *[full(part.shape) for part in modes],
+                pl.BlockSpec((STEP * SLOTS, 2 * chans), lambda i, at: (i, 0)),
+                pl.BlockSpec((2, STEP, SLOTS, chans), lambda i, at: (0, i, 0, 0)),
+                pair_sums,
+                full(gain.shape),
+                full(table.shape),
+            ],
+            out_specs=[half_rows, half_rows, pair_sums, full((8, chans))],
+            scratch_shapes=mode_scratch(mode_total, 2 * chans),
+        ),
         out_shape=[
-            shape_of(field.shape, wide),
+            shape_of(field.shape[1:], wide),
+            shape_of(field.shape[1:], wide),
             shape_of(sums.shape, wide),
             shape_of((8, chans), wide),
         ],
-        scratch_shapes=mode_scratch(mode_total, 2 * chans),
         compiler_params=params(),
         cost_estimate=cost(1e6, 1e5),
         name="collect_back",
-    )(*modes, grad, field, sums, gain, table)
+    )(lax.axis_index("lon").astype(jnp.int32).reshape(1), *modes, grad, field, sums, gain, table)
 
 
 def turn_rows(both):
@@ -679,7 +727,7 @@
 
 
 FF_TILE = 256
-WEIGHT_ROWS = 128
+CHUNKS = 4
 
 
 def token_tile(values, side, start, count):
@@ -706,9 +754,16 @@
     place,
     *refs,
 ):
-    middle, cot = refs[:blks], refs[blks : 2 * blks]
-    refs = refs[2 * blks :]
-    mlp_body(tile, place, middle, cot, *refs[:3], refs[3:7], refs[7:11], *refs[11:])
+    middle, pieces = refs[:blks], refs[blks : 2 * blks]
+    *refs, cot_all = refs[2 * blks :]
+
+    @pl.when(pl.program_id(0) == 0)
+    def _():
+        for by, piece in enumerate(pieces):
+            cot_all[pl.ds(lax.rem(place[0] + blks - by, blks), 1)] = piece[...][None]
+
+    cot = [cot_all.at[pl.ds(b, 1)] for b in range(blks)]
+    mlp_body(tile, place, middle, cot, *refs[:3], refs[3:5], refs[5:7], *refs[7:])
 
 
 def mlp_body(
@@ -752,35 +807,35 @@
                 branch[place, :] = jnp.zeros((tile, C), wide)
                 grad_sum[place, :] = jnp.zeros((tile, C), wide)
 
-    up_tile = jnp.concatenate(
-        [
-            jnp.where(first_core, ups[k][0, j], ups[2 + k][0, j])
-            for j in range(ups[0].shape[1])
-            for k in range(2)
-        ],
-        axis=0,
-    )
-    down_tile = jnp.concatenate(
-        [jnp.where(first_core, downs[2 + k][0, 0], downs[k][0, 0]) for k in range(2)], axis=0
-    )
+    up_tile = jnp.where(first_core, ups[0][0], ups[1][0])
+    down_tile = jnp.where(first_core, downs[1][0], downs[0][0])
     tokens, grads = tokens_in[...], grads_in[...]
-    before = dot(tokens, up_tile) + up_bias[...]
-    cumulative, density = normal_parts(before)
-    hidden = (before * cumulative).astype(narrow)
-    before_grad = (dot_nt(grads, down_tile) * (cumulative + before * density)).astype(narrow)
+    count = tokens.shape[0]
+    piece = count // CHUNKS
+    hidden, before_grad = [], []
+    for c in range(CHUNKS):
+        place = slice(c * piece, (c + 1) * piece)
+        before = dot(tokens[place], up_tile) + up_bias[...]
+        into = dot_nt(grads[place], down_tile)
+        cumulative, density = normal_parts(before)
+        hidden.append((before * cumulative).astype(narrow))
+        before_grad.append((into * (cumulative + before * density)).astype(narrow))
+    hidden, before_grad = jnp.concatenate(hidden, axis=0), jnp.concatenate(before_grad, axis=0)
     branch[...] += dot(hidden, down_tile)
     grad_sum[...] += dot_nt(before_grad, up_tile)
     rows = up_tile.shape[1] // 2
     for which, total in enumerate((dot_tn(before_grad, tokens), dot_tn(hidden, grads))):
-        first, second = total[:rows], total[rows:]
+        first, second = (
+            half.reshape(weight_grads[0].shape) for half in (total[:rows], total[rows:])
+        )
         parts = (
             jnp.where(first_core, first, second),
             jnp.where(first_core, second, first),
         )
         for k, part in enumerate(parts):
             if before_refs:
-                part = part + before_refs[2 * which + k][0].astype(wide)
-            weight_grads[2 * which + k][0] = part.astype(narrow)
+                part = part + before_refs[2 * which + k][...].astype(wide)
+            weight_grads[2 * which + k][...] = part.astype(narrow)
     bias_total = jnp.sum(before_grad.astype(wide), axis=0, keepdims=True)
     bias_grad[...] = bias_total + before_refs[4][...] if before_refs else bias_total
 
@@ -826,26 +881,19 @@
 def mlp(middle, cot, cols, gain, shift, weights, up_bias, down_bias, before):
     blks, share, lanes = middle.shape
     count = 2 * share
-    ff_here = weights[0].shape[3]
+    ff_here = weights[0].shape[2]
     per = ff_here // FF_TILE if ff_here % FF_TILE == 0 else 1
     width = ff_here // per
-    tile = share // 4 if share % 64 == 0 else share // 2
+    tile = share
     by_source = [
-        pl.BlockSpec((1, share, lanes), lambda i, at, b=b: (b, 0, 0)) for b in range(blks)
+        once((1, share, lanes), lambda i, at, b=b: (b, 0, 0)) for b in range(blks)
     ]
-    by_ring = [
-        pl.BlockSpec((1, share, lanes), lambda i, at, b=b: ((at[0] + blks - b) % blks, 0, 0))
-        for b in range(blks)
-    ]
-    grad_out = pl.BlockSpec((1, width // 2, C), lambda i, at: (i // per, i % per, 0))
+    by_ring = [once((share, lanes), lambda i, at: (0, 0))] * blks
+    lats = lax.axis_size("lat")
+    grad_shape = (lats, blks * per, width // 2 // lats, C)
+    grad_out = pl.BlockSpec((lats, 1) + grad_shape[2:], lambda i, at: (0, i, 0, 0))
     bias_out = pl.BlockSpec((1, width), lambda i, at: (0, i))
-    groups = weights[0].shape[1]
-    down_weights = weights
-    if ff_here != C:
-        down_weights = []
-        for first in (0, 2):
-            whole = jnp.stack(weights[first : first + 2], axis=2).reshape(blks, ff_here, C)
-            down_weights += jnp.split(whole[:, None], 2, axis=2)
+    down_weights = [part.reshape(blks, ff_here, C) for part in weights]
     return pl.pallas_call(
         functools.partial(mlp_kernel, tile, blks),
         grid_spec=pltpu.PrefetchScalarGridSpec(
@@ -857,16 +905,8 @@
                 full(cols.shape),
                 full(gain.shape),
                 full(shift.shape),
-                *[
-                    pl.BlockSpec(
-                        (1, groups, WEIGHT_ROWS, width), lambda i, at: (i // per, 0, 0, i % per)
-                    )
-                ]
-                * 4,
-                *[
-                    pl.BlockSpec((1, 1, width // 2, C), lambda i, at: (i // per, i % per, 0, 0))
-                ]
-                * 4,
+                *[pl.BlockSpec((1, C, width), lambda i, at: (i // per, 0, i % per))] * 2,
+                *[pl.BlockSpec((1, width, C), lambda i, at: (i // per, i % per, 0))] * 2,
                 bias_out,
                 full(down_bias.shape),
             ]
@@ -884,13 +924,14 @@
                 pltpu.VMEM((count, C), narrow),
                 pltpu.VMEM((count, C), wide),
                 pltpu.VMEM((count, C), wide),
+                pltpu.VMEM(middle.shape, narrow),
             ],
         ),
         out_shape=[
             shape_of((blks, share, lanes // 2), narrow),
             shape_of((blks, share, lanes // 2), narrow),
             shape_of(middle.shape, narrow),
-            *[shape_of((blks, ff_here // 2, C), narrow)] * 4,
+            *[shape_of(grad_shape, narrow)] * 4,
             shape_of((1, blks * ff_here), wide),
             shape_of((8, C), wide),
         ],
@@ -900,7 +941,7 @@
     )(
         jnp.stack([lax.axis_index("blk"), lax.axis_index("lon")]).astype(jnp.int32),
         *([middle] * blks),
-        *([cot] * blks),
+        *cot,
         cols,
         gain,
         shift,
@@ -913,16 +954,15 @@
 
 
 def weight_grads_kernel(pieces, up, down):
-    lons = pieces.shape[1]
+    lats, lons, tiles = pieces.shape[:3]
     for which, out in ((0, up), (1, down)):
-        halves = [
-            jnp.concatenate([pieces[lat, lon, which] for lat in range(pieces.shape[0])], axis=0)
+        rows = [
+            pieces[lat, lon, tile, which]
+            for tile in range(tiles)
             for lon in range(lons)
+            for lat in range(lats)
         ]
-        rows = halves[0].shape[0]
-        group = FF_TILE // 2 if 2 * rows % FF_TILE == 0 else rows
-        tiles = [half[k : k + group] for k in range(0, rows, group) for half in halves]
-        grad = jnp.concatenate(tiles, axis=0).astype(wide)
+        grad = jnp.concatenate(rows, axis=0).astype(wide)
         out[...] = jnp.transpose(grad) if which == 0 else grad
 
 
@@ -958,21 +998,17 @@
     return [values] + [shifted(values, axis, by) for by in range(1, lax.axis_size(axis))]
 
 
+def send_slices(values, axis):
+    size, here = lax.axis_size(axis), lax.axis_index(axis)
+    return [pick(values, here)] + [pick(values, (here + by) % size) for by in range(1, size)]
+
+
+def send_pieces(pieces, axis):
+    return pieces[:1] + [shifted(piece, axis, by) for by, piece in enumerate(pieces) if by]
+
+
 def send(values, axis):
-    size, here = lax.axis_size(axis), lax.axis_index(axis)
-    pieces = [pick(values, here)]
-    for by in range(1, size):
-        pieces.append(shifted(pick(values, (here + by) % size), axis, by))
-    return pieces
-
-
-def send_across(values, axis):
-    size, here = lax.axis_size(axis), lax.axis_index(axis)
-    pieces = [pick(values, here)]
-    for by in range(1, size):
-        turn = [(i, i ^ by) for i in range(size)]
-        pieces.append(lax.ppermute(pick(values, here ^ by), axis, turn))
-    return pieces
+    return send_pieces(send_slices(values, axis), axis)
 
 
 def in_order(halves):
@@ -1032,23 +1068,25 @@
     lanes = 2 * chans
     ff_here = up_bias.shape[0]
     ahead, ahead_rest = split_table(column_table(mode_total, False))
+    ahead_back, _ = split_table(column_table(mode_total, False).T)
     doubled, _ = split_table(column_table(mode_total, True))
+    doubled_back, _ = split_table(column_table(mode_total, True).T)
     turn, turn_rest = split_table(row_table(rows * lats, group))
     gain_row, shift_row = gain_one[None, :], shift_one[None, :]
 
     weight_own = jnp.where(lon == 0, up_weight, down_weight.reshape(up_weight.shape))
-    weight_own = weight_own.reshape(-1, 2, WEIGHT_ROWS, ff_here)
-    weights = [lax.all_gather(weight_own[:, k], "blk", axis=0, tiled=False) for k in range(2)]
+    weights = lax.all_gather(weight_own, "blk", axis=0, tiled=False)
 
     field_cols, sums_part = from_flat(field, rows, chans, True)
     row_params = jnp.concatenate([up_bias.astype(wide), down_bias, gain_two, shift_two])
     param_count = row_params.shape[0]
     row_params = jnp.pad(row_params, (0, -param_count % (2 * SLOTS))).reshape(-1, 2, SLOTS)
     sums_ring = ring(jnp.concatenate([sums_part, row_params]), "blk")
+    field_rows = swap_first(field_cols.reshape(2, half, SLOTS, chans), "lon")
+    field_rows, *sums_ring = tied(field_rows, *sums_ring)
     sums_cols = sum(piece[:rows] for piece in sums_ring)
     seen = presence.reshape(rows, 45, 2).transpose(0, 2, 1)
     seen = jnp.pad(seen, ((0, 0), (0, 0), (0, 3))).reshape(rows, 1, SLOTS).astype(wide)
-    field_rows = swap_first(field_cols.reshape(2, half, SLOTS, chans), "lon")
     scalars = jnp.concatenate([sums_cols, seen], axis=1).reshape(2, half, 3, SLOTS)
     scalars = swap_first(scalars, "lon")
     sums_rows = scalars[:, :, :2]
@@ -1066,9 +1104,10 @@
         group,
         lanes,
         wide,
+        45 // STEP,
         "spread_norm",
     )
-    cotangent, modes_a, modes_b, weights[0] = tied(cotangent, modes_a, modes_b, weights[0])
+    cotangent, modes_a, modes_b = tied(cotangent, modes_a, modes_b)
     modes_a = swap_first(modes_a, grid_axes)
     cot_cols = from_flat(cotangent, rows, chans, False).reshape(2, half, SLOTS, chans)
     cot_own, cot_other = pick(cot_cols, lon), other_core(pick(cot_cols, 1 - lon))
@@ -1083,20 +1122,6 @@
     cot_pairs = jnp.pad(cot_pairs.reshape(padded, lanes), ((0, tokens - padded), (0, 0)))
     w1, w2 = block_matrices(spec_w1, spec_w2)
     b1, b2 = spec_b1.reshape(1, lanes), spec_b2.reshape(1, lanes)
-    modes_b, cot_pairs, w1, w2, weights[1] = tied(modes_b, cot_pairs, w1, w2, weights[1])
-    modes_b = swap_first(modes_b, grid_axes)
-    cot_rings = [
-        send(cot_pairs[first : first + blks * share].reshape(blks, share, lanes), "blk")
-        for first, share in halves
-    ]
-    shrunk_a, *kept_a = spectral(modes_a, turn, turn_rest, w1, b1, w2, b2)
-    modes_b, shrunk_a, cot_rings[0] = tied(modes_b, shrunk_a, cot_rings[0])
-    shrunk_a = swap_first(shrunk_a, grid_axes)
-    weights_other = [other_core(part) for part in weights]
-    shrunk_b, *kept_b = spectral(modes_b, turn, turn_rest, w1, b1, w2, b2)
-    cot_b = cot_rings[1]
-    shrunk_b, shrunk_a, cot_b[1] = tied(shrunk_b, shrunk_a, cot_b[1])
-    shrunk_b = swap_first(shrunk_b, grid_axes)
     per_token = jnp.stack(
         [scalars[:, :, 0] * (1.0 / C), (1.0 + scalars[:, :, 2]) * 0.25], axis=-1
     ).reshape(2, padded, 2)
@@ -1106,17 +1131,30 @@
         for first, share in halves
     ]
     params_ring = jnp.stack([piece[rows:].reshape(-1)[:param_count] for piece in sums_ring])
-    params_all = jnp.concatenate([params_ring[:1], params_ring[:0:-1]])
-    params_all = jnp.concatenate([params_all, params_all])
-    params_all = lax.dynamic_slice_in_dim(params_all, blks - blk, blks, 0)
+    params_ring = [params_ring[k] for k in [0] + list(range(blks - 1, 0, -1))] * 2
+    params_all = lax.dynamic_slice_in_dim(jnp.stack(params_ring), blks - blk, blks, 0)
     bias_all = params_all[:, :ff_here].reshape(1, -1)
     token_params = [
         params_all[:, ff_here + i * chans : ff_here + (i + 1) * chans].reshape(1, C)
         for i in range(3)
     ]
-    shrunk_b, shrunk_a, per_token, bias_all, cot_rings, token_params = tied(
-        shrunk_b, shrunk_a, per_token, bias_all, cot_rings, token_params
-    )
+    modes_b, cot_pairs, w1, w2, weights, per_token, bias_all, token_params = tied(
+        modes_b, cot_pairs, w1, w2, weights, per_token, bias_all, token_params
+    )
+    modes_b = swap_first(modes_b, grid_axes)
+    cot_rings = [
+        send(cot_pairs[first : first + blks * share].reshape(blks, share, lanes), "blk")
+        for first, share in halves
+    ]
+    shrunk_a, *kept_a = spectral(modes_a, turn, turn_rest, w1, b1, w2, b2)
+    modes_b, shrunk_a, cot_rings[0] = tied(modes_b, shrunk_a, cot_rings[0])
+    shrunk_a = swap_first(shrunk_a, grid_axes)
+    weights_other = other_core(weights)
+    shrunk_b, *kept_b = spectral(modes_b, turn, turn_rest, w1, b1, w2, b2)
+    cot_b = cot_rings[1]
+    shrunk_b, shrunk_a, cot_b[1], cot_b[-1] = tied(shrunk_b, shrunk_a, cot_b[1], cot_b[-1])
+    shrunk_b = swap_first(shrunk_b, grid_axes)
+    shrunk_b, shrunk_a, cot_rings = tied(shrunk_b, shrunk_a, cot_rings)
 
     middles = []
     for (first, share), spans in zip(halves, TOKEN_HALVES):
@@ -1126,7 +1164,7 @@
             sums_rows,
             gain_row,
             shift_row,
-            doubled,
+            doubled_back,
             spans,
             blks * share,
         )
@@ -1136,11 +1174,11 @@
     for middle, cot_ring, scalar in zip(middles, cot_rings, per_token):
         kept, sent, middle_grad, *before = mlp(
             middle,
-            jnp.stack(cot_ring),
+            cot_ring,
             scalar,
             token_params[1],
             token_params[2],
-            [*weights, *weights_other],
+            (weights, weights_other),
             bias_all,
             token_params[0],
             before,
@@ -1151,17 +1189,17 @@
         grad_parts.append(swap_first(middle_grad, "blk"))
     up_kept, up_sent, down_kept, down_sent, bias_part, small_part = before
 
-    ff_half = ff_here // 2
     summed = jnp.stack(
         [
             (kept.astype(wide) + other_core(sent).astype(wide)).astype(narrow)
             for kept, sent in ((up_kept, up_sent), (down_kept, down_sent))
-        ]
-    ).reshape(2, blks, lats, ff_half // lats, C)
-    summed = summed.transpose(2, 1, 0, 3, 4).reshape(-1, C)
-    summed = lax.psum_scatter(summed, "lat", scatter_dimension=0, tiled=True)
+        ],
+        axis=2,
+    )
+    tile_shape = (-1,) + summed.shape[2:]
+    summed = lax.psum_scatter(summed.reshape(-1, C), "lat", scatter_dimension=0, tiled=True)
     total = lax.psum_scatter(summed, "blk", scatter_dimension=0, tiled=True)
-    total = total.reshape(2, ff_half // lats, C)
+    total = total.reshape(tile_shape)
     mixed_rows = []
     for kept, sent in mixed_parts:
         sent = other_core(sent)
@@ -1171,63 +1209,71 @@
             )
         )
     owned = small_part[:3].reshape(3, blks, chans).transpose(1, 0, 2).reshape(blks, -1)
-    owned = jnp.concatenate([owned, bias_part.reshape(blks, -1)], axis=1)
-    owned = send(owned[:, None, :], "blk")
+    owned = jnp.concatenate([owned, bias_part.reshape(blks, -1)], axis=1)[:, None, :]
     grad_parts[1], mixed_rows, owned = tied(grad_parts[1], mixed_rows, owned)
-    middle_grad = jnp.concatenate([part.reshape(-1, lanes) for part in grad_parts])
+    owned = send(owned, "blk")
 
     back_a, back_b = spread(
-        (middle_grad,),
-        [pl.BlockSpec((STEP * SLOTS, lanes), lambda i: (i, 0))],
+        [part.reshape(-1, lanes) for part in grad_parts],
+        [
+            pl.BlockSpec((TOKEN_STEP * SLOTS, lanes), lambda i: (jnp.minimum(i, 2), 0)),
+            pl.BlockSpec((TOKEN_STEP * SLOTS, lanes), lambda i: (jnp.maximum(i - 3, 0), 0)),
+        ],
         spread_kernel,
         (doubled,),
         group,
         lanes,
         narrow,
+        6,
         "spread_grad",
     )
-    ring_a, ring_b = [send(mixed, "blk") for mixed in mixed_rows]
+    ring_a = send(mixed_rows[0], "blk")
+    blk_pieces = send_slices(mixed_rows[1], "blk")
+    middle_grad = jnp.concatenate([part.reshape(-1, lanes) for part in grad_parts])
     back_a = swap_first(back_a, grid_axes)
     back_b, ring_a[1], ring_a[-1] = tied(back_b, ring_a[1], ring_a[-1])
     back_b = swap_first(back_b, grid_axes)
     back_a, *spec_sums = spectral_back(back_a, *kept_a, turn, w1, b1, w2, b2)
-    back_a, back_b = tied(back_a, back_b)
+    back_a, back_b, owned = tied(back_a, back_b, owned)
     back_a = swap_first(back_a, grid_axes)
     back_b, spec_grads, spec_small = spectral_back(
         back_b, *kept_b, turn, w1, b1, w2, b2, tuple(spec_sums)
     )
-    back_b, back_a, total, ring_a, ring_b[1] = tied(back_b, back_a, total, ring_a, ring_b[1])
+    back_b, back_a = tied(back_b, back_a)
     back_b = swap_first(back_b, grid_axes)
-    total = lax.all_gather(total, grid_axes, axis=0, tiled=False)
-    back_a, back_b, ring_b[-1], total, spec_grads = tied(
-        back_a, back_b, ring_b[-1], total, spec_grads
-    )
-
     vector = jnp.concatenate([spec_small[:2].reshape(-1), sum(owned).reshape(-1)])
     vector_size, vector_rows = vector.shape[0], -(-vector.shape[0] // (BS * group))
     vector = jnp.pad(vector, (0, group * vector_rows * BS - vector_size))
     shared = jnp.concatenate(
         [spec_grads.reshape(group, -1, BS), vector.reshape(group, vector_rows, BS)], axis=1
     )
+    back_a, back_b, total, shared, ring_a, blk_pieces, middle_grad = tied(
+        back_a, back_b, total, shared, ring_a, blk_pieces, middle_grad
+    )
+    total = lax.all_gather(total, grid_axes, axis=0, tiled=False)
+    ring_b = send_pieces(blk_pieces, "blk")
     shared = jnp.sum(swap_first(shared, grid_axes), axis=0)
 
-    base, part_sums, one_small = collect_back(
-        (back_a, back_b), middle_grad, field_rows, sums_rows, gain_row, ahead
-    )
-    base, part_sums, total, ring_b, shared = tied(base, part_sums, total, ring_b, shared)
-    grad_sums = swap_first(part_sums, "lon").reshape(rows, 2, SLOTS)
-    base, grad_sums = tied(base, grad_sums)
-    base = swap_first(base, "lon").reshape(rows, SLOTS, chans)
-    mixed = in_order((ring_a, ring_b))
-    base, mixed, one_small, total, shared = tied(base, mixed, one_small, total, shared)
-    mixed = to_flat(mixed)
+    base_kept, base_sent, part_sums, one_small = collect_back(
+        (back_a, back_b), middle_grad, field_rows, sums_rows, gain_row, ahead_back
+    )
+    base_kept, base_sent, part_sums, ring_b, shared = tied(
+        base_kept, base_sent, part_sums, ring_b, shared
+    )
+    grad_sums = jnp.broadcast_to(part_sums[:, None], (lons, blks) + part_sums.shape[1:])
+    grad_sums = swap_first(grad_sums.reshape((-1,) + part_sums.shape[1:]), ("lon", "blk"))
+    grad_sums = jnp.sum(grad_sums.reshape((lons, blks) + part_sums.shape[1:]), axis=1)
+    grad_sums = grad_sums.reshape(rows, 2, SLOTS)
+    base_other = other_core(base_sent)
+    mixed = to_flat((ring_a, ring_b))
+    base_other, grad_sums, one_small, total, shared, mixed = tied(
+        base_other, grad_sums, one_small, total, shared, mixed
+    )
     up_grad, down_grad = weight_grads(total, lons, ff_here)
     own_rows = shared.shape[0]
     shared = grid_broadcast(jnp.concatenate([shared, one_small[:2].reshape(-1, BS)]))
-    base, grad_sums, mixed, up_grad, down_grad = tied(
-        base, sum(ring(grad_sums, "blk")), mixed, up_grad, down_grad
-    )
-    input_grad = final_flat(base, field_cols, sums_cols, grad_sums)
+    grad_sums, mixed, up_grad, down_grad = tied(grad_sums, mixed, up_grad, down_grad)
+    input_grad = final_flat(base_kept, base_other, field_cols, sums_cols, grad_sums)
 
     one_small = jnp.sum(shared[:, own_rows:], axis=0).reshape(-1)
     vector = shared[:, own_rows - vector_rows : own_rows].reshape(-1)

time: 764 us -> 665 us (0.87)
  waiting for transfers between devices: 174 us -> 126 us
  starting transfers between devices: 136 us -> 120 us
  Pallas kernels: 310 us -> 298 us
  other arithmetic: 36.4 us -> 25.5 us
    all_gather x2 -> x1, waiting for transfers between devices: 25.3 us -> 3.14 us  [per_device(): weights = lax.all_gather(weight_own, 'blk', axis=0, tiled=False)]
    all_to_all x16, starting transfers between devices: 99.8 us -> 80.2 us  [swap_first(): return lax.all_to_all(values, axes, split_axis=0, concat_axis=0, tiled=True)]
    ppermute x21 -> x18, waiting for transfers between devices: 77.3 us -> 62.9 us  [shifted(): lax.ppermute(values, axis, [(i, (i + by) % size) for i in range(size)])]
    pallas_call x2, Pallas kernels: 110 us -> 99.3 us  [mlp(): pl.pallas_call(functools.partial(mlp_kernel, tile, blks), grid_spec=pltpu...]
    all_gather x1, waiting for transfers between devices: 10.3 us -> 0.01 us  [per_device(): total = lax.all_gather(total, grid_axes, axis=0, tiled=False)]
    dynamic_update_slice x8 -> x0, local copies, waits for them, and re-layouts: 8.62 us -> none  [in_order(): out = lax.dynamic_update_slice_in_dim(out, piece, place, 0)]
    ppermute x21 -> x18, starting transfers between devices: 32.4 us -> 33.2 us  [shifted(): lax.ppermute(values, axis, [(i, (i + by) % size) for i in range(size)])]
  transfers between devices with their start and end apart: 49 -> 45, of which waited for: 22 -> 14; matrix products, arithmetic and copies ran while one was open for 11% -> 10% of each run, Pallas kernels for 40% -> 44%
where the time goes in v2:
time: 665 us; the launch traced here: 654 us
  Pallas kernels  298 us (45%)
  waiting for transfers between devices  126 us (19%)
  starting transfers between devices  120 us (18%)
  local copies, waits for them, and re-layouts  66.2 us (10%)
  other arithmetic  25.5 us (4%)
  between operations  15 us (2%)
    pallas_call x2, Pallas kernels, mlp(): pl.pallas_call(functools.partial(mlp_kernel, tile, blks), grid_spec=pltpu...  99.3 us
    all_to_all x16, starting transfers between devices, swap_first(): return lax.all_to_all(values, axes, split_axis=0, concat_axis=0, tiled=True)  80.2 us
    ppermute x18, waiting for transfers between devices, shifted(): lax.ppermute(values, axis, [(i, (i + by) % size) for i in range(size)])  62.9 us
    all_to_all x16, waiting for transfers between devices, swap_first(): return lax.all_to_all(values, axes, split_axis=0, concat_axis=0, tiled=True)  53.5 us
    pallas_call x2, Pallas kernels, spectral_back(): pl.pallas_call(spectral_back_kernel, grid=(share,), in_specs=[mode_block,...  36.8 us
    pallas_call x2, Pallas kernels, spectral(): pl.pallas_call(spectral_kernel, grid=(share,), in_specs=[mode_block] + [f...  36.3 us
    ppermute x18, starting transfers between devices, shifted(): lax.ppermute(values, axis, [(i, (i + by) % size) for i in range(size)])  33.2 us
    pallas_call x1, Pallas kernels, collect_back(): pl.pallas_call(collect_back_kernel, grid_spec=pltpu.PrefetchScalarGridSpe...  27.9 us
  transfers between devices with their start and end apart: 45, of which 14 were waited for; matrix products, arithmetic and copies ran while one was open for 10% of the time, Pallas kernels for 44%

profile of v2, /device:TPU:1, one launch (start us, length us, event | category | flops | bytes accessed | tf_op | source)
XLA Modules:
  0.0 654.4 jit_solution(12310504995132023093)
XLA Ops:
  7.3 2.4 broadcast_select_fusion.2
  9.9 10.0 %from_flat.2 = (bf16[90,96,192]{2,1,0:T(8,128)(2,1)}, f32[90,2,96]{2,1,0:T(2,128)}) custom-call(bf16[1,1,1555200]{2,1,0:T(2,128)(2,1)} %flat.1), custom_call_target="tpu_custom_call" | custom-call | flops 1000000 | bytes 100000 | tf_op jit(solution)/shard_map/from_flat/pallas_call | solution.py:240
  20.8 2.2 collective-permute-start
  23.0 2.3 collective-permute-start.1
  26.4 7.3 %all-to-all-start = ((bf16[2,45,96,192]{3,2,1,0:T(8,128)(2,1)}), bf16[2,45,96,192]{3,2,1,0:T(8,128)(2,1)}, u32[]{:S(2)}, u32[]{:S(2)}) async-start(bf16[2,45,96,192]{3,2,1,0:T(8,128)(2,1)} %bitcast.103), calls=%async_computation | async-start | bytes 8847360 | tf_op jit(solution)/shard_map/all_to_all | solution.py:981
  34.1 3.9 all-to-all-done.field
  38.8 4.5 all_to_all.85
  44.6 15.6 %spread_norm.1 = (f32[8,6,48,384]{3,2,1,0:T(8,128)}, f32[8,6,48,384]{3,2,1,0:T(8,128)}) custom-call(bf16[2,45,96,192]{3,2,1,0:T(8,128)(2,1)} %all-to-all-done.field, f32[2,45,2,96]{3,2,1,0:T(2,128)} %copy.244.sums, f32[1,192]{1,0:T(1,128)} %bitcast.128, f32[1,192]{1,0:T(1,128)} %bitcast.132, bf16[192,192]{1,0:T(8,128)(2,1)} %constant.151.clone.table, ...), custom_call_target="tpu_custom_call" | custom-call | flops 1000000 | bytes 100000 | tf_op jit(solution)/shard_map/spread_norm/pallas_call | solution.py:444
  60.2 4.1 all-to-all-start.3
  64.3 8.4 %from_flat.3 = bf16[90,96,192]{2,1,0:T(8,128)(2,1)} custom-call(bf16[1,1,1555200]{2,1,0:T(2,128)(2,1)} %flat.2), custom_call_target="tpu_custom_call" | custom-call | flops 1000000 | bytes 100000 | tf_op jit(solution)/shard_map/from_flat/pallas_call | solution.py:240
  72.8 3.1 dynamic-slice_bitcast_fusion
  75.9 1.9 block_matrices.1
  87.0 1.8 copy.218
  101.1 2.6 bitcast_select_fusion.1
  104.9 2.1 pad.17
  107.0 3.1 all-gather.5.cloned.1.call-done
  112.0 4.9 all-to-all-start.2
  119.5 3.0 collective-permute-start.4
  122.5 3.8 collective-permute-start.5
  127.7 18.1 %spectral.2 = (bf16[8,6,48,384]{3,2,1,0:T(8,128)(2,1)}, bf16[6,384,384]{2,1,0:T(8,128)(2,1)}, bf16[6,384,384]{2,1,0:T(8,128)(2,1)}) custom-call(f32[8,6,48,384]{3,2,1,0:T(8,128)} %copy-done.6, bf16[768,384]{1,0:T(8,128)(2,1)} %constant.156.clone.table, bf16[768,384]{1,0:T(8,128)(2,1)} %constant.157.clone.table_rest, bf16[384,384]{1,0:T(8,128)(2,1)} %get-tuple-element.170.w1, ...), custom_call_target="tpu_custom_call" | custom-call | flops 1000000 | bytes 100000 | tf_op jit(solution)/shard_map/spectral/pallas_call | solution.py:615
  145.9 10.0 %collective-permute-done.5.refs_6_ = bf16[576,384]{1,0:T(8,128)(2,1)S(1)} collective-permute-done((bf16[576,384]{1,0:T(8,128)(2,1)}, bf16[576,384]{1,0:T(8,128)(2,1)S(1)}, u32[]{:S(2)}, u32[]{:S(2)}) %collective-permute-start.5) | collective-permute-done | bytes 442400 | tf_op jit(solution)/shard_map/ppermute | solution.py:986
  156.9 5.8 all-to-all-start.4
  165.1 8.0 %collective-permute-start.7 = (bf16[512,384]{1,0:T(8,128)(2,1)S(1)}, bf16[512,384]{1,0:T(8,128)(2,1)S(1)}, u32[]{:S(2)}, u32[]{:S(2)}) collective-permute-start(bf16[512,384]{1,0:T(8,128)(2,1)S(1)} %get-tuple-element.429), channel_id=1, source_target_pairs={{0,1},{1,2},{2,3},{3,0},{4,5},{5,6},{6,7},{7,4},{8,9},{9,10},{10,1... | collective-permute-start | bytes 1179656 | tf_op jit(solution)/shard_map/ppermute | solution.py:986
  173.1 18.2 %spectral.3 = (bf16[8,6,48,384]{3,2,1,0:T(8,128)(2,1)}, bf16[6,384,384]{2,1,0:T(8,128)(2,1)}, bf16[6,384,384]{2,1,0:T(8,128)(2,1)}) custom-call(f32[8,6,48,384]{3,2,1,0:T(8,128)} %all-to-all-done.2.modes, bf16[768,384]{1,0:T(8,128)(2,1)} %constant.156.clone.table, bf16[768,384]{1,0:T(8,128)(2,1)} %constant.157.clone.table_rest, ...), custom_call_target="tpu_custom_call" | custom-call | flops 1000000 | bytes 100000 | tf_op jit(solution)/shard_map/spectral/pallas_call | solution.py:615
  192.8 4.5 all-to-all-start.5
  198.5 19.2 %collective-permute-done.9.refs_6_ = bf16[512,384]{1,0:T(8,128)(2,1)} collective-permute-done((bf16[512,384]{1,0:T(8,128)(2,1)}, bf16[512,384]{1,0:T(8,128)(2,1)}, u32[]{:S(2)}, u32[]{:S(2)}) %collective-permute-start.9) | collective-permute-done | bytes 393248 | tf_op jit(solution)/shard_map/ppermute | solution.py:986
  218.9 9.7 %collect_norm.2 = bf16[2304,384]{1,0:T(8,128)(2,1)} custom-call(bf16[8,6,48,384]{3,2,1,0:T(8,128)(2,1)} %copy-done.4, bf16[8,6,48,384]{3,2,1,0:T(8,128)(2,1)} %copy-done.5, bf16[2,45,96,192]{3,2,1,0:T(8,128)(2,1)} %all-to-all-done.field, f32[2,45,2,96]{3,2,1,0:T(2,128)} %copy.244.sums, f32[1,192]{1,0:T(1,128)} %bitcast.129, f32[1,192]{1,0:T(1,128)} %bitcast.133, ...), custom_call_target="tpu_custom_call" | custom-call | flops 1000000 | bytes 100000 | tf_op jit(solution)/shard_map/collect_norm/pallas_call | solution.py:490
  228.6 3.7 all-to-all-start.7
  232.3 2.8 collective-permute-start.10
  235.1 9.7 %collect_norm.3 = bf16[2048,384]{1,0:T(8,128)(2,1)} custom-call(bf16[8,6,48,384]{3,2,1,0:T(8,128)(2,1)} %copy-done.4, bf16[8,6,48,384]{3,2,1,0:T(8,128)(2,1)} %copy-done.5, bf16[2,45,96,192]{3,2,1,0:T(8,128)(2,1)} %all-to-all-done.field, f32[2,45,2,96]{3,2,1,0:T(2,128)} %copy.244.sums, f32[1,192]{1,0:T(1,128)} %bitcast.130, f32[1,192]{1,0:T(1,128)} %bitcast.134, ...), custom_call_target="tpu_custom_call" | custom-call | flops 1000000 | bytes 100000 | tf_op jit(solution)/shard_map/collect_norm/pallas_call | solution.py:490
  244.8 28.2 %all-to-all-done.7.refs_0_.refs_1_.refs_2_.refs_3_ = bf16[4,576,384]{2,1,0:T(8,128)(2,1)S(1)} async-done(((bf16[4,576,384]{2,1,0:T(8,128)(2,1)}), bf16[4,576,384]{2,1,0:T(8,128)(2,1)S(1)}, u32[]{:S(2)}, u32[]{:S(2)}) %all-to-all-start.7) | async-done | bytes 1769504 | tf_op jit(solution)/shard_map/all_to_all | solution.py:981
  273.0 4.0 all-to-all-start.6
  277.5 52.1 %channel_mlp.2 = (bf16[4,576,192]{2,1,0:T(8,128)(2,1)}, bf16[4,576,192]{2,1,0:T(8,128)(2,1)}, bf16[4,576,384]{2,1,0:T(8,128)(2,1)}, bf16[4,12,32,768]{3,2,1,0:T(...) custom-call(s32[2]{0:T(128)} %pad_add_fusion.place, ...), custom_call_target="tpu_custom_call" | custom-call | flops 1000000 | bytes 100000 | tf_op jit(solution)/shard_map/channel_mlp/pallas_call | solution.py:897
  329.6 4.5 all-to-all-start.8
  334.3 47.3 %channel_mlp.3 = (bf16[4,512,192]{2,1,0:T(8,128)(2,1)}, bf16[4,512,192]{2,1,0:T(8,128)(2,1)}, bf16[4,512,384]{2,1,0:T(8,128)(2,1)}, bf16[4,12,32,768]{3,2,1,0:T(...) custom-call(s32[2]{0:T(128)} %pad_add_fusion.place, ...), custom_call_target="tpu_custom_call" | custom-call | flops 1000000 | bytes 100000 | tf_op jit(solution)/shard_map/channel_mlp/pallas_call | solution.py:897
  381.6 2.1 collective-permute-start.18
  383.8 4.3 collective-permute-done.18
  388.1 2.5 fusion
  392.8 2.7 copy.227
  395.5 5.0 all-to-all-start.9
  412.3 1.9 pad_maximum_fusion.3
  416.2 20.8 %all-to-all-done.9 = bf16[4,512,384]{2,1,0:T(8,128)(2,1)S(1)} async-done(((bf16[4,512,384]{2,1,0:T(8,128)(2,1)}), bf16[4,512,384]{2,1,0:T(8,128)(2,1)S(1)}, u32[]{:S(2)}, u32[]{:S(2)}) %all-to-all-start.9) | async-done | bytes 1572896 | tf_op jit(solution)/shard_map/all_to_all | solution.py:981
  438.2 8.7 %spread_grad.1 = (bf16[8,6,48,384]{3,2,1,0:T(8,128)(2,1)}, bf16[8,6,48,384]{3,2,1,0:T(8,128)(2,1)}) custom-call(bf16[2304,384]{1,0:T(8,128)(2,1)} %bitcast.106, bf16[2048,384]{1,0:T(8,128)(2,1)} %bitcast.108, bf16[192,192]{1,0:T(8,128)(2,1)} %constant.154.clone.table), custom_call_target="tpu_custom_call" | custom-call | flops 1000000 | bytes 100000 | tf_op jit(solution)/shard_map/spread_grad/pallas_call | solution.py:444
  446.9 5.3 all-to-all-start.10
  453.2 3.3 collective-permute-start.14
  456.5 10.4 %collective-permute-done.13.refs_1_ = bf16[576,384]{1,0:T(8,128)(2,1)S(1)} collective-permute-done((bf16[576,384]{1,0:T(8,128)(2,1)S(1)}, bf16[576,384]{1,0:T(8,128)(2,1)S(1)}, u32[]{:S(2)}, u32[]{:S(2)}) %collective-permute-start.13) | collective-permute-done | bytes 442400 | tf_op jit(solution)/shard_map/ppermute | solution.py:986
  466.9 7.6 %collective-permute-done.14.refs_3_ = bf16[576,384]{1,0:T(8,128)(2,1)S(1)} collective-permute-done((bf16[576,384]{1,0:T(8,128)(2,1)S(1)}, bf16[576,384]{1,0:T(8,128)(2,1)S(1)}, u32[]{:S(2)}, u32[]{:S(2)}) %collective-permute-start.14) | collective-permute-done | bytes 442400 | tf_op jit(solution)/shard_map/ppermute | solution.py:986
  475.3 4.6 all-to-all-start.11
  483.1 2.3 collective-permute-start.17
  485.4 18.0 %spectral_back.2 = (bf16[8,6,48,384]{3,2,1,0:T(8,128)(2,1)}, f32[8,384]{1,0:T(8,128)}, f32[384,384]{1,0:T(8,128)}, f32[384,384]{1,0:T(8,128)}) custom-call(bf16[8,6,48,384]{3,2,1,0:T(8,128)(2,1)} %copy-done.10, bf16[6,384,384]{2,1,0:T(8,128)(2,1)} %get-tuple-element.229.low, bf16[6,384,384]{2,1,0:T(8,128)(2,1)} %get-tuple-element.230.act, ...), custom_call_target="tpu_custom_call" | custom-call | flops 1000000 | bytes 100000 | tf_op jit(solution)/shard_map/spectral_back/pallas_call | solution.py:686
  504.0 5.1 all-to-all-start.12
  509.8 18.8 %spectral_back.3 = (bf16[8,6,48,384]{3,2,1,0:T(8,128)(2,1)}, f32[768,96]{1,0:T(8,128)}, f32[8,384]{1,0:T(8,128)}) custom-call(bf16[8,6,48,384]{3,2,1,0:T(8,128)(2,1)} %copy-done.9, bf16[6,384,384]{2,1,0:T(8,128)(2,1)} %get-tuple-element.237.low, bf16[6,384,384]{2,1,0:T(8,128)(2,1)} %get-tuple-element.238.act, bf16[768,384]{1,0:T(8,128)(2,1)} %constant.156.clone.table, ...), custom_call_target="tpu_custom_call" | custom-call | flops 1000000 | bytes 100000 | tf_op jit(solution)/shard_map/spectral_back/pallas_call | solution.py:686
  528.7 7.9 %all-to-all-start.13 = ((bf16[8,6,48,384]{3,2,1,0:T(8,128)(2,1)}), bf16[8,6,48,384]{3,2,1,0:T(8,128)(2,1)}, u32[]{:S(2)}, u32[]{:S(2)}) async-start(bf16[8,6,48,384]{3,2,1,0:T(8,128)(2,1)} %get-tuple-element.245), calls=%async_computation.13 | async-start | bytes 3538944 | tf_op jit(solution)/shard_map/all_to_all | solution.py:981
  537.0 2.1 pad_maximum_fusion.1.grad
  542.8 15.6 %collective-permute-done.20.refs_2_ = bf16[576,384]{1,0:T(8,128)(2,1)} collective-permute-done((bf16[576,384]{1,0:T(8,128)(2,1)}, bf16[576,384]{1,0:T(8,128)(2,1)}, u32[]{:S(2)}, u32[]{:S(2)}) %collective-permute-start.20) | collective-permute-done | bytes 442400 | tf_op jit(solution)/shard_map/ppermute | solution.py:986
  559.3 2.5 collective-permute-start.23
  561.8 5.4 all-to-all-start.14
  567.1 27.9 %collect_back.1 = (f32[45,96,192]{2,1,0:T(8,128)}, f32[45,96,192]{2,1,0:T(8,128)}, f32[2,45,2,96]{3,2,1,0:T(2,128)}, f32[8,192]{1,0:T(8,128)}) custom-call(s32[1]{0:T(128)} %bitcast.place, bf16[8,6,48,384]{3,2,1,0:T(8,128)(2,1)} %all-to-all-done.12.modes_a, bf16[8,6,48,384]{3,2,1,0:T(8,128)(2,1)} %all-to-all-done.13.modes_b, ...), custom_call_target="tpu_custom_call" | custom-call | flops 1000000 | bytes 100000 | tf_op jit(solution)/shard_map/collect_back/pallas_call | solution.py:552
  595.3 1.8 broadcast_in_dim.24
  597.2 3.7 all-to-all-start.15
  600.8 10.8 %to_flat.1 = bf16[1,1,1555200]{2,1,0:T(2,128)(2,1)} custom-call(s32[1]{0:T(128)} %bitcast.1.blk, bf16[576,384]{1,0:T(8,128)(2,1)} %get-tuple-element.275.refs_0_, bf16[576,384]{1,0:T(8,128)(2,1)} %copy-done.20, bf16[576,384]{1,0:T(8,128)(2,1)} %collective-permute-done.20.refs_2_, bf16[576,384]{1,0:T(8,128)(2,1)} %copy-done.21, ...), custom_call_target="tpu_custom_call" | custom-call | flops 1000000 | bytes 100000 | tf_op jit(solution)/shard_map/to_flat/pallas_call | solution.py:309
  614.7 4.5 all-to-all-start.16
  619.2 4.2 weight_grads.1
  623.5 18.2 %final_flat.1 = f32[1,1,1555200]{2,1,0:T(1,128)} custom-call(s32[1]{0:T(128)} %bitcast.place, f32[45,96,192]{2,1,0:T(8,128)} %get-tuple-element.289.kept, f32[45,96,192]{2,1,0:T(8,128)} %collective-permute-done.24.other, bf16[90,96,192]{2,1,0:T(8,128)(2,1)} %get-tuple-element.155.field, f32[90,2,96]{2,1,0:T(2,128)} %copy-done.15, f32[90,2,96]{2,1,0:T(2,128)} %bitcast.122), custom_call_target="tpu_custom_call" | custom-call | flops 1000000 | bytes 100000 | tf_op jit(solution)/shard_map/final_flat/pallas_call | solution.py:371
  (246 shorter events, 78.9 us)
Async XLA Ops:
  7.2 103.0 %all-gather.5.cloned.1.call-start = ((), (), s32[]{:S(2)}) async-start(), calls=%async_computation.21 | async-start | bytes 5898240 | tf_op jit(solution)/shard_map/all_gather | solution.py:1078
  20.8 17.2 %copy-start.28 = (f32[97,2,96]{2,1,0:T(2,128)}, f32[97,2,96]{2,1,0:T(2,128)S(1)}, u32[]{:S(2)}) copy-start(f32[97,2,96]{2,1,0:T(2,128)S(1)} %constant_dynamic-update-slice_fusion) | copy-start | bytes 223492
  20.8 17.2 %collective-permute-start = (f32[97,2,96]{2,1,0:T(2,128)S(1)}, f32[97,2,96]{2,1,0:T(2,128)S(1)}, u32[]{:S(2)}, u32[]{:S(2)}) collective-permute-start(f32[97,2,96]{2,1,0:T(2,128)S(1)} %constant_dynamic-update-slice_fusion), channel_id=1, source_target_pairs={{0,1},{1,2},{2,3},{3,0},{4,5},{5,6},{6,7},{7,4},{8,9},{9,10},{10,1... | collective-permute-start | bytes 223496 | tf_op jit(solution)/shard_map/ppermute | solution.py:986
  23.0 15.0 %collective-permute-start.1 = (f32[97,2,96]{2,1,0:T(2,128)S(1)}, f32[97,2,96]{2,1,0:T(2,128)S(1)}, u32[]{:S(2)}, u32[]{:S(2)}) collective-permute-start(f32[97,2,96]{2,1,0:T(2,128)S(1)} %constant_dynamic-update-slice_fusion), channel_id=1, source_target_pairs={{0,2},{1,3},{2,0},{3,1},{4,6},{5,7},{6,4},{7,5},{8,10},{9,11},{10,... | collective-permute-start | bytes 223496 | tf_op jit(solution)/shard_map/ppermute | solution.py:986
  25.3 12.7 %collective-permute-start.2 = (f32[97,2,96]{2,1,0:T(2,128)S(1)}, f32[97,2,96]{2,1,0:T(2,128)S(1)}, u32[]{:S(2)}, u32[]{:S(2)}) collective-permute-start(f32[97,2,96]{2,1,0:T(2,128)S(1)} %constant_dynamic-update-slice_fusion), channel_id=1, source_target_pairs={{0,3},{1,0},{2,1},{3,2},{4,7},{5,4},{6,5},{7,6},{8,11},{9,8},{10,9... | collective-permute-start | bytes 223496 | tf_op jit(solution)/shard_map/ppermute | solution.py:986
  26.4 7.3 %copy-start.33 = (s32[90,90]{1,0:T(8,128)S(1)}, s32[90,90]{1,0:T(8,128)}, u32[]{:S(2)}) copy-start(s32[90,90]{1,0:T(8,128)} %param.35) | copy-start | bytes 97204
  26.4 11.6 %all-to-all-start = ((bf16[2,45,96,192]{3,2,1,0:T(8,128)(2,1)}), bf16[2,45,96,192]{3,2,1,0:T(8,128)(2,1)}, u32[]{:S(2)}, u32[]{:S(2)}) async-start(bf16[2,45,96,192]{3,2,1,0:T(8,128)(2,1)} %bitcast.103), calls=%async_computation | async-start | bytes 8847360 | tf_op jit(solution)/shard_map/all_to_all | solution.py:981
  38.0 22.2 %copy-start.30 = (f32[97,2,96]{2,1,0:T(2,128)}, f32[97,2,96]{2,1,0:T(2,128)S(1)}, u32[]{:S(2)}) copy-start(f32[97,2,96]{2,1,0:T(2,128)S(1)} %collective-permute-done) | copy-start | bytes 223492
  38.0 22.2 %copy-start.31 = (f32[97,2,96]{2,1,0:T(2,128)}, f32[97,2,96]{2,1,0:T(2,128)S(1)}, u32[]{:S(2)}) copy-start(f32[97,2,96]{2,1,0:T(2,128)S(1)} %collective-permute-done.1) | copy-start | bytes 223492
  38.0 22.2 %copy-start.32 = (f32[97,2,96]{2,1,0:T(2,128)}, f32[97,2,96]{2,1,0:T(2,128)S(1)}, u32[]{:S(2)}) copy-start(f32[97,2,96]{2,1,0:T(2,128)S(1)} %collective-permute-done.2) | copy-start | bytes 223492
  60.2 49.9 %all-to-all-start.3 = ((f32[8,6,48,384]{3,2,1,0:T(8,128)}), f32[8,6,48,384]{3,2,1,0:T(8,128)S(1)}, u32[]{:S(2)}, u32[]{:S(2)}) async-start(f32[8,6,48,384]{3,2,1,0:T(8,128)} %get-tuple-element.169), calls=%async_computation.3 | async-start | bytes 7077888 | tf_op jit(solution)/shard_map/all_to_all | solution.py:981
  72.8 21.8 %slice-start.3 = ((f32[97,2,96]{2,1,0:T(2,128)}), f32[7,2,96]{2,1,0:T(2,128)S(1)}, s32[]{:S(2)}) async-start(f32[97,2,96]{2,1,0:T(2,128)} %copy-done.31), calls=%async_computation.26 | async-start | bytes 14336 | tf_op jit(solution)/shard_map/slice | solution.py:1133
  72.8 22.5 %slice-start.2 = ((f32[97,2,96]{2,1,0:T(2,128)}), f32[7,2,96]{2,1,0:T(2,128)S(1)}, s32[]{:S(2)}) async-start(f32[97,2,96]{2,1,0:T(2,128)} %copy-done.30), calls=%async_computation.25 | async-start | bytes 14336 | tf_op jit(solution)/shard_map/slice | solution.py:1133
  75.9 25.1 %collective-permute-start.3 = (bf16[45,96,192]{2,1,0:T(8,128)(2,1)}, bf16[45,96,192]{2,1,0:T(8,128)(2,1)}, u32[]{:S(2)}, u32[]{:S(2)}) collective-permute-start(bf16[45,96,192]{2,1,0:T(8,128)(2,1)} %dynamic-slice_bitcast_fusion), channel_id=1, source_target_pairs={{0,4},{4,0},{1,5},{5,1},{2,6},{6,2},{3,7},{7,3},{8,12},{12,8},{9,1... | collective-permute-start | bytes 4976648 | tf_op jit(solution)/shard_map/ppermute | solution.py:990
  112.0 44.0 %all-to-all-start.2 = ((f32[8,6,48,384]{3,2,1,0:T(8,128)}), f32[8,6,48,384]{3,2,1,0:T(8,128)}, u32[]{:S(2)}, u32[]{:S(2)}) async-start(f32[8,6,48,384]{3,2,1,0:T(8,128)} %get-tuple-element.168), calls=%async_computation.2 | async-start | bytes 7077888 | tf_op jit(solution)/shard_map/all_to_all | solution.py:981
  116.9 9.5 %copy-start.38 = (f32[2,2,96]{2,1,0:T(2,128)S(1)}, f32[2,2,96]{2,1,0:T(2,128)}, u32[]{:S(2)}) copy-start(f32[2,2,96]{2,1,0:T(2,128)} %param.26) | copy-start | bytes 4612
  116.9 10.2 %copy-start.39 = (f32[2,2,96]{2,1,0:T(2,128)S(1)}, f32[2,2,96]{2,1,0:T(2,128)}, u32[]{:S(2)}) copy-start(f32[2,2,96]{2,1,0:T(2,128)} %param.28) | copy-start | bytes 4612
  119.5 26.4 %collective-permute-start.4 = (bf16[576,384]{1,0:T(8,128)(2,1)}, bf16[576,384]{1,0:T(8,128)(2,1)S(1)}, u32[]{:S(2)}, u32[]{:S(2)}) collective-permute-start(bf16[576,384]{1,0:T(8,128)(2,1)} %get-tuple-element.420), channel_id=1, source_target_pairs={{0,1},{1,2},{2,3},{3,0},{4,5},{5,6},{6,7},{7,4},{8,9},{9,10},{10,1... | collective-permute-start | bytes 1327112 | tf_op jit(solution)/shard_map/ppermute | solution.py:986
  122.5 33.5 %collective-permute-start.5 = (bf16[576,384]{1,0:T(8,128)(2,1)}, bf16[576,384]{1,0:T(8,128)(2,1)S(1)}, u32[]{:S(2)}, u32[]{:S(2)}) collective-permute-start(bf16[576,384]{1,0:T(8,128)(2,1)} %get-tuple-element.419), channel_id=1, source_target_pairs={{0,2},{1,3},{2,0},{3,1},{4,6},{5,7},{6,4},{7,5},{8,10},{9,11},{10,... | collective-permute-start | bytes 1327112 | tf_op jit(solution)/shard_map/ppermute | solution.py:986
  126.2 29.7 %collective-permute-start.6 = (bf16[576,384]{1,0:T(8,128)(2,1)S(1)}, bf16[576,384]{1,0:T(8,128)(2,1)S(1)}, u32[]{:S(2)}, u32[]{:S(2)}) collective-permute-start(bf16[576,384]{1,0:T(8,128)(2,1)S(1)} %get-tuple-element.418), channel_id=1, source_target_pairs={{0,3},{1,0},{2,1},{3,2},{4,7},{5,4},{6,5},{7,6},{8,11},{9,8},{10,9... | collective-permute-start | bytes 1327112 | tf_op jit(solution)/shard_map/ppermute | solution.py:986
  145.9 10.1 %copy-start.17 = (bf16[576,384]{1,0:T(8,128)(2,1)}, bf16[576,384]{1,0:T(8,128)(2,1)S(1)}, u32[]{:S(2)}) copy-start(bf16[576,384]{1,0:T(8,128)(2,1)S(1)} %collective-permute-done.4.refs_5_) | copy-start | bytes 1327108
  156.9 35.2 %all-to-all-start.4 = ((bf16[8,6,48,384]{3,2,1,0:T(8,128)(2,1)}), bf16[8,6,48,384]{3,2,1,0:T(8,128)(2,1)S(1)}, u32[]{:S(2)}, u32[]{:S(2)}) async-start(bf16[8,6,48,384]{3,2,1,0:T(8,128)(2,1)} %get-tuple-element.176), calls=%async_computation.4 | async-start | bytes 3538944 | tf_op jit(solution)/shard_map/all_to_all | solution.py:981
  165.1 26.2 %collective-permute-start.7 = (bf16[512,384]{1,0:T(8,128)(2,1)S(1)}, bf16[512,384]{1,0:T(8,128)(2,1)S(1)}, u32[]{:S(2)}, u32[]{:S(2)}) collective-permute-start(bf16[512,384]{1,0:T(8,128)(2,1)S(1)} %get-tuple-element.429), channel_id=1, source_target_pairs={{0,1},{1,2},{2,3},{3,0},{4,5},{5,6},{6,7},{7,4},{8,9},{9,10},{10,1... | collective-permute-start | bytes 1179656 | tf_op jit(solution)/shard_map/ppermute | solution.py:986
  173.1 18.9 %collective-permute-start.8 = (bf16[512,384]{1,0:T(8,128)(2,1)S(1)}, bf16[512,384]{1,0:T(8,128)(2,1)S(1)}, u32[]{:S(2)}, u32[]{:S(2)}) collective-permute-start(bf16[512,384]{1,0:T(8,128)(2,1)S(1)} %get-tuple-element.428), channel_id=1, source_target_pairs={{0,3},{1,0},{2,1},{3,2},{4,7},{5,4},{6,5},{7,6},{8,11},{9,8},{10,9... | collective-permute-start | bytes 1179656 | tf_op jit(solution)/shard_map/ppermute | solution.py:986
  192.1 25.6 %copy-start.4 = (bf16[8,6,48,384]{3,2,1,0:T(8,128)(2,1)}, bf16[8,6,48,384]{3,2,1,0:T(8,128)(2,1)S(1)}, u32[]{:S(2)}) copy-start(bf16[8,6,48,384]{3,2,1,0:T(8,128)(2,1)S(1)} %all-to-all-done.4.modes_a) | copy-start | bytes 5308420
  192.8 24.9 %all-to-all-start.5 = ((bf16[8,6,48,384]{3,2,1,0:T(8,128)(2,1)}), bf16[8,6,48,384]{3,2,1,0:T(8,128)(2,1)S(1)}, u32[]{:S(2)}, u32[]{:S(2)}) async-start(bf16[8,6,48,384]{3,2,1,0:T(8,128)(2,1)} %get-tuple-element.177), calls=%async_computation.5 | async-start | bytes 3538944 | tf_op jit(solution)/shard_map/all_to_all | solution.py:981
  197.3 20.4 %collective-permute-start.9 = (bf16[512,384]{1,0:T(8,128)(2,1)}, bf16[512,384]{1,0:T(8,128)(2,1)}, u32[]{:S(2)}, u32[]{:S(2)}) collective-permute-start(bf16[512,384]{1,0:T(8,128)(2,1)} %get-tuple-element.426), channel_id=1, source_target_pairs={{0,2},{1,3},{2,0},{3,1},{4,6},{5,7},{6,4},{7,5},{8,10},{9,11},{10,... | collective-permute-start | bytes 1179656 | tf_op jit(solution)/shard_map/ppermute | solution.py:986
  228.6 44.3 %all-to-all-start.7 = ((bf16[4,576,384]{2,1,0:T(8,128)(2,1)}), bf16[4,576,384]{2,1,0:T(8,128)(2,1)S(1)}, u32[]{:S(2)}, u32[]{:S(2)}) async-start(bf16[4,576,384]{2,1,0:T(8,128)(2,1)} %bitcast.113), calls=%async_computation.7 | async-start | bytes 3538944 | tf_op jit(solution)/shard_map/all_to_all | solution.py:981
  232.3 45.2 %collective-permute-start.10 = (bf16[4,768,768]{2,1,0:T(8,128)(2,1)}, bf16[4,768,768]{2,1,0:T(8,128)(2,1)}, u32[]{:S(2)}, u32[]{:S(2)}) collective-permute-start(bf16[4,768,768]{2,1,0:T(8,128)(2,1)} %bitcast.97), channel_id=1, source_target_pairs={{0,4},{4,0},{1,5},{5,1},{2,6},{6,2},{3,7},{7,3},{8,12},{12,8},{9,1... | collective-permute-start | bytes 14155784 | tf_op jit(solution)/shard_map/ppermute | solution.py:990
  273.0 56.7 %all-to-all-start.6 = ((bf16[4,512,384]{2,1,0:T(8,128)(2,1)}), bf16[4,512,384]{2,1,0:T(8,128)(2,1)S(1)}, u32[]{:S(2)}, u32[]{:S(2)}) async-start(bf16[4,512,384]{2,1,0:T(8,128)(2,1)} %bitcast.114), calls=%async_computation.6 | async-start | bytes 3145728 | tf_op jit(solution)/shard_map/all_to_all | solution.py:981
  329.6 52.0 %all-to-all-start.8 = ((bf16[4,576,384]{2,1,0:T(8,128)(2,1)}), bf16[4,576,384]{2,1,0:T(8,128)(2,1)S(1)}, u32[]{:S(2)}, u32[]{:S(2)}) async-start(bf16[4,576,384]{2,1,0:T(8,128)(2,1)} %get-tuple-element.218), calls=%async_computation.8 | async-start | bytes 3538944 | tf_op jit(solution)/shard_map/all_to_all | solution.py:981
  334.2 174.9 %reduce-scatter.3.cloned.1.call-start = ((), (), s32[]{:S(2)}) async-start(), calls=%async_computation.19 | async-start | bytes 5898240 | tf_op jit(solution)/shard_map/reduce_scatter | solution.py:1200
  381.6 9.0 %copy-start.2 = (bf16[4,576,384]{2,1,0:T(8,128)(2,1)}, bf16[4,576,384]{2,1,0:T(8,128)(2,1)S(1)}, u32[]{:S(2)}) copy-start(bf16[4,576,384]{2,1,0:T(8,128)(2,1)S(1)} %all-to-all-done.8) | copy-start | bytes 5308420
  381.6 9.8 %copy-start.13 = (bf16[4,12,32,768]{3,2,1,0:T(8,128)(2,1)S(1)}, bf16[4,12,32,768]{3,2,1,0:T(8,128)(2,1)}, u32[]{:S(2)}) copy-start(bf16[4,12,32,768]{3,2,1,0:T(8,128)(2,1)} %get-tuple-element.248) | copy-start | bytes 7077892
  381.6 6.5 collective-permute-start.18
  383.7 7.7 %collective-permute-start.19 = (bf16[4,12,32,768]{3,2,1,0:T(8,128)(2,1)}, bf16[4,12,32,768]{3,2,1,0:T(8,128)(2,1)S(1)}, u32[]{:S(2)}, u32[]{:S(2)}) collective-permute-start(bf16[4,12,32,768]{3,2,1,0:T(8,128)(2,1)} %get-tuple-element.249), channel_id=1, source_target_pairs={{0,4},{4,0},{1,5},{5,1},{2,6},{6,2},{3,7},{7,3},{8,12},{12,8},{9,1... | collective-permute-start | bytes 7077896 | tf_op jit(solution)/shard_map/ppermute | solution.py:990
  395.5 7.2 %copy-start.14 = (bf16[4,576,192]{2,1,0:T(8,128)(2,1)S(1)}, bf16[4,576,192]{2,1,0:T(8,128)(2,1)}, u32[]{:S(2)}) copy-start(bf16[4,576,192]{2,1,0:T(8,128)(2,1)} %get-tuple-element.222) | copy-start | bytes 2654212
  395.5 41.5 %all-to-all-start.9 = ((bf16[4,512,384]{2,1,0:T(8,128)(2,1)}), bf16[4,512,384]{2,1,0:T(8,128)(2,1)S(1)}, u32[]{:S(2)}, u32[]{:S(2)}) async-start(bf16[4,512,384]{2,1,0:T(8,128)(2,1)} %get-tuple-element.220), calls=%async_computation.9 | async-start | bytes 3145728 | tf_op jit(solution)/shard_map/all_to_all | solution.py:981
  402.0 2.8 collective-permute-start.12
  404.0 5.2 collective-permute-start.11
  446.9 28.4 %all-to-all-start.10 = ((bf16[8,6,48,384]{3,2,1,0:T(8,128)(2,1)}), bf16[8,6,48,384]{3,2,1,0:T(8,128)(2,1)S(1)}, u32[]{:S(2)}, u32[]{:S(2)}) async-start(bf16[8,6,48,384]{3,2,1,0:T(8,128)(2,1)} %get-tuple-element.228), calls=%async_computation.10 | async-start | bytes 3538944 | tf_op jit(solution)/shard_map/all_to_all | solution.py:981
  453.2 13.6 %collective-permute-start.13 = (bf16[576,384]{1,0:T(8,128)(2,1)S(1)}, bf16[576,384]{1,0:T(8,128)(2,1)S(1)}, u32[]{:S(2)}, u32[]{:S(2)}) collective-permute-start(bf16[576,384]{1,0:T(8,128)(2,1)S(1)} %get-tuple-element.417), channel_id=1, source_target_pairs={{0,1},{1,2},{2,3},{3,0},{4,5},{5,6},{6,7},{7,4},{8,9},{9,10},{10,1... | collective-permute-start | bytes 1327112 | tf_op jit(solution)/shard_map/ppermute | solution.py:986
  453.2 21.3 %collective-permute-start.14 = (bf16[576,384]{1,0:T(8,128)(2,1)S(1)}, bf16[576,384]{1,0:T(8,128)(2,1)S(1)}, u32[]{:S(2)}, u32[]{:S(2)}) collective-permute-start(bf16[576,384]{1,0:T(8,128)(2,1)S(1)} %get-tuple-element.416), channel_id=1, source_target_pairs={{0,3},{1,0},{2,1},{3,2},{4,7},{5,4},{6,5},{7,6},{8,11},{9,8},{10,9... | collective-permute-start | bytes 1327112 | tf_op jit(solution)/shard_map/ppermute | solution.py:986
  466.9 7.6 %copy-start.20 = (bf16[576,384]{1,0:T(8,128)(2,1)}, bf16[576,384]{1,0:T(8,128)(2,1)S(1)}, u32[]{:S(2)}) copy-start(bf16[576,384]{1,0:T(8,128)(2,1)S(1)} %collective-permute-done.13.refs_1_) | copy-start | bytes 1327108
  475.3 10.1 %copy-start.10 = (bf16[8,6,48,384]{3,2,1,0:T(8,128)(2,1)}, bf16[8,6,48,384]{3,2,1,0:T(8,128)(2,1)S(1)}, u32[]{:S(2)}) copy-start(bf16[8,6,48,384]{3,2,1,0:T(8,128)(2,1)S(1)} %all-to-all-done.10.modes) | copy-start | bytes 5308420
  475.3 28.7 %all-to-all-start.11 = ((bf16[8,6,48,384]{3,2,1,0:T(8,128)(2,1)}), bf16[8,6,48,384]{3,2,1,0:T(8,128)(2,1)S(1)}, u32[]{:S(2)}, u32[]{:S(2)}) async-start(bf16[8,6,48,384]{3,2,1,0:T(8,128)(2,1)} %get-tuple-element.234), calls=%async_computation.11 | async-start | bytes 3538944 | tf_op jit(solution)/shard_map/all_to_all | solution.py:981
  480.8 22.6 %collective-permute-start.15 = (f32[1,1344]{1,0:T(1,128)S(1)}, f32[1,1344]{1,0:T(1,128)S(1)}, u32[]{:S(2)}, u32[]{:S(2)}) collective-permute-start(f32[1,1344]{1,0:T(1,128)S(1)} %get-tuple-element.441), channel_id=1, source_target_pairs={{0,1},{1,2},{2,3},{3,0},{4,5},{5,6},{6,7},{7,4},{8,9},{9,10},{10,1... | collective-permute-start | bytes 16136 | tf_op jit(solution)/shard_map/ppermute | solution.py:986
  481.5 21.9 %collective-permute-start.16 = (f32[1,1344]{1,0:T(1,128)S(1)}, f32[1,1344]{1,0:T(1,128)S(1)}, u32[]{:S(2)}, u32[]{:S(2)}) collective-permute-start(f32[1,1344]{1,0:T(1,128)S(1)} %get-tuple-element.440), channel_id=1, source_target_pairs={{0,2},{1,3},{2,0},{3,1},{4,6},{5,7},{6,4},{7,5},{8,10},{9,11},{10,... | collective-permute-start | bytes 16136 | tf_op jit(solution)/shard_map/ppermute | solution.py:986
  483.1 20.9 %collective-permute-start.17 = (f32[1,1344]{1,0:T(1,128)S(1)}, f32[1,1344]{1,0:T(1,128)}, u32[]{:S(2)}, u32[]{:S(2)}) collective-permute-start(f32[1,1344]{1,0:T(1,128)S(1)} %get-tuple-element.439), channel_id=1, source_target_pairs={{0,3},{1,0},{2,1},{3,2},{4,7},{5,4},{6,5},{7,6},{8,11},{9,8},{10,9... | collective-permute-start | bytes 16136 | tf_op jit(solution)/shard_map/ppermute | solution.py:986
  504.0 5.8 copy-start.9
  504.0 24.7 %all-to-all-start.12 = ((bf16[8,6,48,384]{3,2,1,0:T(8,128)(2,1)}), bf16[8,6,48,384]{3,2,1,0:T(8,128)(2,1)}, u32[]{:S(2)}, u32[]{:S(2)}) async-start(bf16[8,6,48,384]{3,2,1,0:T(8,128)(2,1)} %get-tuple-element.243), calls=%async_computation.12 | async-start | bytes 3538944 | tf_op jit(solution)/shard_map/all_to_all | solution.py:981
  509.1 49.3 %reduce-scatter.5.cloned.1.call-start = ((), (), s32[]{:S(2)}) async-start(), calls=%async_computation.20 | async-start | bytes 1474560 | tf_op jit(solution)/shard_map/reduce_scatter | solution.py:1201
  528.6 8.4 %copy-start.3 = (bf16[4,576,384]{2,1,0:T(8,128)(2,1)S(1)}, bf16[4,576,384]{2,1,0:T(8,128)(2,1)}, u32[]{:S(2)}) copy-start(bf16[4,576,384]{2,1,0:T(8,128)(2,1)} %copy-done.2) | copy-start | bytes 5308420
  528.6 8.4 %copy-start.8 = (bf16[4,512,384]{2,1,0:T(8,128)(2,1)S(1)}, bf16[4,512,384]{2,1,0:T(8,128)(2,1)}, u32[]{:S(2)}) copy-start(bf16[4,512,384]{2,1,0:T(8,128)(2,1)} %copy-done.7) | copy-start | bytes 4718596
  528.7 29.7 %all-to-all-start.13 = ((bf16[8,6,48,384]{3,2,1,0:T(8,128)(2,1)}), bf16[8,6,48,384]{3,2,1,0:T(8,128)(2,1)}, u32[]{:S(2)}, u32[]{:S(2)}) async-start(bf16[8,6,48,384]{3,2,1,0:T(8,128)(2,1)} %get-tuple-element.245), calls=%async_computation.13 | async-start | bytes 3538944 | tf_op jit(solution)/shard_map/all_to_all | solution.py:981
  536.6 76.3 %all-gather.7.cloned.1.call-start = ((), (), s32[]{:S(2)}) async-start(), calls=%async_computation.22 | async-start | bytes 2654208 | tf_op jit(solution)/shard_map/all_gather | solution.py:1253
  536.6 21.8 %collective-permute-start.20 = (bf16[576,384]{1,0:T(8,128)(2,1)}, bf16[576,384]{1,0:T(8,128)(2,1)}, u32[]{:S(2)}, u32[]{:S(2)}) collective-permute-start(bf16[576,384]{1,0:T(8,128)(2,1)} %get-tuple-element.414), channel_id=1, source_target_pairs={{0,2},{1,3},{2,0},{3,1},{4,6},{5,7},{6,4},{7,5},{8,10},{9,11},{10,... | collective-permute-start | bytes 1327112 | tf_op jit(solution)/shard_map/ppermute | solution.py:986
  558.4 36.6 %collective-permute-start.21 = (bf16[512,384]{1,0:T(8,128)(2,1)S(1)}, bf16[512,384]{1,0:T(8,128)(2,1)S(1)}, u32[]{:S(2)}, u32[]{:S(2)}) collective-permute-start(bf16[512,384]{1,0:T(8,128)(2,1)S(1)} %get-tuple-element.266), channel_id=1, source_target_pairs={{0,1},{1,2},{2,3},{3,0},{4,5},{5,6},{6,7},{7,4},{8,9},{9,10},{10,1... | collective-permute-start | bytes 1179656 | tf_op jit(solution)/shard_map/ppermute | solution.py:986
  558.5 36.6 %collective-permute-start.22 = (bf16[512,384]{1,0:T(8,128)(2,1)S(1)}, bf16[512,384]{1,0:T(8,128)(2,1)S(1)}, u32[]{:S(2)}, u32[]{:S(2)}) collective-permute-start(bf16[512,384]{1,0:T(8,128)(2,1)S(1)} %get-tuple-element.267), channel_id=1, source_target_pairs={{0,2},{1,3},{2,0},{3,1},{4,6},{5,7},{6,4},{7,5},{8,10},{9,11},{10,... | collective-permute-start | bytes 1179656 | tf_op jit(solution)/shard_map/ppermute | solution.py:986
  559.3 35.8 %collective-permute-start.23 = (bf16[512,384]{1,0:T(8,128)(2,1)S(1)}, bf16[512,384]{1,0:T(8,128)(2,1)S(1)}, u32[]{:S(2)}, u32[]{:S(2)}) collective-permute-start(bf16[512,384]{1,0:T(8,128)(2,1)S(1)} %get-tuple-element.268), channel_id=1, source_target_pairs={{0,3},{1,0},{2,1},{3,2},{4,7},{5,4},{6,5},{7,6},{8,11},{9,8},{10,9... | collective-permute-start | bytes 1179656 | tf_op jit(solution)/shard_map/ppermute | solution.py:986
  561.8 33.3 %all-to-all-start.14 = ((f32[8,99,96]{1,2,0:T(8,128)}), f32[8,99,96]{1,2,0:T(8,128)S(1)}, u32[]{:S(2)}, u32[]{:S(2)}) async-start(f32[8,99,96]{1,2,0:T(8,128)} %pad_maximum_fusion.5), calls=%async_computation.16 | async-start | bytes 786432 | tf_op jit(solution)/shard_map/all_to_all | solution.py:981
  595.2 17.8 %collective-permute-start.24 = (f32[45,96,192]{2,1,0:T(8,128)}, f32[45,96,192]{2,1,0:T(8,128)}, u32[]{:S(2)}, u32[]{:S(2)}) collective-permute-start(f32[45,96,192]{2,1,0:T(8,128)} %get-tuple-element.270), channel_id=1, source_target_pairs={{0,4},{4,0},{1,5},{5,1},{2,6},{6,2},{3,7},{7,3},{8,12},{12,8},{9,1... | collective-permute-start | bytes 9953288 | tf_op jit(solution)/shard_map/ppermute | solution.py:990
  597.2 15.0 %all-to-all-start.15 = ((f32[8,45,2,96]{3,2,1,0:T(2,128)}), f32[8,45,2,96]{3,2,1,0:T(2,128)S(1)}, u32[]{:S(2)}, u32[]{:S(2)}) async-start(f32[8,45,2,96]{3,2,1,0:T(2,128)} %bitcast.47), calls=%async_computation.17 | async-start | bytes 737280 | tf_op jit(solution)/shard_map/all_to_all | solution.py:981
  614.7 27.0 %all-to-all-start.16 = ((f32[8,103,96]{1,2,0:T(8,128)}), f32[8,103,96]{1,2,0:T(8,128)S(1)}, u32[]{:S(2)}, u32[]{:S(2)}) async-start(f32[8,103,96]{1,2,0:T(8,128)} %broadcast_in_dim.25), calls=%async_computation.18 | async-start | bytes 786432 | tf_op jit(solution)/shard_map/all_to_all | solution.py:981
  (29 other events, 66.5 us)
Sparse Core Ops, SparseCore 0:
  10.2 99.9 all-gather.4
  395.6 58.4 reduce-scatter.2
  512.2 27.1 reduce-scatter.4
  558.6 31.7 all-gather.6

commit v3 on v2

--- a/solution.py
+++ b/solution.py
@@ -332,9 +332,9 @@
     shift = inverse * grad_sums[0:1] * (1.0 / C)
     slope = inverse * inverse * grad_sums[1:2] * (1.0 / C)
     cols = jnp.transpose(
-        jnp.concatenate([mean, shift, slope, jnp.zeros((5, SLOTS), wide)], axis=0)
-    )
-    return base - cols[:, 1:2] - (field.astype(wide) - cols[:, 0:1]) * cols[:, 2:3]
+        jnp.concatenate([mean * slope - shift, slope, jnp.zeros((6, SLOTS), wide)], axis=0)
+    )
+    return (base + cols[:, 0:1]) - field.astype(wide) * cols[:, 1:2]
 
 
 FINAL_ROWS = 15
@@ -745,7 +745,7 @@
     mean = jnp.mean(values, axis=1, keepdims=True)
     offset = values - mean
     inverse = lax.rsqrt(jnp.mean(offset * offset, axis=1, keepdims=True) + EPS)
-    return offset * inverse, inverse
+    return offset * inverse, mean, inverse
 
 
 def mlp_kernel(
@@ -780,10 +780,10 @@
     down_bias,
     *rest,
 ):
-    before_refs = rest[:-13]
-    mixed_kept, mixed_sent, middle_grad = rest[-13:-10]
-    weight_grads, (bias_grad, small) = rest[-10:-6], rest[-6:-4]
-    tokens_in, grads_in, branch, grad_sum = rest[-4:]
+    before_refs = rest[:-14]
+    mixed_kept, mixed_sent, middle_grad = rest[-14:-11]
+    weight_grads, (bias_grad, small) = rest[-11:-7], rest[-7:-5]
+    tokens_in, grads_in, branch, grad_sum, norm_cols = rest[-5:]
     first_core = here[1] == 0
     step = pl.program_id(0)
     share = middle[0].shape[1]
@@ -798,7 +798,9 @@
             def _(piece):
                 start = pl.multiple_of(piece * tile, 16)
                 place = pl.ds(pl.multiple_of(side * share + piece * tile, 16), tile)
-                normed, _ = norm_two(token_tile(middle, side, start, tile))
+                normed, mean, inverse = norm_two(token_tile(middle, side, start, tile))
+                norm_cols[place, 0:1] = mean
+                norm_cols[place, 1:2] = inverse
                 tokens_in[place, :] = (normed * gain[...] + shift[...]).astype(narrow)
                 weight = cols[place, 1:2]
                 grad = (token_tile(cot, side, start, tile) * weight).astype(narrow)
@@ -848,7 +850,8 @@
                 start = pl.multiple_of(piece * tile, 16)
                 place = pl.ds(pl.multiple_of(side * share + piece * tile, 16), tile)
                 values = token_tile(middle, side, start, tile)
-                normed, inverse = norm_two(values)
+                inverse = norm_cols[place, 1:2]
+                normed = (values - norm_cols[place, 0:1]) * inverse
                 result = (
                     values + cols[place, 0:1] + (branch[place, :] + down_bias[...])
                 ).astype(narrow)
@@ -924,6 +927,7 @@
                 pltpu.VMEM((count, C), narrow),
                 pltpu.VMEM((count, C), wide),
                 pltpu.VMEM((count, C), wide),
+                pltpu.VMEM((count, 2), wide),
                 pltpu.VMEM(middle.shape, narrow),
             ],
         ),

time: 665 us -> 663 us (level)
  no operation moved by 1% of the time
where the time goes in v3:
time: 663 us; the launch traced here: 652 us
  Pallas kernels  296 us (45%)
  waiting for transfers between devices  126 us (19%)
  starting transfers between devices  119 us (18%)
  local copies, waits for them, and re-layouts  66.2 us (10%)
  other arithmetic  25.5 us (4%)
  between operations  15 us (2%)
    pallas_call x2, Pallas kernels, mlp(): pl.pallas_call(functools.partial(mlp_kernel, tile, blks), grid_spec=pltpu...  99.2 us
    all_to_all x16, starting transfers between devices, swap_first(): return lax.all_to_all(values, axes, split_axis=0, concat_axis=0, tiled=True)  80 us
    ppermute x18, waiting for transfers between devices, shifted(): lax.ppermute(values, axis, [(i, (i + by) % size) for i in range(size)])  62.9 us
    all_to_all x16, waiting for transfers between devices, swap_first(): return lax.all_to_all(values, axes, split_axis=0, concat_axis=0, tiled=True)  53.5 us
    pallas_call x2, Pallas kernels, spectral_back(): pl.pallas_call(spectral_back_kernel, grid=(share,), in_specs=[mode_block,...  36.8 us
    pallas_call x2, Pallas kernels, spectral(): pl.pallas_call(spectral_kernel, grid=(share,), in_specs=[mode_block] + [f...  36.3 us
    ppermute x18, starting transfers between devices, shifted(): lax.ppermute(values, axis, [(i, (i + by) % size) for i in range(size)])  33.2 us
    pallas_call x1, Pallas kernels, collect_back(): pl.pallas_call(collect_back_kernel, grid_spec=pltpu.PrefetchScalarGridSpe...  27.9 us
  transfers between devices with their start and end apart: 45, of which 14 were waited for; matrix products, arithmetic and copies ran while one was open for 10% of the time, Pallas kernels for 44%

profile of v3, /device:TPU:1, one launch (start us, length us, event | category | flops | bytes accessed | tf_op | source)
XLA Modules:
  0.0 652.3 jit_solution(2826748732659719268)
XLA Ops:
  7.3 2.4 broadcast_select_fusion.2
  9.9 10.0 %from_flat.2 = (bf16[90,96,192]{2,1,0:T(8,128)(2,1)}, f32[90,2,96]{2,1,0:T(2,128)}) custom-call(bf16[1,1,1555200]{2,1,0:T(2,128)(2,1)} %flat.1), custom_call_target="tpu_custom_call" | custom-call | flops 1000000 | bytes 100000 | tf_op jit(solution)/shard_map/from_flat/pallas_call | solution.py:240
  20.8 2.2 collective-permute-start
  23.0 2.3 collective-permute-start.1
  26.4 7.3 %all-to-all-start = ((bf16[2,45,96,192]{3,2,1,0:T(8,128)(2,1)}), bf16[2,45,96,192]{3,2,1,0:T(8,128)(2,1)}, u32[]{:S(2)}, u32[]{:S(2)}) async-start(bf16[2,45,96,192]{3,2,1,0:T(8,128)(2,1)} %bitcast.103), calls=%async_computation | async-start | bytes 8847360 | tf_op jit(solution)/shard_map/all_to_all | solution.py:985
  34.1 3.9 all-to-all-done.field
  38.8 4.5 all_to_all.85
  44.6 15.6 %spread_norm.1 = (f32[8,6,48,384]{3,2,1,0:T(8,128)}, f32[8,6,48,384]{3,2,1,0:T(8,128)}) custom-call(bf16[2,45,96,192]{3,2,1,0:T(8,128)(2,1)} %all-to-all-done.field, f32[2,45,2,96]{3,2,1,0:T(2,128)} %copy.244.sums, f32[1,192]{1,0:T(1,128)} %bitcast.128, f32[1,192]{1,0:T(1,128)} %bitcast.132, bf16[192,192]{1,0:T(8,128)(2,1)} %constant.151.clone.table, ...), custom_call_target="tpu_custom_call" | custom-call | flops 1000000 | bytes 100000 | tf_op jit(solution)/shard_map/spread_norm/pallas_call | solution.py:444
  60.2 4.1 all-to-all-start.3
  64.3 8.4 %from_flat.3 = bf16[90,96,192]{2,1,0:T(8,128)(2,1)} custom-call(bf16[1,1,1555200]{2,1,0:T(2,128)(2,1)} %flat.2), custom_call_target="tpu_custom_call" | custom-call | flops 1000000 | bytes 100000 | tf_op jit(solution)/shard_map/from_flat/pallas_call | solution.py:240
  72.8 3.1 dynamic-slice_bitcast_fusion
  75.9 1.9 block_matrices.1
  87.0 1.8 copy.218
  101.1 2.6 bitcast_select_fusion.1
  104.9 2.1 pad.17
  107.0 3.1 all-gather.5.cloned.1.call-done
  112.0 4.9 all-to-all-start.2
  119.5 3.0 collective-permute-start.4
  122.5 3.8 collective-permute-start.5
  127.7 18.1 %spectral.2 = (bf16[8,6,48,384]{3,2,1,0:T(8,128)(2,1)}, bf16[6,384,384]{2,1,0:T(8,128)(2,1)}, bf16[6,384,384]{2,1,0:T(8,128)(2,1)}) custom-call(f32[8,6,48,384]{3,2,1,0:T(8,128)} %copy-done.6, bf16[768,384]{1,0:T(8,128)(2,1)} %constant.156.clone.table, bf16[768,384]{1,0:T(8,128)(2,1)} %constant.157.clone.table_rest, bf16[384,384]{1,0:T(8,128)(2,1)} %get-tuple-element.170.w1, ...), custom_call_target="tpu_custom_call" | custom-call | flops 1000000 | bytes 100000 | tf_op jit(solution)/shard_map/spectral/pallas_call | solution.py:615
  145.9 10.0 %collective-permute-done.5.refs_6_ = bf16[576,384]{1,0:T(8,128)(2,1)S(1)} collective-permute-done((bf16[576,384]{1,0:T(8,128)(2,1)}, bf16[576,384]{1,0:T(8,128)(2,1)S(1)}, u32[]{:S(2)}, u32[]{:S(2)}) %collective-permute-start.5) | collective-permute-done | bytes 442400 | tf_op jit(solution)/shard_map/ppermute | solution.py:990
  156.9 5.8 all-to-all-start.4
  165.1 8.0 %collective-permute-start.7 = (bf16[512,384]{1,0:T(8,128)(2,1)S(1)}, bf16[512,384]{1,0:T(8,128)(2,1)S(1)}, u32[]{:S(2)}, u32[]{:S(2)}) collective-permute-start(bf16[512,384]{1,0:T(8,128)(2,1)S(1)} %get-tuple-element.429), channel_id=1, source_target_pairs={{0,1},{1,2},{2,3},{3,0},{4,5},{5,6},{6,7},{7,4},{8,9},{9,10},{10,1... | collective-permute-start | bytes 1179656 | tf_op jit(solution)/shard_map/ppermute | solution.py:990
  173.1 18.2 %spectral.3 = (bf16[8,6,48,384]{3,2,1,0:T(8,128)(2,1)}, bf16[6,384,384]{2,1,0:T(8,128)(2,1)}, bf16[6,384,384]{2,1,0:T(8,128)(2,1)}) custom-call(f32[8,6,48,384]{3,2,1,0:T(8,128)} %all-to-all-done.2.modes, bf16[768,384]{1,0:T(8,128)(2,1)} %constant.156.clone.table, bf16[768,384]{1,0:T(8,128)(2,1)} %constant.157.clone.table_rest, ...), custom_call_target="tpu_custom_call" | custom-call | flops 1000000 | bytes 100000 | tf_op jit(solution)/shard_map/spectral/pallas_call | solution.py:615
  192.8 4.5 all-to-all-start.5
  198.5 19.2 %collective-permute-done.9.refs_6_ = bf16[512,384]{1,0:T(8,128)(2,1)} collective-permute-done((bf16[512,384]{1,0:T(8,128)(2,1)}, bf16[512,384]{1,0:T(8,128)(2,1)}, u32[]{:S(2)}, u32[]{:S(2)}) %collective-permute-start.9) | collective-permute-done | bytes 393248 | tf_op jit(solution)/shard_map/ppermute | solution.py:990
  218.9 9.7 %collect_norm.2 = bf16[2304,384]{1,0:T(8,128)(2,1)} custom-call(bf16[8,6,48,384]{3,2,1,0:T(8,128)(2,1)} %copy-done.4, bf16[8,6,48,384]{3,2,1,0:T(8,128)(2,1)} %copy-done.5, bf16[2,45,96,192]{3,2,1,0:T(8,128)(2,1)} %all-to-all-done.field, f32[2,45,2,96]{3,2,1,0:T(2,128)} %copy.244.sums, f32[1,192]{1,0:T(1,128)} %bitcast.129, f32[1,192]{1,0:T(1,128)} %bitcast.133, ...), custom_call_target="tpu_custom_call" | custom-call | flops 1000000 | bytes 100000 | tf_op jit(solution)/shard_map/collect_norm/pallas_call | solution.py:490
  228.6 3.7 all-to-all-start.7
  232.3 2.8 collective-permute-start.10
  235.1 9.7 %collect_norm.3 = bf16[2048,384]{1,0:T(8,128)(2,1)} custom-call(bf16[8,6,48,384]{3,2,1,0:T(8,128)(2,1)} %copy-done.4, bf16[8,6,48,384]{3,2,1,0:T(8,128)(2,1)} %copy-done.5, bf16[2,45,96,192]{3,2,1,0:T(8,128)(2,1)} %all-to-all-done.field, f32[2,45,2,96]{3,2,1,0:T(2,128)} %copy.244.sums, f32[1,192]{1,0:T(1,128)} %bitcast.130, f32[1,192]{1,0:T(1,128)} %bitcast.134, ...), custom_call_target="tpu_custom_call" | custom-call | flops 1000000 | bytes 100000 | tf_op jit(solution)/shard_map/collect_norm/pallas_call | solution.py:490
  244.8 28.2 %all-to-all-done.7.refs_0_.refs_1_.refs_2_.refs_3_ = bf16[4,576,384]{2,1,0:T(8,128)(2,1)S(1)} async-done(((bf16[4,576,384]{2,1,0:T(8,128)(2,1)}), bf16[4,576,384]{2,1,0:T(8,128)(2,1)S(1)}, u32[]{:S(2)}, u32[]{:S(2)}) %all-to-all-start.7) | async-done | bytes 1769504 | tf_op jit(solution)/shard_map/all_to_all | solution.py:985
  273.0 4.0 all-to-all-start.6
  277.5 52.0 %channel_mlp.2 = (bf16[4,576,192]{2,1,0:T(8,128)(2,1)}, bf16[4,576,192]{2,1,0:T(8,128)(2,1)}, bf16[4,576,384]{2,1,0:T(8,128)(2,1)}, bf16[4,12,32,768]{3,2,1,0:T(...) custom-call(s32[2]{0:T(128)} %pad_add_fusion.place, ...), custom_call_target="tpu_custom_call" | custom-call | flops 1000000 | bytes 100000 | tf_op jit(solution)/shard_map/channel_mlp/pallas_call | solution.py:900
  329.6 4.5 all-to-all-start.8
  334.3 47.2 %channel_mlp.3 = (bf16[4,512,192]{2,1,0:T(8,128)(2,1)}, bf16[4,512,192]{2,1,0:T(8,128)(2,1)}, bf16[4,512,384]{2,1,0:T(8,128)(2,1)}, bf16[4,12,32,768]{3,2,1,0:T(...) custom-call(s32[2]{0:T(128)} %pad_add_fusion.place, ...), custom_call_target="tpu_custom_call" | custom-call | flops 1000000 | bytes 100000 | tf_op jit(solution)/shard_map/channel_mlp/pallas_call | solution.py:900
  381.5 2.2 collective-permute-start.18
  383.7 4.3 collective-permute-done.18
  388.0 2.5 fusion
  392.7 2.7 copy.227
  395.4 4.8 all-to-all-start.9
  412.0 1.9 pad_maximum_fusion.3
  415.9 20.8 %all-to-all-done.9 = bf16[4,512,384]{2,1,0:T(8,128)(2,1)S(1)} async-done(((bf16[4,512,384]{2,1,0:T(8,128)(2,1)}), bf16[4,512,384]{2,1,0:T(8,128)(2,1)S(1)}, u32[]{:S(2)}, u32[]{:S(2)}) %all-to-all-start.9) | async-done | bytes 1572896 | tf_op jit(solution)/shard_map/all_to_all | solution.py:985
  437.9 8.7 %spread_grad.1 = (bf16[8,6,48,384]{3,2,1,0:T(8,128)(2,1)}, bf16[8,6,48,384]{3,2,1,0:T(8,128)(2,1)}) custom-call(bf16[2304,384]{1,0:T(8,128)(2,1)} %bitcast.106, bf16[2048,384]{1,0:T(8,128)(2,1)} %bitcast.108, bf16[192,192]{1,0:T(8,128)(2,1)} %constant.154.clone.table), custom_call_target="tpu_custom_call" | custom-call | flops 1000000 | bytes 100000 | tf_op jit(solution)/shard_map/spread_grad/pallas_call | solution.py:444
  446.6 5.3 all-to-all-start.10
  453.0 3.3 collective-permute-start.14
  456.3 10.4 %collective-permute-done.13.refs_1_ = bf16[576,384]{1,0:T(8,128)(2,1)S(1)} collective-permute-done((bf16[576,384]{1,0:T(8,128)(2,1)S(1)}, bf16[576,384]{1,0:T(8,128)(2,1)S(1)}, u32[]{:S(2)}, u32[]{:S(2)}) %collective-permute-start.13) | collective-permute-done | bytes 442400 | tf_op jit(solution)/shard_map/ppermute | solution.py:990
  466.7 7.6 %collective-permute-done.14.refs_3_ = bf16[576,384]{1,0:T(8,128)(2,1)S(1)} collective-permute-done((bf16[576,384]{1,0:T(8,128)(2,1)S(1)}, bf16[576,384]{1,0:T(8,128)(2,1)S(1)}, u32[]{:S(2)}, u32[]{:S(2)}) %collective-permute-start.14) | collective-permute-done | bytes 442400 | tf_op jit(solution)/shard_map/ppermute | solution.py:990
  475.1 4.6 all-to-all-start.11
  482.9 2.3 collective-permute-start.17
  485.2 18.0 %spectral_back.2 = (bf16[8,6,48,384]{3,2,1,0:T(8,128)(2,1)}, f32[8,384]{1,0:T(8,128)}, f32[384,384]{1,0:T(8,128)}, f32[384,384]{1,0:T(8,128)}) custom-call(bf16[8,6,48,384]{3,2,1,0:T(8,128)(2,1)} %copy-done.10, bf16[6,384,384]{2,1,0:T(8,128)(2,1)} %get-tuple-element.229.low, bf16[6,384,384]{2,1,0:T(8,128)(2,1)} %get-tuple-element.230.act, ...), custom_call_target="tpu_custom_call" | custom-call | flops 1000000 | bytes 100000 | tf_op jit(solution)/shard_map/spectral_back/pallas_call | solution.py:686
  503.8 5.1 all-to-all-start.12
  509.6 18.8 %spectral_back.3 = (bf16[8,6,48,384]{3,2,1,0:T(8,128)(2,1)}, f32[768,96]{1,0:T(8,128)}, f32[8,384]{1,0:T(8,128)}) custom-call(bf16[8,6,48,384]{3,2,1,0:T(8,128)(2,1)} %copy-done.9, bf16[6,384,384]{2,1,0:T(8,128)(2,1)} %get-tuple-element.237.low, bf16[6,384,384]{2,1,0:T(8,128)(2,1)} %get-tuple-element.238.act, bf16[768,384]{1,0:T(8,128)(2,1)} %constant.156.clone.table, ...), custom_call_target="tpu_custom_call" | custom-call | flops 1000000 | bytes 100000 | tf_op jit(solution)/shard_map/spectral_back/pallas_call | solution.py:686
  528.5 7.9 %all-to-all-start.13 = ((bf16[8,6,48,384]{3,2,1,0:T(8,128)(2,1)}), bf16[8,6,48,384]{3,2,1,0:T(8,128)(2,1)}, u32[]{:S(2)}, u32[]{:S(2)}) async-start(bf16[8,6,48,384]{3,2,1,0:T(8,128)(2,1)} %get-tuple-element.245), calls=%async_computation.13 | async-start | bytes 3538944 | tf_op jit(solution)/shard_map/all_to_all | solution.py:985
  536.8 2.1 pad_maximum_fusion.1.grad
  542.6 15.6 %collective-permute-done.20.refs_2_ = bf16[576,384]{1,0:T(8,128)(2,1)} collective-permute-done((bf16[576,384]{1,0:T(8,128)(2,1)}, bf16[576,384]{1,0:T(8,128)(2,1)}, u32[]{:S(2)}, u32[]{:S(2)}) %collective-permute-start.20) | collective-permute-done | bytes 442400 | tf_op jit(solution)/shard_map/ppermute | solution.py:990
  559.1 2.4 collective-permute-start.23
  561.6 5.4 all-to-all-start.14
  566.9 27.9 %collect_back.1 = (f32[45,96,192]{2,1,0:T(8,128)}, f32[45,96,192]{2,1,0:T(8,128)}, f32[2,45,2,96]{3,2,1,0:T(2,128)}, f32[8,192]{1,0:T(8,128)}) custom-call(s32[1]{0:T(128)} %bitcast.place, bf16[8,6,48,384]{3,2,1,0:T(8,128)(2,1)} %all-to-all-done.12.modes_a, bf16[8,6,48,384]{3,2,1,0:T(8,128)(2,1)} %all-to-all-done.13.modes_b, ...), custom_call_target="tpu_custom_call" | custom-call | flops 1000000 | bytes 100000 | tf_op jit(solution)/shard_map/collect_back/pallas_call | solution.py:552
  595.1 1.8 broadcast_in_dim.24
  597.0 3.7 all-to-all-start.15
  600.6 10.8 %to_flat.1 = bf16[1,1,1555200]{2,1,0:T(2,128)(2,1)} custom-call(s32[1]{0:T(128)} %bitcast.1.blk, bf16[576,384]{1,0:T(8,128)(2,1)} %get-tuple-element.275.refs_0_, bf16[576,384]{1,0:T(8,128)(2,1)} %copy-done.20, bf16[576,384]{1,0:T(8,128)(2,1)} %collective-permute-done.20.refs_2_, bf16[576,384]{1,0:T(8,128)(2,1)} %copy-done.21, ...), custom_call_target="tpu_custom_call" | custom-call | flops 1000000 | bytes 100000 | tf_op jit(solution)/shard_map/to_flat/pallas_call | solution.py:309
  614.5 4.5 all-to-all-start.16
  619.0 4.2 weight_grads.1
  623.3 16.3 %final_flat.1 = f32[1,1,1555200]{2,1,0:T(1,128)} custom-call(s32[1]{0:T(128)} %bitcast.place, f32[45,96,192]{2,1,0:T(8,128)} %get-tuple-element.289.kept, f32[45,96,192]{2,1,0:T(8,128)} %collective-permute-done.24.other, bf16[90,96,192]{2,1,0:T(8,128)(2,1)} %get-tuple-element.155.field, f32[90,2,96]{2,1,0:T(2,128)} %copy-done.15, f32[90,2,96]{2,1,0:T(2,128)} %bitcast.122), custom_call_target="tpu_custom_call" | custom-call | flops 1000000 | bytes 100000 | tf_op jit(solution)/shard_map/final_flat/pallas_call | solution.py:371
  (246 shorter events, 78.9 us)
Async XLA Ops:
  7.2 103.0 %all-gather.5.cloned.1.call-start = ((), (), s32[]{:S(2)}) async-start(), calls=%async_computation.21 | async-start | bytes 5898240 | tf_op jit(solution)/shard_map/all_gather | solution.py:1082
  20.8 17.2 %copy-start.28 = (f32[97,2,96]{2,1,0:T(2,128)}, f32[97,2,96]{2,1,0:T(2,128)S(1)}, u32[]{:S(2)}) copy-start(f32[97,2,96]{2,1,0:T(2,128)S(1)} %constant_dynamic-update-slice_fusion) | copy-start | bytes 223492
  20.8 17.2 %collective-permute-start = (f32[97,2,96]{2,1,0:T(2,128)S(1)}, f32[97,2,96]{2,1,0:T(2,128)S(1)}, u32[]{:S(2)}, u32[]{:S(2)}) collective-permute-start(f32[97,2,96]{2,1,0:T(2,128)S(1)} %constant_dynamic-update-slice_fusion), channel_id=1, source_target_pairs={{0,1},{1,2},{2,3},{3,0},{4,5},{5,6},{6,7},{7,4},{8,9},{9,10},{10,1... | collective-permute-start | bytes 223496 | tf_op jit(solution)/shard_map/ppermute | solution.py:990
  23.0 15.0 %collective-permute-start.1 = (f32[97,2,96]{2,1,0:T(2,128)S(1)}, f32[97,2,96]{2,1,0:T(2,128)S(1)}, u32[]{:S(2)}, u32[]{:S(2)}) collective-permute-start(f32[97,2,96]{2,1,0:T(2,128)S(1)} %constant_dynamic-update-slice_fusion), channel_id=1, source_target_pairs={{0,2},{1,3},{2,0},{3,1},{4,6},{5,7},{6,4},{7,5},{8,10},{9,11},{10,... | collective-permute-start | bytes 223496 | tf_op jit(solution)/shard_map/ppermute | solution.py:990
  25.3 12.7 %collective-permute-start.2 = (f32[97,2,96]{2,1,0:T(2,128)S(1)}, f32[97,2,96]{2,1,0:T(2,128)S(1)}, u32[]{:S(2)}, u32[]{:S(2)}) collective-permute-start(f32[97,2,96]{2,1,0:T(2,128)S(1)} %constant_dynamic-update-slice_fusion), channel_id=1, source_target_pairs={{0,3},{1,0},{2,1},{3,2},{4,7},{5,4},{6,5},{7,6},{8,11},{9,8},{10,9... | collective-permute-start | bytes 223496 | tf_op jit(solution)/shard_map/ppermute | solution.py:990
  26.4 7.3 %copy-start.33 = (s32[90,90]{1,0:T(8,128)S(1)}, s32[90,90]{1,0:T(8,128)}, u32[]{:S(2)}) copy-start(s32[90,90]{1,0:T(8,128)} %param.35) | copy-start | bytes 97204
  26.4 11.6 %all-to-all-start = ((bf16[2,45,96,192]{3,2,1,0:T(8,128)(2,1)}), bf16[2,45,96,192]{3,2,1,0:T(8,128)(2,1)}, u32[]{:S(2)}, u32[]{:S(2)}) async-start(bf16[2,45,96,192]{3,2,1,0:T(8,128)(2,1)} %bitcast.103), calls=%async_computation | async-start | bytes 8847360 | tf_op jit(solution)/shard_map/all_to_all | solution.py:985
  38.0 22.2 %copy-start.30 = (f32[97,2,96]{2,1,0:T(2,128)}, f32[97,2,96]{2,1,0:T(2,128)S(1)}, u32[]{:S(2)}) copy-start(f32[97,2,96]{2,1,0:T(2,128)S(1)} %collective-permute-done) | copy-start | bytes 223492
  38.0 22.2 %copy-start.31 = (f32[97,2,96]{2,1,0:T(2,128)}, f32[97,2,96]{2,1,0:T(2,128)S(1)}, u32[]{:S(2)}) copy-start(f32[97,2,96]{2,1,0:T(2,128)S(1)} %collective-permute-done.1) | copy-start | bytes 223492
  38.0 22.2 %copy-start.32 = (f32[97,2,96]{2,1,0:T(2,128)}, f32[97,2,96]{2,1,0:T(2,128)S(1)}, u32[]{:S(2)}) copy-start(f32[97,2,96]{2,1,0:T(2,128)S(1)} %collective-permute-done.2) | copy-start | bytes 223492
  60.2 49.9 %all-to-all-start.3 = ((f32[8,6,48,384]{3,2,1,0:T(8,128)}), f32[8,6,48,384]{3,2,1,0:T(8,128)S(1)}, u32[]{:S(2)}, u32[]{:S(2)}) async-start(f32[8,6,48,384]{3,2,1,0:T(8,128)} %get-tuple-element.169), calls=%async_computation.3 | async-start | bytes 7077888 | tf_op jit(solution)/shard_map/all_to_all | solution.py:985
  72.8 21.8 %slice-start.3 = ((f32[97,2,96]{2,1,0:T(2,128)}), f32[7,2,96]{2,1,0:T(2,128)S(1)}, s32[]{:S(2)}) async-start(f32[97,2,96]{2,1,0:T(2,128)} %copy-done.31), calls=%async_computation.26 | async-start | bytes 14336 | tf_op jit(solution)/shard_map/slice | solution.py:1137
  72.8 22.5 %slice-start.2 = ((f32[97,2,96]{2,1,0:T(2,128)}), f32[7,2,96]{2,1,0:T(2,128)S(1)}, s32[]{:S(2)}) async-start(f32[97,2,96]{2,1,0:T(2,128)} %copy-done.30), calls=%async_computation.25 | async-start | bytes 14336 | tf_op jit(solution)/shard_map/slice | solution.py:1137
  75.9 25.1 %collective-permute-start.3 = (bf16[45,96,192]{2,1,0:T(8,128)(2,1)}, bf16[45,96,192]{2,1,0:T(8,128)(2,1)}, u32[]{:S(2)}, u32[]{:S(2)}) collective-permute-start(bf16[45,96,192]{2,1,0:T(8,128)(2,1)} %dynamic-slice_bitcast_fusion), channel_id=1, source_target_pairs={{0,4},{4,0},{1,5},{5,1},{2,6},{6,2},{3,7},{7,3},{8,12},{12,8},{9,1... | collective-permute-start | bytes 4976648 | tf_op jit(solution)/shard_map/ppermute | solution.py:994
  112.0 44.0 %all-to-all-start.2 = ((f32[8,6,48,384]{3,2,1,0:T(8,128)}), f32[8,6,48,384]{3,2,1,0:T(8,128)}, u32[]{:S(2)}, u32[]{:S(2)}) async-start(f32[8,6,48,384]{3,2,1,0:T(8,128)} %get-tuple-element.168), calls=%async_computation.2 | async-start | bytes 7077888 | tf_op jit(solution)/shard_map/all_to_all | solution.py:985
  116.9 9.5 %copy-start.38 = (f32[2,2,96]{2,1,0:T(2,128)S(1)}, f32[2,2,96]{2,1,0:T(2,128)}, u32[]{:S(2)}) copy-start(f32[2,2,96]{2,1,0:T(2,128)} %param.26) | copy-start | bytes 4612
  116.9 10.2 %copy-start.39 = (f32[2,2,96]{2,1,0:T(2,128)S(1)}, f32[2,2,96]{2,1,0:T(2,128)}, u32[]{:S(2)}) copy-start(f32[2,2,96]{2,1,0:T(2,128)} %param.28) | copy-start | bytes 4612
  119.5 26.4 %collective-permute-start.4 = (bf16[576,384]{1,0:T(8,128)(2,1)}, bf16[576,384]{1,0:T(8,128)(2,1)S(1)}, u32[]{:S(2)}, u32[]{:S(2)}) collective-permute-start(bf16[576,384]{1,0:T(8,128)(2,1)} %get-tuple-element.420), channel_id=1, source_target_pairs={{0,1},{1,2},{2,3},{3,0},{4,5},{5,6},{6,7},{7,4},{8,9},{9,10},{10,1... | collective-permute-start | bytes 1327112 | tf_op jit(solution)/shard_map/ppermute | solution.py:990
  122.5 33.5 %collective-permute-start.5 = (bf16[576,384]{1,0:T(8,128)(2,1)}, bf16[576,384]{1,0:T(8,128)(2,1)S(1)}, u32[]{:S(2)}, u32[]{:S(2)}) collective-permute-start(bf16[576,384]{1,0:T(8,128)(2,1)} %get-tuple-element.419), channel_id=1, source_target_pairs={{0,2},{1,3},{2,0},{3,1},{4,6},{5,7},{6,4},{7,5},{8,10},{9,11},{10,... | collective-permute-start | bytes 1327112 | tf_op jit(solution)/shard_map/ppermute | solution.py:990
  126.2 29.7 %collective-permute-start.6 = (bf16[576,384]{1,0:T(8,128)(2,1)S(1)}, bf16[576,384]{1,0:T(8,128)(2,1)S(1)}, u32[]{:S(2)}, u32[]{:S(2)}) collective-permute-start(bf16[576,384]{1,0:T(8,128)(2,1)S(1)} %get-tuple-element.418), channel_id=1, source_target_pairs={{0,3},{1,0},{2,1},{3,2},{4,7},{5,4},{6,5},{7,6},{8,11},{9,8},{10,9... | collective-permute-start | bytes 1327112 | tf_op jit(solution)/shard_map/ppermute | solution.py:990
  145.9 10.1 %copy-start.17 = (bf16[576,384]{1,0:T(8,128)(2,1)}, bf16[576,384]{1,0:T(8,128)(2,1)S(1)}, u32[]{:S(2)}) copy-start(bf16[576,384]{1,0:T(8,128)(2,1)S(1)} %collective-permute-done.4.refs_5_) | copy-start | bytes 1327108
  156.9 35.2 %all-to-all-start.4 = ((bf16[8,6,48,384]{3,2,1,0:T(8,128)(2,1)}), bf16[8,6,48,384]{3,2,1,0:T(8,128)(2,1)S(1)}, u32[]{:S(2)}, u32[]{:S(2)}) async-start(bf16[8,6,48,384]{3,2,1,0:T(8,128)(2,1)} %get-tuple-element.176), calls=%async_computation.4 | async-start | bytes 3538944 | tf_op jit(solution)/shard_map/all_to_all | solution.py:985
  165.1 26.2 %collective-permute-start.7 = (bf16[512,384]{1,0:T(8,128)(2,1)S(1)}, bf16[512,384]{1,0:T(8,128)(2,1)S(1)}, u32[]{:S(2)}, u32[]{:S(2)}) collective-permute-start(bf16[512,384]{1,0:T(8,128)(2,1)S(1)} %get-tuple-element.429), channel_id=1, source_target_pairs={{0,1},{1,2},{2,3},{3,0},{4,5},{5,6},{6,7},{7,4},{8,9},{9,10},{10,1... | collective-permute-start | bytes 1179656 | tf_op jit(solution)/shard_map/ppermute | solution.py:990
  173.1 18.9 %collective-permute-start.8 = (bf16[512,384]{1,0:T(8,128)(2,1)S(1)}, bf16[512,384]{1,0:T(8,128)(2,1)S(1)}, u32[]{:S(2)}, u32[]{:S(2)}) collective-permute-start(bf16[512,384]{1,0:T(8,128)(2,1)S(1)} %get-tuple-element.428), channel_id=1, source_target_pairs={{0,3},{1,0},{2,1},{3,2},{4,7},{5,4},{6,5},{7,6},{8,11},{9,8},{10,9... | collective-permute-start | bytes 1179656 | tf_op jit(solution)/shard_map/ppermute | solution.py:990
  192.1 25.6 %copy-start.4 = (bf16[8,6,48,384]{3,2,1,0:T(8,128)(2,1)}, bf16[8,6,48,384]{3,2,1,0:T(8,128)(2,1)S(1)}, u32[]{:S(2)}) copy-start(bf16[8,6,48,384]{3,2,1,0:T(8,128)(2,1)S(1)} %all-to-all-done.4.modes_a) | copy-start | bytes 5308420
  192.8 24.9 %all-to-all-start.5 = ((bf16[8,6,48,384]{3,2,1,0:T(8,128)(2,1)}), bf16[8,6,48,384]{3,2,1,0:T(8,128)(2,1)S(1)}, u32[]{:S(2)}, u32[]{:S(2)}) async-start(bf16[8,6,48,384]{3,2,1,0:T(8,128)(2,1)} %get-tuple-element.177), calls=%async_computation.5 | async-start | bytes 3538944 | tf_op jit(solution)/shard_map/all_to_all | solution.py:985
  197.3 20.4 %collective-permute-start.9 = (bf16[512,384]{1,0:T(8,128)(2,1)}, bf16[512,384]{1,0:T(8,128)(2,1)}, u32[]{:S(2)}, u32[]{:S(2)}) collective-permute-start(bf16[512,384]{1,0:T(8,128)(2,1)} %get-tuple-element.426), channel_id=1, source_target_pairs={{0,2},{1,3},{2,0},{3,1},{4,6},{5,7},{6,4},{7,5},{8,10},{9,11},{10,... | collective-permute-start | bytes 1179656 | tf_op jit(solution)/shard_map/ppermute | solution.py:990
  228.6 44.3 %all-to-all-start.7 = ((bf16[4,576,384]{2,1,0:T(8,128)(2,1)}), bf16[4,576,384]{2,1,0:T(8,128)(2,1)S(1)}, u32[]{:S(2)}, u32[]{:S(2)}) async-start(bf16[4,576,384]{2,1,0:T(8,128)(2,1)} %bitcast.113), calls=%async_computation.7 | async-start | bytes 3538944 | tf_op jit(solution)/shard_map/all_to_all | solution.py:985
  232.3 45.2 %collective-permute-start.10 = (bf16[4,768,768]{2,1,0:T(8,128)(2,1)}, bf16[4,768,768]{2,1,0:T(8,128)(2,1)}, u32[]{:S(2)}, u32[]{:S(2)}) collective-permute-start(bf16[4,768,768]{2,1,0:T(8,128)(2,1)} %bitcast.97), channel_id=1, source_target_pairs={{0,4},{4,0},{1,5},{5,1},{2,6},{6,2},{3,7},{7,3},{8,12},{12,8},{9,1... | collective-permute-start | bytes 14155784 | tf_op jit(solution)/shard_map/ppermute | solution.py:994
  273.0 56.6 %all-to-all-start.6 = ((bf16[4,512,384]{2,1,0:T(8,128)(2,1)}), bf16[4,512,384]{2,1,0:T(8,128)(2,1)S(1)}, u32[]{:S(2)}, u32[]{:S(2)}) async-start(bf16[4,512,384]{2,1,0:T(8,128)(2,1)} %bitcast.114), calls=%async_computation.6 | async-start | bytes 3145728 | tf_op jit(solution)/shard_map/all_to_all | solution.py:985
  329.6 51.9 %all-to-all-start.8 = ((bf16[4,576,384]{2,1,0:T(8,128)(2,1)}), bf16[4,576,384]{2,1,0:T(8,128)(2,1)S(1)}, u32[]{:S(2)}, u32[]{:S(2)}) async-start(bf16[4,576,384]{2,1,0:T(8,128)(2,1)} %get-tuple-element.218), calls=%async_computation.8 | async-start | bytes 3538944 | tf_op jit(solution)/shard_map/all_to_all | solution.py:985
  334.1 174.8 %reduce-scatter.3.cloned.1.call-start = ((), (), s32[]{:S(2)}) async-start(), calls=%async_computation.19 | async-start | bytes 5898240 | tf_op jit(solution)/shard_map/reduce_scatter | solution.py:1204
  381.5 9.1 %copy-start.2 = (bf16[4,576,384]{2,1,0:T(8,128)(2,1)}, bf16[4,576,384]{2,1,0:T(8,128)(2,1)S(1)}, u32[]{:S(2)}) copy-start(bf16[4,576,384]{2,1,0:T(8,128)(2,1)S(1)} %all-to-all-done.8) | copy-start | bytes 5308420
  381.5 9.9 %copy-start.13 = (bf16[4,12,32,768]{3,2,1,0:T(8,128)(2,1)S(1)}, bf16[4,12,32,768]{3,2,1,0:T(8,128)(2,1)}, u32[]{:S(2)}) copy-start(bf16[4,12,32,768]{3,2,1,0:T(8,128)(2,1)} %get-tuple-element.248) | copy-start | bytes 7077892
  381.5 6.5 %collective-permute-start.18 = (bf16[4,12,32,768]{3,2,1,0:T(8,128)(2,1)}, bf16[4,12,32,768]{3,2,1,0:T(8,128)(2,1)S(1)}, u32[]{:S(2)}, u32[]{:S(2)}) collective-permute-start(bf16[4,12,32,768]{3,2,1,0:T(8,128)(2,1)} %get-tuple-element.247), channel_id=1, source_target_pairs={{0,4},{4,0},{1,5},{5,1},{2,6},{6,2},{3,7},{7,3},{8,12},{12,8},{9,1... | collective-permute-start | bytes 7077896 | tf_op jit(solution)/shard_map/ppermute | solution.py:994
  383.6 7.7 %collective-permute-start.19 = (bf16[4,12,32,768]{3,2,1,0:T(8,128)(2,1)}, bf16[4,12,32,768]{3,2,1,0:T(8,128)(2,1)S(1)}, u32[]{:S(2)}, u32[]{:S(2)}) collective-permute-start(bf16[4,12,32,768]{3,2,1,0:T(8,128)(2,1)} %get-tuple-element.249), channel_id=1, source_target_pairs={{0,4},{4,0},{1,5},{5,1},{2,6},{6,2},{3,7},{7,3},{8,12},{12,8},{9,1... | collective-permute-start | bytes 7077896 | tf_op jit(solution)/shard_map/ppermute | solution.py:994
  395.4 7.0 %copy-start.14 = (bf16[4,576,192]{2,1,0:T(8,128)(2,1)S(1)}, bf16[4,576,192]{2,1,0:T(8,128)(2,1)}, u32[]{:S(2)}) copy-start(bf16[4,576,192]{2,1,0:T(8,128)(2,1)} %get-tuple-element.222) | copy-start | bytes 2654212
  395.4 41.3 %all-to-all-start.9 = ((bf16[4,512,384]{2,1,0:T(8,128)(2,1)}), bf16[4,512,384]{2,1,0:T(8,128)(2,1)S(1)}, u32[]{:S(2)}, u32[]{:S(2)}) async-start(bf16[4,512,384]{2,1,0:T(8,128)(2,1)} %get-tuple-element.220), calls=%async_computation.9 | async-start | bytes 3145728 | tf_op jit(solution)/shard_map/all_to_all | solution.py:985
  401.7 2.8 collective-permute-start.12
  403.7 5.2 collective-permute-start.11
  446.6 28.4 %all-to-all-start.10 = ((bf16[8,6,48,384]{3,2,1,0:T(8,128)(2,1)}), bf16[8,6,48,384]{3,2,1,0:T(8,128)(2,1)S(1)}, u32[]{:S(2)}, u32[]{:S(2)}) async-start(bf16[8,6,48,384]{3,2,1,0:T(8,128)(2,1)} %get-tuple-element.228), calls=%async_computation.10 | async-start | bytes 3538944 | tf_op jit(solution)/shard_map/all_to_all | solution.py:985
  453.0 13.6 %collective-permute-start.13 = (bf16[576,384]{1,0:T(8,128)(2,1)S(1)}, bf16[576,384]{1,0:T(8,128)(2,1)S(1)}, u32[]{:S(2)}, u32[]{:S(2)}) collective-permute-start(bf16[576,384]{1,0:T(8,128)(2,1)S(1)} %get-tuple-element.417), channel_id=1, source_target_pairs={{0,1},{1,2},{2,3},{3,0},{4,5},{5,6},{6,7},{7,4},{8,9},{9,10},{10,1... | collective-permute-start | bytes 1327112 | tf_op jit(solution)/shard_map/ppermute | solution.py:990
  453.0 21.3 %collective-permute-start.14 = (bf16[576,384]{1,0:T(8,128)(2,1)S(1)}, bf16[576,384]{1,0:T(8,128)(2,1)S(1)}, u32[]{:S(2)}, u32[]{:S(2)}) collective-permute-start(bf16[576,384]{1,0:T(8,128)(2,1)S(1)} %get-tuple-element.416), channel_id=1, source_target_pairs={{0,3},{1,0},{2,1},{3,2},{4,7},{5,4},{6,5},{7,6},{8,11},{9,8},{10,9... | collective-permute-start | bytes 1327112 | tf_op jit(solution)/shard_map/ppermute | solution.py:990
  466.7 7.6 %copy-start.20 = (bf16[576,384]{1,0:T(8,128)(2,1)}, bf16[576,384]{1,0:T(8,128)(2,1)S(1)}, u32[]{:S(2)}) copy-start(bf16[576,384]{1,0:T(8,128)(2,1)S(1)} %collective-permute-done.13.refs_1_) | copy-start | bytes 1327108
  475.1 10.1 %copy-start.10 = (bf16[8,6,48,384]{3,2,1,0:T(8,128)(2,1)}, bf16[8,6,48,384]{3,2,1,0:T(8,128)(2,1)S(1)}, u32[]{:S(2)}) copy-start(bf16[8,6,48,384]{3,2,1,0:T(8,128)(2,1)S(1)} %all-to-all-done.10.modes) | copy-start | bytes 5308420
  475.1 28.7 %all-to-all-start.11 = ((bf16[8,6,48,384]{3,2,1,0:T(8,128)(2,1)}), bf16[8,6,48,384]{3,2,1,0:T(8,128)(2,1)S(1)}, u32[]{:S(2)}, u32[]{:S(2)}) async-start(bf16[8,6,48,384]{3,2,1,0:T(8,128)(2,1)} %get-tuple-element.234), calls=%async_computation.11 | async-start | bytes 3538944 | tf_op jit(solution)/shard_map/all_to_all | solution.py:985
  480.6 22.6 %collective-permute-start.15 = (f32[1,1344]{1,0:T(1,128)S(1)}, f32[1,1344]{1,0:T(1,128)S(1)}, u32[]{:S(2)}, u32[]{:S(2)}) collective-permute-start(f32[1,1344]{1,0:T(1,128)S(1)} %get-tuple-element.441), channel_id=1, source_target_pairs={{0,1},{1,2},{2,3},{3,0},{4,5},{5,6},{6,7},{7,4},{8,9},{9,10},{10,1... | collective-permute-start | bytes 16136 | tf_op jit(solution)/shard_map/ppermute | solution.py:990
  481.2 22.0 %collective-permute-start.16 = (f32[1,1344]{1,0:T(1,128)S(1)}, f32[1,1344]{1,0:T(1,128)S(1)}, u32[]{:S(2)}, u32[]{:S(2)}) collective-permute-start(f32[1,1344]{1,0:T(1,128)S(1)} %get-tuple-element.440), channel_id=1, source_target_pairs={{0,2},{1,3},{2,0},{3,1},{4,6},{5,7},{6,4},{7,5},{8,10},{9,11},{10,... | collective-permute-start | bytes 16136 | tf_op jit(solution)/shard_map/ppermute | solution.py:990
  482.9 20.9 %collective-permute-start.17 = (f32[1,1344]{1,0:T(1,128)S(1)}, f32[1,1344]{1,0:T(1,128)}, u32[]{:S(2)}, u32[]{:S(2)}) collective-permute-start(f32[1,1344]{1,0:T(1,128)S(1)} %get-tuple-element.439), channel_id=1, source_target_pairs={{0,3},{1,0},{2,1},{3,2},{4,7},{5,4},{6,5},{7,6},{8,11},{9,8},{10,9... | collective-permute-start | bytes 16136 | tf_op jit(solution)/shard_map/ppermute | solution.py:990
  503.8 5.8 copy-start.9
  503.8 24.7 %all-to-all-start.12 = ((bf16[8,6,48,384]{3,2,1,0:T(8,128)(2,1)}), bf16[8,6,48,384]{3,2,1,0:T(8,128)(2,1)}, u32[]{:S(2)}, u32[]{:S(2)}) async-start(bf16[8,6,48,384]{3,2,1,0:T(8,128)(2,1)} %get-tuple-element.243), calls=%async_computation.12 | async-start | bytes 3538944 | tf_op jit(solution)/shard_map/all_to_all | solution.py:985
  508.9 49.3 %reduce-scatter.5.cloned.1.call-start = ((), (), s32[]{:S(2)}) async-start(), calls=%async_computation.20 | async-start | bytes 1474560 | tf_op jit(solution)/shard_map/reduce_scatter | solution.py:1205
  528.4 8.4 %copy-start.3 = (bf16[4,576,384]{2,1,0:T(8,128)(2,1)S(1)}, bf16[4,576,384]{2,1,0:T(8,128)(2,1)}, u32[]{:S(2)}) copy-start(bf16[4,576,384]{2,1,0:T(8,128)(2,1)} %copy-done.2) | copy-start | bytes 5308420
  528.4 8.4 %copy-start.8 = (bf16[4,512,384]{2,1,0:T(8,128)(2,1)S(1)}, bf16[4,512,384]{2,1,0:T(8,128)(2,1)}, u32[]{:S(2)}) copy-start(bf16[4,512,384]{2,1,0:T(8,128)(2,1)} %copy-done.7) | copy-start | bytes 4718596
  528.5 29.7 %all-to-all-start.13 = ((bf16[8,6,48,384]{3,2,1,0:T(8,128)(2,1)}), bf16[8,6,48,384]{3,2,1,0:T(8,128)(2,1)}, u32[]{:S(2)}, u32[]{:S(2)}) async-start(bf16[8,6,48,384]{3,2,1,0:T(8,128)(2,1)} %get-tuple-element.245), calls=%async_computation.13 | async-start | bytes 3538944 | tf_op jit(solution)/shard_map/all_to_all | solution.py:985
  536.4 76.3 %all-gather.7.cloned.1.call-start = ((), (), s32[]{:S(2)}) async-start(), calls=%async_computation.22 | async-start | bytes 2654208 | tf_op jit(solution)/shard_map/all_gather | solution.py:1257
  536.4 21.8 %collective-permute-start.20 = (bf16[576,384]{1,0:T(8,128)(2,1)}, bf16[576,384]{1,0:T(8,128)(2,1)}, u32[]{:S(2)}, u32[]{:S(2)}) collective-permute-start(bf16[576,384]{1,0:T(8,128)(2,1)} %get-tuple-element.414), channel_id=1, source_target_pairs={{0,2},{1,3},{2,0},{3,1},{4,6},{5,7},{6,4},{7,5},{8,10},{9,11},{10,... | collective-permute-start | bytes 1327112 | tf_op jit(solution)/shard_map/ppermute | solution.py:990
  558.2 36.7 %collective-permute-start.21 = (bf16[512,384]{1,0:T(8,128)(2,1)S(1)}, bf16[512,384]{1,0:T(8,128)(2,1)S(1)}, u32[]{:S(2)}, u32[]{:S(2)}) collective-permute-start(bf16[512,384]{1,0:T(8,128)(2,1)S(1)} %get-tuple-element.266), channel_id=1, source_target_pairs={{0,1},{1,2},{2,3},{3,0},{4,5},{5,6},{6,7},{7,4},{8,9},{9,10},{10,1... | collective-permute-start | bytes 1179656 | tf_op jit(solution)/shard_map/ppermute | solution.py:990
  558.3 36.6 %collective-permute-start.22 = (bf16[512,384]{1,0:T(8,128)(2,1)S(1)}, bf16[512,384]{1,0:T(8,128)(2,1)S(1)}, u32[]{:S(2)}, u32[]{:S(2)}) collective-permute-start(bf16[512,384]{1,0:T(8,128)(2,1)S(1)} %get-tuple-element.267), channel_id=1, source_target_pairs={{0,2},{1,3},{2,0},{3,1},{4,6},{5,7},{6,4},{7,5},{8,10},{9,11},{10,... | collective-permute-start | bytes 1179656 | tf_op jit(solution)/shard_map/ppermute | solution.py:990
  559.1 35.8 %collective-permute-start.23 = (bf16[512,384]{1,0:T(8,128)(2,1)S(1)}, bf16[512,384]{1,0:T(8,128)(2,1)S(1)}, u32[]{:S(2)}, u32[]{:S(2)}) collective-permute-start(bf16[512,384]{1,0:T(8,128)(2,1)S(1)} %get-tuple-element.268), channel_id=1, source_target_pairs={{0,3},{1,0},{2,1},{3,2},{4,7},{5,4},{6,5},{7,6},{8,11},{9,8},{10,9... | collective-permute-start | bytes 1179656 | tf_op jit(solution)/shard_map/ppermute | solution.py:990
  561.6 33.3 %all-to-all-start.14 = ((f32[8,99,96]{1,2,0:T(8,128)}), f32[8,99,96]{1,2,0:T(8,128)S(1)}, u32[]{:S(2)}, u32[]{:S(2)}) async-start(f32[8,99,96]{1,2,0:T(8,128)} %pad_maximum_fusion.5), calls=%async_computation.16 | async-start | bytes 786432 | tf_op jit(solution)/shard_map/all_to_all | solution.py:985
  595.0 17.8 %collective-permute-start.24 = (f32[45,96,192]{2,1,0:T(8,128)}, f32[45,96,192]{2,1,0:T(8,128)}, u32[]{:S(2)}, u32[]{:S(2)}) collective-permute-start(f32[45,96,192]{2,1,0:T(8,128)} %get-tuple-element.270), channel_id=1, source_target_pairs={{0,4},{4,0},{1,5},{5,1},{2,6},{6,2},{3,7},{7,3},{8,12},{12,8},{9,1... | collective-permute-start | bytes 9953288 | tf_op jit(solution)/shard_map/ppermute | solution.py:994
  597.0 15.0 %all-to-all-start.15 = ((f32[8,45,2,96]{3,2,1,0:T(2,128)}), f32[8,45,2,96]{3,2,1,0:T(2,128)S(1)}, u32[]{:S(2)}, u32[]{:S(2)}) async-start(f32[8,45,2,96]{3,2,1,0:T(2,128)} %bitcast.47), calls=%async_computation.17 | async-start | bytes 737280 | tf_op jit(solution)/shard_map/all_to_all | solution.py:985
  614.5 25.1 %all-to-all-start.16 = ((f32[8,103,96]{1,2,0:T(8,128)}), f32[8,103,96]{1,2,0:T(8,128)S(1)}, u32[]{:S(2)}, u32[]{:S(2)}) async-start(f32[8,103,96]{1,2,0:T(8,128)} %broadcast_in_dim.25), calls=%async_computation.18 | async-start | bytes 786432 | tf_op jit(solution)/shard_map/all_to_all | solution.py:985
  (29 other events, 66.5 us)
Sparse Core Ops, SparseCore 0:
  10.2 99.9 all-gather.4
  395.5 58.3 reduce-scatter.2
  512.0 27.0 reduce-scatter.4
  558.4 31.8 all-gather.6

commit v4 on v3

--- a/solution.py
+++ b/solution.py
@@ -337,7 +337,7 @@
     return (base + cols[:, 0:1]) - field.astype(wide) * cols[:, 1:2]
 
 
-FINAL_ROWS = 15
+FINAL_ROWS = 9
 
 
 def final_kernel(place, kept, other, field, sums, grad_sums, flat, *scratch):
@@ -386,6 +386,7 @@
 
 
 STEP = 9
+BACK_STEP = 5
 TOKEN_STEP = 8
 TOKEN_HALVES = ((0, 24), (24, 21))
 
@@ -519,8 +520,8 @@
 
     gain_sum = jnp.zeros((1, gain.shape[1]), wide)
     shift_sum = jnp.zeros((1, gain.shape[1]), wide)
-    for q in range(STEP):
-        spatial = spatial_rows(scratch, step * STEP + q, table, modes_a.shape[3])
+    for q in range(BACK_STEP):
+        spatial = spatial_rows(scratch, step * BACK_STEP + q, table, modes_a.shape[3])
         cols = norm_columns(sums[:, q])
         pair = grad[q * SLOTS : (q + 1) * SLOTS, :].astype(wide)
         chans = pair.shape[1] // 2
@@ -547,17 +548,17 @@
 def collect_back(modes, grad, field, sums, gain, table):
     chans = field.shape[3]
     mode_total = table.shape[1] // 2
-    half_rows = pl.BlockSpec((STEP, SLOTS, chans), lambda i, at: (i, 0, 0))
-    pair_sums = pl.BlockSpec((2, STEP, 2, SLOTS), lambda i, at: (0, i, 0, 0))
+    half_rows = pl.BlockSpec((BACK_STEP, SLOTS, chans), lambda i, at: (i, 0, 0))
+    pair_sums = pl.BlockSpec((2, BACK_STEP, 2, SLOTS), lambda i, at: (0, i, 0, 0))
     return pl.pallas_call(
         collect_back_kernel,
         grid_spec=pltpu.PrefetchScalarGridSpec(
             num_scalar_prefetch=1,
-            grid=(45 // STEP,),
+            grid=(45 // BACK_STEP,),
             in_specs=[
                 *[full(part.shape) for part in modes],
-                pl.BlockSpec((STEP * SLOTS, 2 * chans), lambda i, at: (i, 0)),
-                pl.BlockSpec((2, STEP, SLOTS, chans), lambda i, at: (0, i, 0, 0)),
+                pl.BlockSpec((BACK_STEP * SLOTS, 2 * chans), lambda i, at: (i, 0)),
+                pl.BlockSpec((2, BACK_STEP, SLOTS, chans), lambda i, at: (0, i, 0, 0)),
                 pair_sums,
                 full(gain.shape),
                 full(table.shape),

time: 663 us -> 662 us (level)
  no operation moved by 1% of the time
where the time goes in v4:
time: 662 us; the launch traced here: 651 us
  Pallas kernels  295 us (45%)
  waiting for transfers between devices  126 us (19%)
  starting transfers between devices  119 us (18%)
  local copies, waits for them, and re-layouts  66.2 us (10%)
  other arithmetic  25.5 us (4%)
  between operations  14.9 us (2%)
    pallas_call x2, Pallas kernels, mlp(): pl.pallas_call(functools.partial(mlp_kernel, tile, blks), grid_spec=pltpu...  99.2 us
    all_to_all x16, starting transfers between devices, swap_first(): return lax.all_to_all(values, axes, split_axis=0, concat_axis=0, tiled=True)  79.7 us
    ppermute x18, waiting for transfers between devices, shifted(): lax.ppermute(values, axis, [(i, (i + by) % size) for i in range(size)])  62.9 us
    all_to_all x16, waiting for transfers between devices, swap_first(): return lax.all_to_all(values, axes, split_axis=0, concat_axis=0, tiled=True)  53.5 us
    pallas_call x2, Pallas kernels, spectral_back(): pl.pallas_call(spectral_back_kernel, grid=(share,), in_specs=[mode_block,...  36.8 us
    pallas_call x2, Pallas kernels, spectral(): pl.pallas_call(spectral_kernel, grid=(share,), in_specs=[mode_block] + [f...  36.3 us
    ppermute x18, starting transfers between devices, shifted(): lax.ppermute(values, axis, [(i, (i + by) % size) for i in range(size)])  33.2 us
    pallas_call x1, Pallas kernels, collect_back(): pl.pallas_call(collect_back_kernel, grid_spec=pltpu.PrefetchScalarGridSpe...  27.2 us
  transfers between devices with their start and end apart: 45, of which 14 were waited for; matrix products, arithmetic and copies ran while one was open for 10% of the time, Pallas kernels for 44%

profile of v4, /device:TPU:1, one launch (start us, length us, event | category | flops | bytes accessed | tf_op | source)
XLA Modules:
  0.0 651.5 jit_solution(11930748136919327313)
XLA Ops:
  7.3 2.4 broadcast_select_fusion.2
  9.9 10.0 %from_flat.2 = (bf16[90,96,192]{2,1,0:T(8,128)(2,1)}, f32[90,2,96]{2,1,0:T(2,128)}) custom-call(bf16[1,1,1555200]{2,1,0:T(2,128)(2,1)} %flat.1), custom_call_target="tpu_custom_call" | custom-call | flops 1000000 | bytes 100000 | tf_op jit(solution)/shard_map/from_flat/pallas_call | solution.py:240
  20.8 2.2 collective-permute-start
  23.0 2.3 collective-permute-start.1
  26.4 7.3 %all-to-all-start = ((bf16[2,45,96,192]{3,2,1,0:T(8,128)(2,1)}), bf16[2,45,96,192]{3,2,1,0:T(8,128)(2,1)}, u32[]{:S(2)}, u32[]{:S(2)}) async-start(bf16[2,45,96,192]{3,2,1,0:T(8,128)(2,1)} %bitcast.103), calls=%async_computation | async-start | bytes 8847360 | tf_op jit(solution)/shard_map/all_to_all | solution.py:986
  34.1 3.9 all-to-all-done.field
  38.8 4.5 all_to_all.85
  44.6 15.6 %spread_norm.1 = (f32[8,6,48,384]{3,2,1,0:T(8,128)}, f32[8,6,48,384]{3,2,1,0:T(8,128)}) custom-call(bf16[2,45,96,192]{3,2,1,0:T(8,128)(2,1)} %all-to-all-done.field, f32[2,45,2,96]{3,2,1,0:T(2,128)} %copy.244.sums, f32[1,192]{1,0:T(1,128)} %bitcast.128, f32[1,192]{1,0:T(1,128)} %bitcast.132, bf16[192,192]{1,0:T(8,128)(2,1)} %constant.151.clone.table, ...), custom_call_target="tpu_custom_call" | custom-call | flops 1000000 | bytes 100000 | tf_op jit(solution)/shard_map/spread_norm/pallas_call | solution.py:445
  60.2 4.1 all-to-all-start.3
  64.3 8.4 %from_flat.3 = bf16[90,96,192]{2,1,0:T(8,128)(2,1)} custom-call(bf16[1,1,1555200]{2,1,0:T(2,128)(2,1)} %flat.2), custom_call_target="tpu_custom_call" | custom-call | flops 1000000 | bytes 100000 | tf_op jit(solution)/shard_map/from_flat/pallas_call | solution.py:240
  72.8 3.1 dynamic-slice_bitcast_fusion
  75.9 1.9 block_matrices.1
  87.0 1.8 copy.218
  101.1 2.6 bitcast_select_fusion.1
  104.9 2.1 pad.17
  107.0 3.1 all-gather.5.cloned.1.call-done
  112.0 4.9 all-to-all-start.2
  119.5 3.0 collective-permute-start.4
  122.5 3.8 collective-permute-start.5
  127.7 18.1 %spectral.2 = (bf16[8,6,48,384]{3,2,1,0:T(8,128)(2,1)}, bf16[6,384,384]{2,1,0:T(8,128)(2,1)}, bf16[6,384,384]{2,1,0:T(8,128)(2,1)}) custom-call(f32[8,6,48,384]{3,2,1,0:T(8,128)} %copy-done.6, bf16[768,384]{1,0:T(8,128)(2,1)} %constant.156.clone.table, bf16[768,384]{1,0:T(8,128)(2,1)} %constant.157.clone.table_rest, bf16[384,384]{1,0:T(8,128)(2,1)} %get-tuple-element.170.w1, ...), custom_call_target="tpu_custom_call" | custom-call | flops 1000000 | bytes 100000 | tf_op jit(solution)/shard_map/spectral/pallas_call | solution.py:616
  145.9 10.0 %collective-permute-done.5.refs_6_ = bf16[576,384]{1,0:T(8,128)(2,1)S(1)} collective-permute-done((bf16[576,384]{1,0:T(8,128)(2,1)}, bf16[576,384]{1,0:T(8,128)(2,1)S(1)}, u32[]{:S(2)}, u32[]{:S(2)}) %collective-permute-start.5) | collective-permute-done | bytes 442400 | tf_op jit(solution)/shard_map/ppermute | solution.py:991
  156.9 5.8 all-to-all-start.4
  165.1 8.0 %collective-permute-start.7 = (bf16[512,384]{1,0:T(8,128)(2,1)S(1)}, bf16[512,384]{1,0:T(8,128)(2,1)S(1)}, u32[]{:S(2)}, u32[]{:S(2)}) collective-permute-start(bf16[512,384]{1,0:T(8,128)(2,1)S(1)} %get-tuple-element.429), channel_id=1, source_target_pairs={{0,1},{1,2},{2,3},{3,0},{4,5},{5,6},{6,7},{7,4},{8,9},{9,10},{10,1... | collective-permute-start | bytes 1179656 | tf_op jit(solution)/shard_map/ppermute | solution.py:991
  173.1 18.2 %spectral.3 = (bf16[8,6,48,384]{3,2,1,0:T(8,128)(2,1)}, bf16[6,384,384]{2,1,0:T(8,128)(2,1)}, bf16[6,384,384]{2,1,0:T(8,128)(2,1)}) custom-call(f32[8,6,48,384]{3,2,1,0:T(8,128)} %all-to-all-done.2.modes, bf16[768,384]{1,0:T(8,128)(2,1)} %constant.156.clone.table, bf16[768,384]{1,0:T(8,128)(2,1)} %constant.157.clone.table_rest, ...), custom_call_target="tpu_custom_call" | custom-call | flops 1000000 | bytes 100000 | tf_op jit(solution)/shard_map/spectral/pallas_call | solution.py:616
  192.8 4.5 all-to-all-start.5
  198.5 19.2 %collective-permute-done.9.refs_6_ = bf16[512,384]{1,0:T(8,128)(2,1)} collective-permute-done((bf16[512,384]{1,0:T(8,128)(2,1)}, bf16[512,384]{1,0:T(8,128)(2,1)}, u32[]{:S(2)}, u32[]{:S(2)}) %collective-permute-start.9) | collective-permute-done | bytes 393248 | tf_op jit(solution)/shard_map/ppermute | solution.py:991
  218.9 9.7 %collect_norm.2 = bf16[2304,384]{1,0:T(8,128)(2,1)} custom-call(bf16[8,6,48,384]{3,2,1,0:T(8,128)(2,1)} %copy-done.4, bf16[8,6,48,384]{3,2,1,0:T(8,128)(2,1)} %copy-done.5, bf16[2,45,96,192]{3,2,1,0:T(8,128)(2,1)} %all-to-all-done.field, f32[2,45,2,96]{3,2,1,0:T(2,128)} %copy.244.sums, f32[1,192]{1,0:T(1,128)} %bitcast.129, f32[1,192]{1,0:T(1,128)} %bitcast.133, ...), custom_call_target="tpu_custom_call" | custom-call | flops 1000000 | bytes 100000 | tf_op jit(solution)/shard_map/collect_norm/pallas_call | solution.py:491
  228.6 3.7 all-to-all-start.7
  232.3 2.8 collective-permute-start.10
  235.1 9.7 %collect_norm.3 = bf16[2048,384]{1,0:T(8,128)(2,1)} custom-call(bf16[8,6,48,384]{3,2,1,0:T(8,128)(2,1)} %copy-done.4, bf16[8,6,48,384]{3,2,1,0:T(8,128)(2,1)} %copy-done.5, bf16[2,45,96,192]{3,2,1,0:T(8,128)(2,1)} %all-to-all-done.field, f32[2,45,2,96]{3,2,1,0:T(2,128)} %copy.244.sums, f32[1,192]{1,0:T(1,128)} %bitcast.130, f32[1,192]{1,0:T(1,128)} %bitcast.134, ...), custom_call_target="tpu_custom_call" | custom-call | flops 1000000 | bytes 100000 | tf_op jit(solution)/shard_map/collect_norm/pallas_call | solution.py:491
  244.8 28.2 %all-to-all-done.7.refs_0_.refs_1_.refs_2_.refs_3_ = bf16[4,576,384]{2,1,0:T(8,128)(2,1)S(1)} async-done(((bf16[4,576,384]{2,1,0:T(8,128)(2,1)}), bf16[4,576,384]{2,1,0:T(8,128)(2,1)S(1)}, u32[]{:S(2)}, u32[]{:S(2)}) %all-to-all-start.7) | async-done | bytes 1769504 | tf_op jit(solution)/shard_map/all_to_all | solution.py:986
  273.0 4.0 all-to-all-start.6
  277.5 52.0 %channel_mlp.2 = (bf16[4,576,192]{2,1,0:T(8,128)(2,1)}, bf16[4,576,192]{2,1,0:T(8,128)(2,1)}, bf16[4,576,384]{2,1,0:T(8,128)(2,1)}, bf16[4,12,32,768]{3,2,1,0:T(...) custom-call(s32[2]{0:T(128)} %pad_add_fusion.place, ...), custom_call_target="tpu_custom_call" | custom-call | flops 1000000 | bytes 100000 | tf_op jit(solution)/shard_map/channel_mlp/pallas_call | solution.py:901
  329.6 4.5 all-to-all-start.8
  334.3 47.2 %channel_mlp.3 = (bf16[4,512,192]{2,1,0:T(8,128)(2,1)}, bf16[4,512,192]{2,1,0:T(8,128)(2,1)}, bf16[4,512,384]{2,1,0:T(8,128)(2,1)}, bf16[4,12,32,768]{3,2,1,0:T(...) custom-call(s32[2]{0:T(128)} %pad_add_fusion.place, ...), custom_call_target="tpu_custom_call" | custom-call | flops 1000000 | bytes 100000 | tf_op jit(solution)/shard_map/channel_mlp/pallas_call | solution.py:901
  381.5 2.2 collective-permute-start.18
  383.7 4.3 collective-permute-done.18
  388.0 2.5 fusion
  392.7 2.7 copy.227
  395.4 4.8 all-to-all-start.9
  412.0 1.9 pad_maximum_fusion.3
  415.9 20.8 %all-to-all-done.9 = bf16[4,512,384]{2,1,0:T(8,128)(2,1)S(1)} async-done(((bf16[4,512,384]{2,1,0:T(8,128)(2,1)}), bf16[4,512,384]{2,1,0:T(8,128)(2,1)S(1)}, u32[]{:S(2)}, u32[]{:S(2)}) %all-to-all-start.9) | async-done | bytes 1572896 | tf_op jit(solution)/shard_map/all_to_all | solution.py:986
  437.9 8.7 %spread_grad.1 = (bf16[8,6,48,384]{3,2,1,0:T(8,128)(2,1)}, bf16[8,6,48,384]{3,2,1,0:T(8,128)(2,1)}) custom-call(bf16[2304,384]{1,0:T(8,128)(2,1)} %bitcast.106, bf16[2048,384]{1,0:T(8,128)(2,1)} %bitcast.108, bf16[192,192]{1,0:T(8,128)(2,1)} %constant.154.clone.table), custom_call_target="tpu_custom_call" | custom-call | flops 1000000 | bytes 100000 | tf_op jit(solution)/shard_map/spread_grad/pallas_call | solution.py:445
  446.6 5.3 all-to-all-start.10
  453.0 3.3 collective-permute-start.14
  456.3 10.4 %collective-permute-done.13.refs_1_ = bf16[576,384]{1,0:T(8,128)(2,1)S(1)} collective-permute-done((bf16[576,384]{1,0:T(8,128)(2,1)S(1)}, bf16[576,384]{1,0:T(8,128)(2,1)S(1)}, u32[]{:S(2)}, u32[]{:S(2)}) %collective-permute-start.13) | collective-permute-done | bytes 442400 | tf_op jit(solution)/shard_map/ppermute | solution.py:991
  466.7 7.6 %collective-permute-done.14.refs_3_ = bf16[576,384]{1,0:T(8,128)(2,1)S(1)} collective-permute-done((bf16[576,384]{1,0:T(8,128)(2,1)S(1)}, bf16[576,384]{1,0:T(8,128)(2,1)S(1)}, u32[]{:S(2)}, u32[]{:S(2)}) %collective-permute-start.14) | collective-permute-done | bytes 442400 | tf_op jit(solution)/shard_map/ppermute | solution.py:991
  475.1 4.6 all-to-all-start.11
  482.9 2.3 collective-permute-start.17
  485.2 18.0 %spectral_back.2 = (bf16[8,6,48,384]{3,2,1,0:T(8,128)(2,1)}, f32[8,384]{1,0:T(8,128)}, f32[384,384]{1,0:T(8,128)}, f32[384,384]{1,0:T(8,128)}) custom-call(bf16[8,6,48,384]{3,2,1,0:T(8,128)(2,1)} %copy-done.10, bf16[6,384,384]{2,1,0:T(8,128)(2,1)} %get-tuple-element.229.low, bf16[6,384,384]{2,1,0:T(8,128)(2,1)} %get-tuple-element.230.act, ...), custom_call_target="tpu_custom_call" | custom-call | flops 1000000 | bytes 100000 | tf_op jit(solution)/shard_map/spectral_back/pallas_call | solution.py:687
  503.8 5.1 all-to-all-start.12
  509.6 18.8 %spectral_back.3 = (bf16[8,6,48,384]{3,2,1,0:T(8,128)(2,1)}, f32[768,96]{1,0:T(8,128)}, f32[8,384]{1,0:T(8,128)}) custom-call(bf16[8,6,48,384]{3,2,1,0:T(8,128)(2,1)} %copy-done.9, bf16[6,384,384]{2,1,0:T(8,128)(2,1)} %get-tuple-element.237.low, bf16[6,384,384]{2,1,0:T(8,128)(2,1)} %get-tuple-element.238.act, bf16[768,384]{1,0:T(8,128)(2,1)} %constant.156.clone.table, ...), custom_call_target="tpu_custom_call" | custom-call | flops 1000000 | bytes 100000 | tf_op jit(solution)/shard_map/spectral_back/pallas_call | solution.py:687
  528.5 7.9 %all-to-all-start.13 = ((bf16[8,6,48,384]{3,2,1,0:T(8,128)(2,1)}), bf16[8,6,48,384]{3,2,1,0:T(8,128)(2,1)}, u32[]{:S(2)}, u32[]{:S(2)}) async-start(bf16[8,6,48,384]{3,2,1,0:T(8,128)(2,1)} %get-tuple-element.245), calls=%async_computation.13 | async-start | bytes 3538944 | tf_op jit(solution)/shard_map/all_to_all | solution.py:986
  536.8 2.1 pad_maximum_fusion.1.grad
  542.6 15.6 %collective-permute-done.20.refs_2_ = bf16[576,384]{1,0:T(8,128)(2,1)} collective-permute-done((bf16[576,384]{1,0:T(8,128)(2,1)}, bf16[576,384]{1,0:T(8,128)(2,1)}, u32[]{:S(2)}, u32[]{:S(2)}) %collective-permute-start.20) | collective-permute-done | bytes 442400 | tf_op jit(solution)/shard_map/ppermute | solution.py:991
  559.1 2.4 collective-permute-start.23
  561.6 5.4 all-to-all-start.14
  566.9 27.2 %collect_back.1 = (f32[45,96,192]{2,1,0:T(8,128)}, f32[45,96,192]{2,1,0:T(8,128)}, f32[2,45,2,96]{3,2,1,0:T(2,128)}, f32[8,192]{1,0:T(8,128)}) custom-call(s32[1]{0:T(128)} %bitcast.place, bf16[8,6,48,384]{3,2,1,0:T(8,128)(2,1)} %all-to-all-done.12.modes_a, bf16[8,6,48,384]{3,2,1,0:T(8,128)(2,1)} %all-to-all-done.13.modes_b, ...), custom_call_target="tpu_custom_call" | custom-call | flops 1000000 | bytes 100000 | tf_op jit(solution)/shard_map/collect_back/pallas_call | solution.py:553
  594.4 1.8 broadcast_in_dim.24
  596.2 3.7 all-to-all-start.15
  599.9 10.8 %to_flat.1 = bf16[1,1,1555200]{2,1,0:T(2,128)(2,1)} custom-call(s32[1]{0:T(128)} %bitcast.1.blk, bf16[576,384]{1,0:T(8,128)(2,1)} %get-tuple-element.275.refs_0_, bf16[576,384]{1,0:T(8,128)(2,1)} %copy-done.20, bf16[576,384]{1,0:T(8,128)(2,1)} %collective-permute-done.20.refs_2_, bf16[576,384]{1,0:T(8,128)(2,1)} %copy-done.21, ...), custom_call_target="tpu_custom_call" | custom-call | flops 1000000 | bytes 100000 | tf_op jit(solution)/shard_map/to_flat/pallas_call | solution.py:309
  613.8 4.2 all-to-all-start.16
  618.0 4.2 weight_grads.1
  622.2 16.6 %final_flat.1 = f32[1,1,1555200]{2,1,0:T(1,128)} custom-call(s32[1]{0:T(128)} %bitcast.place, f32[45,96,192]{2,1,0:T(8,128)} %get-tuple-element.289.kept, f32[45,96,192]{2,1,0:T(8,128)} %collective-permute-done.24.other, bf16[90,96,192]{2,1,0:T(8,128)(2,1)} %get-tuple-element.155.field, f32[90,2,96]{2,1,0:T(2,128)} %copy-done.15, f32[90,2,96]{2,1,0:T(2,128)} %bitcast.122), custom_call_target="tpu_custom_call" | custom-call | flops 1000000 | bytes 100000 | tf_op jit(solution)/shard_map/final_flat/pallas_call | solution.py:371
  (246 shorter events, 78.9 us)
Async XLA Ops:
  7.2 103.0 %all-gather.5.cloned.1.call-start = ((), (), s32[]{:S(2)}) async-start(), calls=%async_computation.21 | async-start | bytes 5898240 | tf_op jit(solution)/shard_map/all_gather | solution.py:1083
  20.8 17.2 %copy-start.28 = (f32[97,2,96]{2,1,0:T(2,128)}, f32[97,2,96]{2,1,0:T(2,128)S(1)}, u32[]{:S(2)}) copy-start(f32[97,2,96]{2,1,0:T(2,128)S(1)} %constant_dynamic-update-slice_fusion) | copy-start | bytes 223492
  20.8 17.2 %collective-permute-start = (f32[97,2,96]{2,1,0:T(2,128)S(1)}, f32[97,2,96]{2,1,0:T(2,128)S(1)}, u32[]{:S(2)}, u32[]{:S(2)}) collective-permute-start(f32[97,2,96]{2,1,0:T(2,128)S(1)} %constant_dynamic-update-slice_fusion), channel_id=1, source_target_pairs={{0,1},{1,2},{2,3},{3,0},{4,5},{5,6},{6,7},{7,4},{8,9},{9,10},{10,1... | collective-permute-start | bytes 223496 | tf_op jit(solution)/shard_map/ppermute | solution.py:991
  23.0 15.0 %collective-permute-start.1 = (f32[97,2,96]{2,1,0:T(2,128)S(1)}, f32[97,2,96]{2,1,0:T(2,128)S(1)}, u32[]{:S(2)}, u32[]{:S(2)}) collective-permute-start(f32[97,2,96]{2,1,0:T(2,128)S(1)} %constant_dynamic-update-slice_fusion), channel_id=1, source_target_pairs={{0,2},{1,3},{2,0},{3,1},{4,6},{5,7},{6,4},{7,5},{8,10},{9,11},{10,... | collective-permute-start | bytes 223496 | tf_op jit(solution)/shard_map/ppermute | solution.py:991
  25.3 12.7 %collective-permute-start.2 = (f32[97,2,96]{2,1,0:T(2,128)S(1)}, f32[97,2,96]{2,1,0:T(2,128)S(1)}, u32[]{:S(2)}, u32[]{:S(2)}) collective-permute-start(f32[97,2,96]{2,1,0:T(2,128)S(1)} %constant_dynamic-update-slice_fusion), channel_id=1, source_target_pairs={{0,3},{1,0},{2,1},{3,2},{4,7},{5,4},{6,5},{7,6},{8,11},{9,8},{10,9... | collective-permute-start | bytes 223496 | tf_op jit(solution)/shard_map/ppermute | solution.py:991
  26.4 7.3 %copy-start.33 = (s32[90,90]{1,0:T(8,128)S(1)}, s32[90,90]{1,0:T(8,128)}, u32[]{:S(2)}) copy-start(s32[90,90]{1,0:T(8,128)} %param.35) | copy-start | bytes 97204
  26.4 11.6 %all-to-all-start = ((bf16[2,45,96,192]{3,2,1,0:T(8,128)(2,1)}), bf16[2,45,96,192]{3,2,1,0:T(8,128)(2,1)}, u32[]{:S(2)}, u32[]{:S(2)}) async-start(bf16[2,45,96,192]{3,2,1,0:T(8,128)(2,1)} %bitcast.103), calls=%async_computation | async-start | bytes 8847360 | tf_op jit(solution)/shard_map/all_to_all | solution.py:986
  38.0 22.2 %copy-start.30 = (f32[97,2,96]{2,1,0:T(2,128)}, f32[97,2,96]{2,1,0:T(2,128)S(1)}, u32[]{:S(2)}) copy-start(f32[97,2,96]{2,1,0:T(2,128)S(1)} %collective-permute-done) | copy-start | bytes 223492
  38.0 22.2 %copy-start.31 = (f32[97,2,96]{2,1,0:T(2,128)}, f32[97,2,96]{2,1,0:T(2,128)S(1)}, u32[]{:S(2)}) copy-start(f32[97,2,96]{2,1,0:T(2,128)S(1)} %collective-permute-done.1) | copy-start | bytes 223492
  38.0 22.2 %copy-start.32 = (f32[97,2,96]{2,1,0:T(2,128)}, f32[97,2,96]{2,1,0:T(2,128)S(1)}, u32[]{:S(2)}) copy-start(f32[97,2,96]{2,1,0:T(2,128)S(1)} %collective-permute-done.2) | copy-start | bytes 223492
  60.2 49.9 %all-to-all-start.3 = ((f32[8,6,48,384]{3,2,1,0:T(8,128)}), f32[8,6,48,384]{3,2,1,0:T(8,128)S(1)}, u32[]{:S(2)}, u32[]{:S(2)}) async-start(f32[8,6,48,384]{3,2,1,0:T(8,128)} %get-tuple-element.169), calls=%async_computation.3 | async-start | bytes 7077888 | tf_op jit(solution)/shard_map/all_to_all | solution.py:986
  72.8 21.8 %slice-start.3 = ((f32[97,2,96]{2,1,0:T(2,128)}), f32[7,2,96]{2,1,0:T(2,128)S(1)}, s32[]{:S(2)}) async-start(f32[97,2,96]{2,1,0:T(2,128)} %copy-done.31), calls=%async_computation.26 | async-start | bytes 14336 | tf_op jit(solution)/shard_map/slice | solution.py:1138
  72.8 22.5 %slice-start.2 = ((f32[97,2,96]{2,1,0:T(2,128)}), f32[7,2,96]{2,1,0:T(2,128)S(1)}, s32[]{:S(2)}) async-start(f32[97,2,96]{2,1,0:T(2,128)} %copy-done.30), calls=%async_computation.25 | async-start | bytes 14336 | tf_op jit(solution)/shard_map/slice | solution.py:1138
  75.9 25.1 %collective-permute-start.3 = (bf16[45,96,192]{2,1,0:T(8,128)(2,1)}, bf16[45,96,192]{2,1,0:T(8,128)(2,1)}, u32[]{:S(2)}, u32[]{:S(2)}) collective-permute-start(bf16[45,96,192]{2,1,0:T(8,128)(2,1)} %dynamic-slice_bitcast_fusion), channel_id=1, source_target_pairs={{0,4},{4,0},{1,5},{5,1},{2,6},{6,2},{3,7},{7,3},{8,12},{12,8},{9,1... | collective-permute-start | bytes 4976648 | tf_op jit(solution)/shard_map/ppermute | solution.py:995
  112.0 44.0 %all-to-all-start.2 = ((f32[8,6,48,384]{3,2,1,0:T(8,128)}), f32[8,6,48,384]{3,2,1,0:T(8,128)}, u32[]{:S(2)}, u32[]{:S(2)}) async-start(f32[8,6,48,384]{3,2,1,0:T(8,128)} %get-tuple-element.168), calls=%async_computation.2 | async-start | bytes 7077888 | tf_op jit(solution)/shard_map/all_to_all | solution.py:986
  116.9 9.5 %copy-start.38 = (f32[2,2,96]{2,1,0:T(2,128)S(1)}, f32[2,2,96]{2,1,0:T(2,128)}, u32[]{:S(2)}) copy-start(f32[2,2,96]{2,1,0:T(2,128)} %param.26) | copy-start | bytes 4612
  116.9 10.2 %copy-start.39 = (f32[2,2,96]{2,1,0:T(2,128)S(1)}, f32[2,2,96]{2,1,0:T(2,128)}, u32[]{:S(2)}) copy-start(f32[2,2,96]{2,1,0:T(2,128)} %param.28) | copy-start | bytes 4612
  119.5 26.4 %collective-permute-start.4 = (bf16[576,384]{1,0:T(8,128)(2,1)}, bf16[576,384]{1,0:T(8,128)(2,1)S(1)}, u32[]{:S(2)}, u32[]{:S(2)}) collective-permute-start(bf16[576,384]{1,0:T(8,128)(2,1)} %get-tuple-element.420), channel_id=1, source_target_pairs={{0,1},{1,2},{2,3},{3,0},{4,5},{5,6},{6,7},{7,4},{8,9},{9,10},{10,1... | collective-permute-start | bytes 1327112 | tf_op jit(solution)/shard_map/ppermute | solution.py:991
  122.5 33.5 %collective-permute-start.5 = (bf16[576,384]{1,0:T(8,128)(2,1)}, bf16[576,384]{1,0:T(8,128)(2,1)S(1)}, u32[]{:S(2)}, u32[]{:S(2)}) collective-permute-start(bf16[576,384]{1,0:T(8,128)(2,1)} %get-tuple-element.419), channel_id=1, source_target_pairs={{0,2},{1,3},{2,0},{3,1},{4,6},{5,7},{6,4},{7,5},{8,10},{9,11},{10,... | collective-permute-start | bytes 1327112 | tf_op jit(solution)/shard_map/ppermute | solution.py:991
  126.2 29.7 %collective-permute-start.6 = (bf16[576,384]{1,0:T(8,128)(2,1)S(1)}, bf16[576,384]{1,0:T(8,128)(2,1)S(1)}, u32[]{:S(2)}, u32[]{:S(2)}) collective-permute-start(bf16[576,384]{1,0:T(8,128)(2,1)S(1)} %get-tuple-element.418), channel_id=1, source_target_pairs={{0,3},{1,0},{2,1},{3,2},{4,7},{5,4},{6,5},{7,6},{8,11},{9,8},{10,9... | collective-permute-start | bytes 1327112 | tf_op jit(solution)/shard_map/ppermute | solution.py:991
  145.9 10.1 %copy-start.17 = (bf16[576,384]{1,0:T(8,128)(2,1)}, bf16[576,384]{1,0:T(8,128)(2,1)S(1)}, u32[]{:S(2)}) copy-start(bf16[576,384]{1,0:T(8,128)(2,1)S(1)} %collective-permute-done.4.refs_5_) | copy-start | bytes 1327108
  156.9 35.2 %all-to-all-start.4 = ((bf16[8,6,48,384]{3,2,1,0:T(8,128)(2,1)}), bf16[8,6,48,384]{3,2,1,0:T(8,128)(2,1)S(1)}, u32[]{:S(2)}, u32[]{:S(2)}) async-start(bf16[8,6,48,384]{3,2,1,0:T(8,128)(2,1)} %get-tuple-element.176), calls=%async_computation.4 | async-start | bytes 3538944 | tf_op jit(solution)/shard_map/all_to_all | solution.py:986
  165.1 26.2 %collective-permute-start.7 = (bf16[512,384]{1,0:T(8,128)(2,1)S(1)}, bf16[512,384]{1,0:T(8,128)(2,1)S(1)}, u32[]{:S(2)}, u32[]{:S(2)}) collective-permute-start(bf16[512,384]{1,0:T(8,128)(2,1)S(1)} %get-tuple-element.429), channel_id=1, source_target_pairs={{0,1},{1,2},{2,3},{3,0},{4,5},{5,6},{6,7},{7,4},{8,9},{9,10},{10,1... | collective-permute-start | bytes 1179656 | tf_op jit(solution)/shard_map/ppermute | solution.py:991
  173.1 18.9 %collective-permute-start.8 = (bf16[512,384]{1,0:T(8,128)(2,1)S(1)}, bf16[512,384]{1,0:T(8,128)(2,1)S(1)}, u32[]{:S(2)}, u32[]{:S(2)}) collective-permute-start(bf16[512,384]{1,0:T(8,128)(2,1)S(1)} %get-tuple-element.428), channel_id=1, source_target_pairs={{0,3},{1,0},{2,1},{3,2},{4,7},{5,4},{6,5},{7,6},{8,11},{9,8},{10,9... | collective-permute-start | bytes 1179656 | tf_op jit(solution)/shard_map/ppermute | solution.py:991
  192.1 25.6 %copy-start.4 = (bf16[8,6,48,384]{3,2,1,0:T(8,128)(2,1)}, bf16[8,6,48,384]{3,2,1,0:T(8,128)(2,1)S(1)}, u32[]{:S(2)}) copy-start(bf16[8,6,48,384]{3,2,1,0:T(8,128)(2,1)S(1)} %all-to-all-done.4.modes_a) | copy-start | bytes 5308420
  192.8 24.9 %all-to-all-start.5 = ((bf16[8,6,48,384]{3,2,1,0:T(8,128)(2,1)}), bf16[8,6,48,384]{3,2,1,0:T(8,128)(2,1)S(1)}, u32[]{:S(2)}, u32[]{:S(2)}) async-start(bf16[8,6,48,384]{3,2,1,0:T(8,128)(2,1)} %get-tuple-element.177), calls=%async_computation.5 | async-start | bytes 3538944 | tf_op jit(solution)/shard_map/all_to_all | solution.py:986
  197.3 20.4 %collective-permute-start.9 = (bf16[512,384]{1,0:T(8,128)(2,1)}, bf16[512,384]{1,0:T(8,128)(2,1)}, u32[]{:S(2)}, u32[]{:S(2)}) collective-permute-start(bf16[512,384]{1,0:T(8,128)(2,1)} %get-tuple-element.426), channel_id=1, source_target_pairs={{0,2},{1,3},{2,0},{3,1},{4,6},{5,7},{6,4},{7,5},{8,10},{9,11},{10,... | collective-permute-start | bytes 1179656 | tf_op jit(solution)/shard_map/ppermute | solution.py:991
  228.6 44.3 %all-to-all-start.7 = ((bf16[4,576,384]{2,1,0:T(8,128)(2,1)}), bf16[4,576,384]{2,1,0:T(8,128)(2,1)S(1)}, u32[]{:S(2)}, u32[]{:S(2)}) async-start(bf16[4,576,384]{2,1,0:T(8,128)(2,1)} %bitcast.113), calls=%async_computation.7 | async-start | bytes 3538944 | tf_op jit(solution)/shard_map/all_to_all | solution.py:986
  232.3 45.2 %collective-permute-start.10 = (bf16[4,768,768]{2,1,0:T(8,128)(2,1)}, bf16[4,768,768]{2,1,0:T(8,128)(2,1)}, u32[]{:S(2)}, u32[]{:S(2)}) collective-permute-start(bf16[4,768,768]{2,1,0:T(8,128)(2,1)} %bitcast.97), channel_id=1, source_target_pairs={{0,4},{4,0},{1,5},{5,1},{2,6},{6,2},{3,7},{7,3},{8,12},{12,8},{9,1... | collective-permute-start | bytes 14155784 | tf_op jit(solution)/shard_map/ppermute | solution.py:995
  273.0 56.6 %all-to-all-start.6 = ((bf16[4,512,384]{2,1,0:T(8,128)(2,1)}), bf16[4,512,384]{2,1,0:T(8,128)(2,1)S(1)}, u32[]{:S(2)}, u32[]{:S(2)}) async-start(bf16[4,512,384]{2,1,0:T(8,128)(2,1)} %bitcast.114), calls=%async_computation.6 | async-start | bytes 3145728 | tf_op jit(solution)/shard_map/all_to_all | solution.py:986
  329.6 51.9 %all-to-all-start.8 = ((bf16[4,576,384]{2,1,0:T(8,128)(2,1)}), bf16[4,576,384]{2,1,0:T(8,128)(2,1)S(1)}, u32[]{:S(2)}, u32[]{:S(2)}) async-start(bf16[4,576,384]{2,1,0:T(8,128)(2,1)} %get-tuple-element.218), calls=%async_computation.8 | async-start | bytes 3538944 | tf_op jit(solution)/shard_map/all_to_all | solution.py:986
  334.1 174.8 %reduce-scatter.3.cloned.1.call-start = ((), (), s32[]{:S(2)}) async-start(), calls=%async_computation.19 | async-start | bytes 5898240 | tf_op jit(solution)/shard_map/reduce_scatter | solution.py:1205
  381.5 9.1 %copy-start.2 = (bf16[4,576,384]{2,1,0:T(8,128)(2,1)}, bf16[4,576,384]{2,1,0:T(8,128)(2,1)S(1)}, u32[]{:S(2)}) copy-start(bf16[4,576,384]{2,1,0:T(8,128)(2,1)S(1)} %all-to-all-done.8) | copy-start | bytes 5308420
  381.5 9.9 %copy-start.13 = (bf16[4,12,32,768]{3,2,1,0:T(8,128)(2,1)S(1)}, bf16[4,12,32,768]{3,2,1,0:T(8,128)(2,1)}, u32[]{:S(2)}) copy-start(bf16[4,12,32,768]{3,2,1,0:T(8,128)(2,1)} %get-tuple-element.248) | copy-start | bytes 7077892
  381.5 6.5 %collective-permute-start.18 = (bf16[4,12,32,768]{3,2,1,0:T(8,128)(2,1)}, bf16[4,12,32,768]{3,2,1,0:T(8,128)(2,1)S(1)}, u32[]{:S(2)}, u32[]{:S(2)}) collective-permute-start(bf16[4,12,32,768]{3,2,1,0:T(8,128)(2,1)} %get-tuple-element.247), channel_id=1, source_target_pairs={{0,4},{4,0},{1,5},{5,1},{2,6},{6,2},{3,7},{7,3},{8,12},{12,8},{9,1... | collective-permute-start | bytes 7077896 | tf_op jit(solution)/shard_map/ppermute | solution.py:995
  383.6 7.7 %collective-permute-start.19 = (bf16[4,12,32,768]{3,2,1,0:T(8,128)(2,1)}, bf16[4,12,32,768]{3,2,1,0:T(8,128)(2,1)S(1)}, u32[]{:S(2)}, u32[]{:S(2)}) collective-permute-start(bf16[4,12,32,768]{3,2,1,0:T(8,128)(2,1)} %get-tuple-element.249), channel_id=1, source_target_pairs={{0,4},{4,0},{1,5},{5,1},{2,6},{6,2},{3,7},{7,3},{8,12},{12,8},{9,1... | collective-permute-start | bytes 7077896 | tf_op jit(solution)/shard_map/ppermute | solution.py:995
  395.4 7.0 %copy-start.14 = (bf16[4,576,192]{2,1,0:T(8,128)(2,1)S(1)}, bf16[4,576,192]{2,1,0:T(8,128)(2,1)}, u32[]{:S(2)}) copy-start(bf16[4,576,192]{2,1,0:T(8,128)(2,1)} %get-tuple-element.222) | copy-start | bytes 2654212
  395.4 41.3 %all-to-all-start.9 = ((bf16[4,512,384]{2,1,0:T(8,128)(2,1)}), bf16[4,512,384]{2,1,0:T(8,128)(2,1)S(1)}, u32[]{:S(2)}, u32[]{:S(2)}) async-start(bf16[4,512,384]{2,1,0:T(8,128)(2,1)} %get-tuple-element.220), calls=%async_computation.9 | async-start | bytes 3145728 | tf_op jit(solution)/shard_map/all_to_all | solution.py:986
  401.7 2.8 collective-permute-start.12
  403.7 5.2 collective-permute-start.11
  446.6 28.4 %all-to-all-start.10 = ((bf16[8,6,48,384]{3,2,1,0:T(8,128)(2,1)}), bf16[8,6,48,384]{3,2,1,0:T(8,128)(2,1)S(1)}, u32[]{:S(2)}, u32[]{:S(2)}) async-start(bf16[8,6,48,384]{3,2,1,0:T(8,128)(2,1)} %get-tuple-element.228), calls=%async_computation.10 | async-start | bytes 3538944 | tf_op jit(solution)/shard_map/all_to_all | solution.py:986
  453.0 13.6 %collective-permute-start.13 = (bf16[576,384]{1,0:T(8,128)(2,1)S(1)}, bf16[576,384]{1,0:T(8,128)(2,1)S(1)}, u32[]{:S(2)}, u32[]{:S(2)}) collective-permute-start(bf16[576,384]{1,0:T(8,128)(2,1)S(1)} %get-tuple-element.417), channel_id=1, source_target_pairs={{0,1},{1,2},{2,3},{3,0},{4,5},{5,6},{6,7},{7,4},{8,9},{9,10},{10,1... | collective-permute-start | bytes 1327112 | tf_op jit(solution)/shard_map/ppermute | solution.py:991
  453.0 21.3 %collective-permute-start.14 = (bf16[576,384]{1,0:T(8,128)(2,1)S(1)}, bf16[576,384]{1,0:T(8,128)(2,1)S(1)}, u32[]{:S(2)}, u32[]{:S(2)}) collective-permute-start(bf16[576,384]{1,0:T(8,128)(2,1)S(1)} %get-tuple-element.416), channel_id=1, source_target_pairs={{0,3},{1,0},{2,1},{3,2},{4,7},{5,4},{6,5},{7,6},{8,11},{9,8},{10,9... | collective-permute-start | bytes 1327112 | tf_op jit(solution)/shard_map/ppermute | solution.py:991
  466.7 7.6 %copy-start.20 = (bf16[576,384]{1,0:T(8,128)(2,1)}, bf16[576,384]{1,0:T(8,128)(2,1)S(1)}, u32[]{:S(2)}) copy-start(bf16[576,384]{1,0:T(8,128)(2,1)S(1)} %collective-permute-done.13.refs_1_) | copy-start | bytes 1327108
  475.1 10.1 %copy-start.10 = (bf16[8,6,48,384]{3,2,1,0:T(8,128)(2,1)}, bf16[8,6,48,384]{3,2,1,0:T(8,128)(2,1)S(1)}, u32[]{:S(2)}) copy-start(bf16[8,6,48,384]{3,2,1,0:T(8,128)(2,1)S(1)} %all-to-all-done.10.modes) | copy-start | bytes 5308420
  475.1 28.7 %all-to-all-start.11 = ((bf16[8,6,48,384]{3,2,1,0:T(8,128)(2,1)}), bf16[8,6,48,384]{3,2,1,0:T(8,128)(2,1)S(1)}, u32[]{:S(2)}, u32[]{:S(2)}) async-start(bf16[8,6,48,384]{3,2,1,0:T(8,128)(2,1)} %get-tuple-element.234), calls=%async_computation.11 | async-start | bytes 3538944 | tf_op jit(solution)/shard_map/all_to_all | solution.py:986
  480.6 22.6 %collective-permute-start.15 = (f32[1,1344]{1,0:T(1,128)S(1)}, f32[1,1344]{1,0:T(1,128)S(1)}, u32[]{:S(2)}, u32[]{:S(2)}) collective-permute-start(f32[1,1344]{1,0:T(1,128)S(1)} %get-tuple-element.441), channel_id=1, source_target_pairs={{0,1},{1,2},{2,3},{3,0},{4,5},{5,6},{6,7},{7,4},{8,9},{9,10},{10,1... | collective-permute-start | bytes 16136 | tf_op jit(solution)/shard_map/ppermute | solution.py:991
  481.2 22.0 %collective-permute-start.16 = (f32[1,1344]{1,0:T(1,128)S(1)}, f32[1,1344]{1,0:T(1,128)S(1)}, u32[]{:S(2)}, u32[]{:S(2)}) collective-permute-start(f32[1,1344]{1,0:T(1,128)S(1)} %get-tuple-element.440), channel_id=1, source_target_pairs={{0,2},{1,3},{2,0},{3,1},{4,6},{5,7},{6,4},{7,5},{8,10},{9,11},{10,... | collective-permute-start | bytes 16136 | tf_op jit(solution)/shard_map/ppermute | solution.py:991
  482.9 20.9 %collective-permute-start.17 = (f32[1,1344]{1,0:T(1,128)S(1)}, f32[1,1344]{1,0:T(1,128)}, u32[]{:S(2)}, u32[]{:S(2)}) collective-permute-start(f32[1,1344]{1,0:T(1,128)S(1)} %get-tuple-element.439), channel_id=1, source_target_pairs={{0,3},{1,0},{2,1},{3,2},{4,7},{5,4},{6,5},{7,6},{8,11},{9,8},{10,9... | collective-permute-start | bytes 16136 | tf_op jit(solution)/shard_map/ppermute | solution.py:991
  503.8 5.8 copy-start.9
  503.8 24.7 %all-to-all-start.12 = ((bf16[8,6,48,384]{3,2,1,0:T(8,128)(2,1)}), bf16[8,6,48,384]{3,2,1,0:T(8,128)(2,1)}, u32[]{:S(2)}, u32[]{:S(2)}) async-start(bf16[8,6,48,384]{3,2,1,0:T(8,128)(2,1)} %get-tuple-element.243), calls=%async_computation.12 | async-start | bytes 3538944 | tf_op jit(solution)/shard_map/all_to_all | solution.py:986
  508.9 49.3 %reduce-scatter.5.cloned.1.call-start = ((), (), s32[]{:S(2)}) async-start(), calls=%async_computation.20 | async-start | bytes 1474560 | tf_op jit(solution)/shard_map/reduce_scatter | solution.py:1206
  528.4 8.4 %copy-start.3 = (bf16[4,576,384]{2,1,0:T(8,128)(2,1)S(1)}, bf16[4,576,384]{2,1,0:T(8,128)(2,1)}, u32[]{:S(2)}) copy-start(bf16[4,576,384]{2,1,0:T(8,128)(2,1)} %copy-done.2) | copy-start | bytes 5308420
  528.4 8.4 %copy-start.8 = (bf16[4,512,384]{2,1,0:T(8,128)(2,1)S(1)}, bf16[4,512,384]{2,1,0:T(8,128)(2,1)}, u32[]{:S(2)}) copy-start(bf16[4,512,384]{2,1,0:T(8,128)(2,1)} %copy-done.7) | copy-start | bytes 4718596
  528.5 29.7 %all-to-all-start.13 = ((bf16[8,6,48,384]{3,2,1,0:T(8,128)(2,1)}), bf16[8,6,48,384]{3,2,1,0:T(8,128)(2,1)}, u32[]{:S(2)}, u32[]{:S(2)}) async-start(bf16[8,6,48,384]{3,2,1,0:T(8,128)(2,1)} %get-tuple-element.245), calls=%async_computation.13 | async-start | bytes 3538944 | tf_op jit(solution)/shard_map/all_to_all | solution.py:986
  536.4 75.6 %all-gather.7.cloned.1.call-start = ((), (), s32[]{:S(2)}) async-start(), calls=%async_computation.22 | async-start | bytes 2654208 | tf_op jit(solution)/shard_map/all_gather | solution.py:1258
  536.4 21.8 %collective-permute-start.20 = (bf16[576,384]{1,0:T(8,128)(2,1)}, bf16[576,384]{1,0:T(8,128)(2,1)}, u32[]{:S(2)}, u32[]{:S(2)}) collective-permute-start(bf16[576,384]{1,0:T(8,128)(2,1)} %get-tuple-element.414), channel_id=1, source_target_pairs={{0,2},{1,3},{2,0},{3,1},{4,6},{5,7},{6,4},{7,5},{8,10},{9,11},{10,... | collective-permute-start | bytes 1327112 | tf_op jit(solution)/shard_map/ppermute | solution.py:991
  558.2 35.9 %collective-permute-start.21 = (bf16[512,384]{1,0:T(8,128)(2,1)S(1)}, bf16[512,384]{1,0:T(8,128)(2,1)S(1)}, u32[]{:S(2)}, u32[]{:S(2)}) collective-permute-start(bf16[512,384]{1,0:T(8,128)(2,1)S(1)} %get-tuple-element.266), channel_id=1, source_target_pairs={{0,1},{1,2},{2,3},{3,0},{4,5},{5,6},{6,7},{7,4},{8,9},{9,10},{10,1... | collective-permute-start | bytes 1179656 | tf_op jit(solution)/shard_map/ppermute | solution.py:991
  558.3 35.9 %collective-permute-start.22 = (bf16[512,384]{1,0:T(8,128)(2,1)S(1)}, bf16[512,384]{1,0:T(8,128)(2,1)S(1)}, u32[]{:S(2)}, u32[]{:S(2)}) collective-permute-start(bf16[512,384]{1,0:T(8,128)(2,1)S(1)} %get-tuple-element.267), channel_id=1, source_target_pairs={{0,2},{1,3},{2,0},{3,1},{4,6},{5,7},{6,4},{7,5},{8,10},{9,11},{10,... | collective-permute-start | bytes 1179656 | tf_op jit(solution)/shard_map/ppermute | solution.py:991
  559.1 35.1 %collective-permute-start.23 = (bf16[512,384]{1,0:T(8,128)(2,1)S(1)}, bf16[512,384]{1,0:T(8,128)(2,1)S(1)}, u32[]{:S(2)}, u32[]{:S(2)}) collective-permute-start(bf16[512,384]{1,0:T(8,128)(2,1)S(1)} %get-tuple-element.268), channel_id=1, source_target_pairs={{0,3},{1,0},{2,1},{3,2},{4,7},{5,4},{6,5},{7,6},{8,11},{9,8},{10,9... | collective-permute-start | bytes 1179656 | tf_op jit(solution)/shard_map/ppermute | solution.py:991
  561.6 32.5 %all-to-all-start.14 = ((f32[8,99,96]{1,2,0:T(8,128)}), f32[8,99,96]{1,2,0:T(8,128)S(1)}, u32[]{:S(2)}, u32[]{:S(2)}) async-start(f32[8,99,96]{1,2,0:T(8,128)} %pad_maximum_fusion.5), calls=%async_computation.16 | async-start | bytes 786432 | tf_op jit(solution)/shard_map/all_to_all | solution.py:986
  594.2 17.8 %collective-permute-start.24 = (f32[45,96,192]{2,1,0:T(8,128)}, f32[45,96,192]{2,1,0:T(8,128)}, u32[]{:S(2)}, u32[]{:S(2)}) collective-permute-start(f32[45,96,192]{2,1,0:T(8,128)} %get-tuple-element.270), channel_id=1, source_target_pairs={{0,4},{4,0},{1,5},{5,1},{2,6},{6,2},{3,7},{7,3},{8,12},{12,8},{9,1... | collective-permute-start | bytes 9953288 | tf_op jit(solution)/shard_map/ppermute | solution.py:995
  596.2 15.0 %all-to-all-start.15 = ((f32[8,45,2,96]{3,2,1,0:T(2,128)}), f32[8,45,2,96]{3,2,1,0:T(2,128)S(1)}, u32[]{:S(2)}, u32[]{:S(2)}) async-start(f32[8,45,2,96]{3,2,1,0:T(2,128)} %bitcast.47), calls=%async_computation.17 | async-start | bytes 737280 | tf_op jit(solution)/shard_map/all_to_all | solution.py:986
  613.8 25.1 %all-to-all-start.16 = ((f32[8,103,96]{1,2,0:T(8,128)}), f32[8,103,96]{1,2,0:T(8,128)S(1)}, u32[]{:S(2)}, u32[]{:S(2)}) async-start(f32[8,103,96]{1,2,0:T(8,128)} %broadcast_in_dim.25), calls=%async_computation.18 | async-start | bytes 786432 | tf_op jit(solution)/shard_map/all_to_all | solution.py:986
  (29 other events, 66.5 us)
Sparse Core Ops, SparseCore 0:
  10.2 99.9 all-gather.4
  395.5 58.3 reduce-scatter.2
  512.0 27.0 reduce-scatter.4
  558.4 31.8 all-gather.6
